TPU v7x, 32 devices: a whole 2x2x4 slice. The times are simulated.
32 devices in a mesh: dp: 4 (over y, x), fsdp: 8 (over z, core).
Axes of the slice: x: 2, y: 2, z: 4, core: 2. Of those that a mesh axis runs over, the one named last changes fastest.
Arguments:
- tokens: bfloat16 [32768, 768], P(('dp', 'fsdp')), may hold values from -6 to 6
- seq_lengths: int32 [32, 9], P(('dp', 'fsdp')), may hold values from 1 to 512, 1024 in all within a row
- query_weight: bfloat16 [768, 768], P(('dp', 'fsdp')), may hold values from -0.21875 to 0.21875
- query_bias: bfloat16 [768], P(('dp', 'fsdp')), may hold values from -3 to 3
- key_weight: bfloat16 [768, 768], P(('dp', 'fsdp')), may hold values from -0.21875 to 0.21875
- value_weight: bfloat16 [768, 768], P(('dp', 'fsdp')), may hold values from -0.21875 to 0.21875
- value_bias: bfloat16 [768], P(('dp', 'fsdp')), may hold values from -0.59765625 to 0.59765625
- out_weight: bfloat16 [768, 768], P(('dp', 'fsdp')), may hold values from -1.75 to 1.75
- out_bias: bfloat16 [768], P(('dp', 'fsdp')), may hold values from -3 to 3
- first_gain: bfloat16 [768], P(('dp', 'fsdp')), may hold values from 0.5 to 1.5
- first_shift: bfloat16 [768], P(('dp', 'fsdp')), may hold values from -3 to 3
- up_weight: bfloat16 [768, 3072], P(('dp', 'fsdp')), may hold values from -0.21875 to 0.21875
- up_bias: bfloat16 [3072], P(('dp', 'fsdp')), may hold values from -3 to 3
- down_weight: bfloat16 [3072, 768], P(('dp', 'fsdp')), may hold values from -0.109375 to 0.109375
- down_bias: bfloat16 [768], P(('dp', 'fsdp')), may hold values from -3 to 3
- second_gain: bfloat16 [768], P(('dp', 'fsdp')), may hold values from 0.5 to 1.5
- second_shift: bfloat16 [768], P(('dp', 'fsdp')), may hold values from -3 to 3
- out_grad: bfloat16 [32768, 768], P(('dp', 'fsdp')), may hold values from -6 to 6
Outputs:
- output: bfloat16 [32768, 768], P(('dp', 'fsdp'))
- tokens_grad: float32 [32768, 768], P(('dp', 'fsdp'))
- grad_query_weight: float32 [768, 768], P(('dp', 'fsdp'))
- grad_query_bias: float32 [768], P(('dp', 'fsdp'))
- grad_key_weight: float32 [768, 768], P(('dp', 'fsdp'))
- grad_value_weight: float32 [768, 768], P(('dp', 'fsdp'))
- grad_value_bias: float32 [768], P(('dp', 'fsdp'))
- grad_out_weight: float32 [768, 768], P(('dp', 'fsdp'))
- grad_out_bias: float32 [768], P(('dp', 'fsdp'))
- grad_first_gain: float32 [768], P(('dp', 'fsdp'))
- grad_first_shift: float32 [768], P(('dp', 'fsdp'))
- grad_up_weight: float32 [768, 3072], P(('dp', 'fsdp'))
- grad_up_bias: float32 [3072], P(('dp', 'fsdp'))
- grad_down_weight: float32 [3072, 768], P(('dp', 'fsdp'))
- grad_down_bias: float32 [768], P(('dp', 'fsdp'))
- grad_second_gain: float32 [768], P(('dp', 'fsdp'))
- grad_second_shift: float32 [768], P(('dp', 'fsdp'))
Inputs may be any that keep to these rules, and one draw needn't show every extreme that they name: `seq_lengths`: each row sums to 1024, and its largest entry is exactly 512.
All inputs are finite; a program needn't handle non-finite values.
Results may differ from a plain program's by a relative error of at most 0.014.
Values may be sent and summed in bfloat16 or wider, within the bound.
No kernel may reach another device: no remote copies, remote signals or barrier semaphores. Data moves between devices by JAX's collectives and lax.ppermute only.
A program may use at most 256 MiB of HBM per device.

v0:
```python
import math

import jax
import jax.numpy as jnp
from jax import lax
from jax.sharding import PartitionSpec as P

HEADS = 12
HEAD_DIM = 64


EPSILON = 1e-06
MASKED = -1e30


def product(left, right):
    return jnp.dot(left, right, preferred_element_type=jnp.float32)


def product_left(left, right):
    return lax.dot_general(
        left, right, (((0,), (0,)), ((), ())), preferred_element_type=jnp.float32
    )


def product_right(left, right):
    return lax.dot_general(
        left, right, (((1,), (1,)), ((), ())), preferred_element_type=jnp.float32
    )


def rounded(value):
    return lax.optimization_barrier(value.astype(jnp.bfloat16)).astype(jnp.float32)


def gelu_tanh(value):
    return jax.nn.gelu(value, approximate=True)


def column_sum(value):
    return jnp.sum(value.astype(jnp.float32), axis=0)


def segment_ids(lengths, row_count):
    seq_ends = jnp.cumsum(lengths)
    positions = jnp.arange(row_count, dtype=jnp.int32)
    return jnp.sum((positions[:, None] >= seq_ends[None, :]).astype(jnp.int32), axis=1)


def norm_forward(value, gain, shift):
    center = value - jnp.mean(value, axis=-1, keepdims=True)
    inverse = lax.rsqrt(jnp.mean(center * center, axis=-1, keepdims=True) + EPSILON)
    normed = center * inverse
    return (normed * gain + shift, normed, inverse)


def norm_backward(upstream, normed, inverse, gain):
    gain_grad = jnp.sum(upstream * normed, axis=0)
    shift_grad = jnp.sum(upstream, axis=0)
    scaled = upstream * gain
    centered = scaled - jnp.mean(scaled, axis=-1, keepdims=True)
    centered = centered - normed * jnp.mean(scaled * normed, axis=-1, keepdims=True)
    return (inverse * centered, gain_grad, shift_grad)


def collect(params):
    return (
        lax.all_gather(params[0], ("dp", "fsdp"), axis=0, tiled=True),
        lax.all_gather(params[1], ("dp", "fsdp"), axis=0, tiled=True),
        lax.all_gather(params[2], ("dp", "fsdp"), axis=0, tiled=True),
        lax.all_gather(params[3], ("dp", "fsdp"), axis=0, tiled=True),
        lax.all_gather(params[4], ("dp", "fsdp"), axis=0, tiled=True),
        lax.all_gather(params[5], ("dp", "fsdp"), axis=0, tiled=True),
        lax.all_gather(params[6], ("dp", "fsdp"), axis=0, tiled=True),
        lax.all_gather(params[7], ("dp", "fsdp"), axis=0, tiled=True),
        lax.all_gather(params[8], ("dp", "fsdp"), axis=0, tiled=True),
        lax.all_gather(params[9], ("dp", "fsdp"), axis=0, tiled=True),
        lax.all_gather(params[10], ("dp", "fsdp"), axis=0, tiled=True),
        lax.all_gather(params[11], ("dp", "fsdp"), axis=0, tiled=True),
        lax.all_gather(params[12], ("dp", "fsdp"), axis=0, tiled=True),
        lax.all_gather(params[13], ("dp", "fsdp"), axis=0, tiled=True),
        lax.all_gather(params[14], ("dp", "fsdp"), axis=0, tiled=True),
    )


def spread(grads):
    return (
        lax.psum_scatter(grads[0], ("dp", "fsdp"), scatter_dimension=0, tiled=True),
        lax.psum_scatter(grads[1], ("dp", "fsdp"), scatter_dimension=0, tiled=True),
        lax.psum_scatter(grads[2], ("dp", "fsdp"), scatter_dimension=0, tiled=True),
        lax.psum_scatter(grads[3], ("dp", "fsdp"), scatter_dimension=0, tiled=True),
        lax.psum_scatter(grads[4], ("dp", "fsdp"), scatter_dimension=0, tiled=True),
        lax.psum_scatter(grads[5], ("dp", "fsdp"), scatter_dimension=0, tiled=True),
        lax.psum_scatter(grads[6], ("dp", "fsdp"), scatter_dimension=0, tiled=True),
        lax.psum_scatter(grads[7], ("dp", "fsdp"), scatter_dimension=0, tiled=True),
        lax.psum_scatter(grads[8], ("dp", "fsdp"), scatter_dimension=0, tiled=True),
        lax.psum_scatter(grads[9], ("dp", "fsdp"), scatter_dimension=0, tiled=True),
        lax.psum_scatter(grads[10], ("dp", "fsdp"), scatter_dimension=0, tiled=True),
        lax.psum_scatter(grads[11], ("dp", "fsdp"), scatter_dimension=0, tiled=True),
        lax.psum_scatter(grads[12], ("dp", "fsdp"), scatter_dimension=0, tiled=True),
        lax.psum_scatter(grads[13], ("dp", "fsdp"), scatter_dimension=0, tiled=True),
        lax.psum_scatter(grads[14], ("dp", "fsdp"), scatter_dimension=0, tiled=True),
    )


def body(
    tokens,
    seq_lengths,
    query_weight,
    query_bias,
    key_weight,
    value_weight,
    value_bias,
    out_weight,
    out_bias,
    first_gain,
    first_shift,
    up_weight,
    up_bias,
    down_weight,
    down_bias,
    second_gain,
    second_shift,
    out_grad,
):
    gathered = collect(
        (
            query_weight,
            query_bias,
            key_weight,
            value_weight,
            value_bias,
            out_weight,
            out_bias,
            first_gain,
            first_shift,
            up_weight,
            up_bias,
            down_weight,
            down_bias,
            second_gain,
            second_shift,
        )
    )
    (
        query_mat,
        query_vec,
        key_mat,
        value_mat,
        value_vec,
        out_mat,
        out_vec,
        gain_one,
        shift_one,
        up_mat,
        up_vec,
        down_mat,
        down_vec,
        gain_two,
        shift_two,
    ) = gathered
    row_count = tokens.shape[0]
    block_rows = min(512, row_count)
    block_count = row_count // block_rows
    num_heads = HEADS
    head_size = HEAD_DIM
    score_scale = 1.0 / math.sqrt(head_size)
    segment = segment_ids(seq_lengths[0], row_count)
    query_low = (product(tokens, query_mat) + query_vec.astype(jnp.float32)).astype(jnp.bfloat16)
    key_low = product(tokens, key_mat).astype(jnp.bfloat16)
    value_low = (product(tokens, value_mat) + value_vec.astype(jnp.float32)).astype(jnp.bfloat16)
    key_heads = key_low.reshape(row_count, num_heads, head_size)
    value_heads = value_low.reshape(row_count, num_heads, head_size)
    query_blocks = query_low.reshape(block_count, block_rows, num_heads, head_size)
    segment_blocks = segment.reshape(block_count, block_rows)

    def block_scores(query_block, segment_block):
        scores = (
            jnp.einsum("qhd,khd->hqk", query_block, key_heads, preferred_element_type=jnp.float32)
            * score_scale
        )
        same_seq = segment_block[:, None] == segment[None, :]
        return jnp.where(same_seq[None], scores, MASKED)

    def attend(inputs):
        scores = block_scores(inputs[0], inputs[1])
        row_max = jnp.max(scores, axis=-1, keepdims=True)
        exp_scores = jnp.exp(scores - row_max)
        row_total = jnp.sum(exp_scores, axis=-1, keepdims=True)
        prob_low = (exp_scores / row_total).astype(jnp.bfloat16)
        context = jnp.einsum(
            "hqk,khd->qhd", prob_low, value_heads, preferred_element_type=jnp.float32
        )
        return (context.astype(jnp.bfloat16), row_max + jnp.log(row_total))

    context_blocks, log_totals = lax.map(attend, (query_blocks, segment_blocks))
    context_low = context_blocks.reshape(row_count, num_heads * head_size)
    attended = product(context_low, out_mat) + out_vec.astype(jnp.float32)
    middle, normed_one, inverse_one = norm_forward(
        tokens.astype(jnp.float32) + attended,
        gain_one.astype(jnp.float32),
        shift_one.astype(jnp.float32),
    )
    middle_low = middle.astype(jnp.bfloat16)
    expand_pre = product(middle_low, up_mat) + up_vec.astype(jnp.float32)
    expand_act, gelu_pull = jax.vjp(gelu_tanh, expand_pre)
    expand_low = expand_act.astype(jnp.bfloat16)
    shrink_out = product(expand_low, down_mat) + down_vec.astype(jnp.float32)
    final, normed_two, inverse_two = norm_forward(
        middle + shrink_out, gain_two.astype(jnp.float32), shift_two.astype(jnp.float32)
    )
    upstream = out_grad.astype(jnp.float32)
    second_back, grad_gain_two, grad_shift_two = norm_backward(
        upstream, normed_two, inverse_two, gain_two.astype(jnp.float32)
    )
    shrink_back = second_back.astype(jnp.bfloat16)
    grad_down_vec = column_sum(shrink_back)
    grad_down_mat = product_left(expand_low, shrink_back)
    expand_back = gelu_pull(product_right(shrink_back, down_mat))[0].astype(jnp.bfloat16)
    grad_up_vec = column_sum(expand_back)
    grad_up_mat = product_left(middle_low, expand_back)
    middle_back = second_back + rounded(product_right(expand_back, up_mat))
    entry_back, grad_gain_one, grad_shift_one = norm_backward(
        middle_back, normed_one, inverse_one, gain_one.astype(jnp.float32)
    )
    attended_back = entry_back.astype(jnp.bfloat16)
    grad_out_vec = column_sum(attended_back)
    grad_out_mat = product_left(context_low, attended_back)
    context_back = product_right(attended_back, out_mat).astype(jnp.bfloat16)
    context_back_blocks = context_back.reshape(block_count, block_rows, num_heads, head_size)

    def attend_back(running, inputs):
        query_block, segment_block, log_block, back_block = inputs
        scores = block_scores(query_block, segment_block)
        probs = jnp.exp(scores - log_block)
        prob_low = probs.astype(jnp.bfloat16)
        prob_back = jnp.einsum(
            "qhd,khd->hqk", back_block, value_heads, preferred_element_type=jnp.float32
        )
        score_back = probs * (prob_back - jnp.sum(probs * prob_back, axis=-1, keepdims=True))
        score_back = score_back.astype(jnp.bfloat16)
        query_part = (
            jnp.einsum("hqk,khd->qhd", score_back, key_heads, preferred_element_type=jnp.float32)
            * score_scale
        )
        key_sum = (
            running[0]
            + jnp.einsum(
                "hqk,qhd->khd", score_back, query_block, preferred_element_type=jnp.float32
            )
            * score_scale
        )
        value_sum = running[1] + jnp.einsum(
            "hqk,qhd->khd", prob_low, back_block, preferred_element_type=jnp.float32
        )
        return ((key_sum, value_sum), query_part)

    zero_heads = jnp.zeros((row_count, num_heads, head_size), jnp.float32)
    (key_sum, value_sum), query_parts = lax.scan(
        attend_back,
        (zero_heads, zero_heads),
        (query_blocks, segment_blocks, log_totals, context_back_blocks),
    )
    query_back = query_parts.reshape(row_count, num_heads * head_size).astype(jnp.bfloat16)
    key_back = key_sum.reshape(row_count, num_heads * head_size).astype(jnp.bfloat16)
    value_back = value_sum.reshape(row_count, num_heads * head_size).astype(jnp.bfloat16)
    grad_query_vec = column_sum(query_back)
    grad_value_vec = column_sum(value_back)
    grad_query_mat = product_left(tokens, query_back)
    grad_key_mat = product_left(tokens, key_back)
    grad_value_mat = product_left(tokens, value_back)
    tokens_grad = entry_back + product_right(query_back, query_mat)
    tokens_grad = tokens_grad + product_right(key_back, key_mat)
    tokens_grad = tokens_grad + product_right(value_back, value_mat)
    owned = spread(
        (
            grad_query_mat,
            grad_query_vec,
            grad_key_mat,
            grad_value_mat,
            grad_value_vec,
            grad_out_mat,
            grad_out_vec,
            grad_gain_one,
            grad_shift_one,
            grad_up_mat,
            grad_up_vec,
            grad_down_mat,
            grad_down_vec,
            grad_gain_two,
            grad_shift_two,
        )
    )
    return (
        final.astype(jnp.bfloat16),
        tokens_grad,
        owned[0],
        owned[1],
        owned[2],
        owned[3],
        owned[4],
        owned[5],
        owned[6],
        owned[7],
        owned[8],
        owned[9],
        owned[10],
        owned[11],
        owned[12],
        owned[13],
        owned[14],
    )


def solution(mesh):
    in_specs = (
        P(("dp", "fsdp"), None),
        P(("dp", "fsdp"), None),
        P(("dp", "fsdp"), None),
        P(("dp", "fsdp")),
        P(("dp", "fsdp"), None),
        P(("dp", "fsdp"), None),
        P(("dp", "fsdp")),
        P(("dp", "fsdp"), None),
        P(("dp", "fsdp")),
        P(("dp", "fsdp")),
        P(("dp", "fsdp")),
        P(("dp", "fsdp"), None),
        P(("dp", "fsdp")),
        P(("dp", "fsdp"), None),
        P(("dp", "fsdp")),
        P(("dp", "fsdp")),
        P(("dp", "fsdp")),
        P(("dp", "fsdp"), None),
    )
    out_specs = (
        P(("dp", "fsdp"), None),
        P(("dp", "fsdp"), None),
        P(("dp", "fsdp"), None),
        P(("dp", "fsdp")),
        P(("dp", "fsdp"), None),
        P(("dp", "fsdp"), None),
        P(("dp", "fsdp")),
        P(("dp", "fsdp"), None),
        P(("dp", "fsdp")),
        P(("dp", "fsdp")),
        P(("dp", "fsdp")),
        P(("dp", "fsdp"), None),
        P(("dp", "fsdp")),
        P(("dp", "fsdp"), None),
        P(("dp", "fsdp")),
        P(("dp", "fsdp")),
        P(("dp", "fsdp")),
    )
    return jax.shard_map(body, mesh=mesh, in_specs=in_specs, out_specs=out_specs, check_vma=False)
```

profile of v0, /device:TPU:0, one launch (start us, length us, event | category | flops | bytes accessed | tf_op | source)
XLA Modules:
  0.0 1212.6 jit_solution(15062505915260321659)
XLA Ops:
  19.8 42.6 %all-reduce.19 = (bf16[768]{0:T(1024)(128)(2,1)S(1)}, bf16[768]{0:T(1024)(128)(2,1)S(1)}, bf16[768]{0:T(1024)(128)(2,1)S(1)}, bf16[768]{0:T(1024)(128)(2,1)S(1)}...) all-reduce(bf16[768]{0:T(1024)(128)(2,1)S(1)} %dynamic-update-slice, ...), channel_id=1, replica_groups=mesh['dp'=4,'fsdp'=8] {'dp','fsdp'}, use_global_device_ids=true, to_apply=%add | all-reduce | flops 9216 | bytes 36864
  66.5 2.6 copy.93
  70.8 2.7 add_convert_fusion.2
  74.2 2.4 reshape.220
  76.6 1.7 copy.90
  78.3 45.9 %all-gather.9.cloned.1.call-done = bf16[768,768]{1,0:T(8,128)(2,1)} async-done(((bf16[24,768]{1,0:T(8,128)(2,1)}), bf16[768,768]{1,0:T(8,128)(2,1)}) %all-gather.9.cloned.1.call-update) | async-done | bytes 1179664 | tf_op jit(solution)/shard_map/all_gather | solution.py:70
  124.3 3.2 convolution_convert_fusion.2
  127.5 53.0 %all-gather.11.cloned.1.call-done = bf16[768,768]{1,0:T(8,128)(2,1)} async-done(((bf16[24,768]{1,0:T(8,128)(2,1)}), bf16[768,768]{1,0:T(8,128)(2,1)}) %all-gather.11.cloned.1.call-update) | async-done | bytes 1179664 | tf_op jit(solution)/shard_map/all_gather | solution.py:71
  180.5 4.4 add_convert_fusion.1
  184.8 70.7 %while.27 = (s32[]{:T(128)}, bf16[2,512,12,64]{1,3,2,0:T(8,128)(2,1)}, f32[2,12,512,1]{2,1,3,0:T(8,128)S(1)}, s32[2,512]{1,0:T(2,128)S(1)}, s32[1024]{0:T(1024)S...) while((s32[]{:T(128)}, ...), condition=%wide.region_5.6_spmd, body=%wide.region_2.5_spmd.sunk | while | flops 1687021568 | bytes 189499568 | solution.py:196
  185.2 10.7 fusion.117
  195.9 12.3 %fusion.118 = f32[12,512]{1,0:T(8,128)S(1)} fusion(f32[12,512,1024]{2,1,0:T(8,128)} %get-tuple-element.497, f32[12,512]{1,0:T(8,128)S(1)} %get-tuple-element.498, pred[512,1024]{1,0:T(8,128)(4,1)S(1)} %broadcast_compare_fusion.4), kind=kLoop, calls=%fused_computation.4.clone.1 | loop fusion | flops 25159680 | bytes 25739264 | tf_op jit(solution)/shard_map/while/body/eval_jaxpr/reduce_sum | solution.py:189
  208.2 3.1 copy-done
  211.3 8.5 fusion.119
  220.3 10.7 fusion.117
  231.0 12.4 %fusion.118 = f32[12,512]{1,0:T(8,128)S(1)} fusion(f32[12,512,1024]{2,1,0:T(8,128)} %get-tuple-element.497, f32[12,512]{1,0:T(8,128)S(1)} %get-tuple-element.498, pred[512,1024]{1,0:T(8,128)(4,1)S(1)} %broadcast_compare_fusion.4), kind=kLoop, calls=%fused_computation.4.clone.1 | loop fusion | flops 25159680 | bytes 25739264 | tf_op jit(solution)/shard_map/while/body/eval_jaxpr/reduce_sum | solution.py:189
  243.4 3.1 copy-done
  246.5 8.5 fusion.119
  255.5 3.0 copy.91
  260.1 3.9 fusion.59
  266.1 35.9 %all-gather.15.cloned.1.call-done = bf16[768,3072]{1,0:T(8,128)(2,1)} async-done(((bf16[24,3072]{1,0:T(8,128)(2,1)}), bf16[768,3072]{1,0:T(8,128)(2,1)}) %all-gather.15.cloned.1.call-update) | async-done | bytes 4718608 | tf_op jit(solution)/shard_map/all_gather | solution.py:77
  302.0 11.0 fusion.55
  313.0 54.4 %all-gather.17.cloned.1.call-done = bf16[3072,768]{1,0:T(8,128)(2,1)} async-done(((bf16[96,768]{1,0:T(8,128)(2,1)}), bf16[3072,768]{1,0:T(8,128)(2,1)}) %all-gather.17.cloned.1.call-update) | async-done | bytes 4718608 | tf_op jit(solution)/shard_map/all_gather | solution.py:79
  367.4 12.0 fusion.60
  380.9 2.0 fusion.47
  382.8 1.9 convert_reduce_fusion.2
  384.7 17.6 %convert_reduce_fusion = (f32[3072]{0:T(1024)}, bf16[1024,3072]{1,0:T(8,128)(2,1)}) fusion(f32[1024,3072]{1,0:T(8,128)} %fusion.55, f32[3072]{0:T(1024)S(1)} %copy-done.43, bf16[1024,768]{0,1:T(8,128)(2,1)S(1)} %get-tuple-element.369, bf16[3072,768]{1,0:T(8,128)(2,1)S(1)} %bitcast.161), kind=kOutput, calls=%fused_computation.55 | convolution fusion | flops 4904186880 | bytes 25190400 | tf_op jit(solution)/shard_map/dot_general | solution.py:27
  402.4 7.5 convolution_convert_fusion.1
  409.9 4.8 multiply_reduce_fusion.1
  414.7 1.7 convert_reduce_fusion.3
  418.1 2.9 fusion.50
  421.0 4.8 convolution_convert_fusion
  425.8 2.6 copy.95
  428.4 3.8 reshape.224
  432.3 2.9 copy.97
  435.2 171.6 %while.28 = (s32[]{:T(128)}, f32[1024,12,64]{0,2,1:T(8,128)}, f32[1024,12,64]{0,2,1:T(8,128)}, bf16[2,512,12,64]{1,3,2,0:T(8,128)(2,1)}, bf16[2,512,12,64]{1,3,2...) while((s32[]{:T(128)}, f32[1024,12,64]{0,2,1:T(8,128)}, ...), condition=%wide.region_16.17_spmd.clone, body=%wide.region_14.16_spmd.clone.sunk | while | flops 4125747200 | bytes 231926000 | solution.py:259
  437.2 11.7 fusion.129
  448.8 13.7 %bitcast_add_fusion.5 = f32[1024,12,64]{0,2,1:T(8,128)} fusion(f32[1024,12,64]{0,2,1:T(8,128)} %get-tuple-element.554, f32[12,512,1024]{2,1,0:T(8,128)} %fusion.129, f32[12,512]{1,0:T(8,128)S(1)} %dynamic-slice_bitcast_fusion.2, pred[512,1024]{1,0:T(8,128)(4,1)S(1)} %broadcast_compare_fusion.5, pred[]{:T(512)S(6)} %compare.3, ...), kind=kOutput, calls=%fused_computation.24.clone.1 | convolution fusion | flops 832045056 | bytes 32800772 | tf_op jit(solution)/shard_map/while/body/eval_jaxpr/hqk,qhd->khd/dot_general | solution.py:253
  462.6 18.3 %multiply_reduce_fusion.7 = (f32[12,512]{1,0:T(8,128)S(1)}, f32[12,512,1024]{2,1,0:T(8,128)}) fusion(f32[12,512,1024]{2,1,0:T(8,128)} %fusion.129, f32[12,512]{1,0:T(8,128)S(1)} %dynamic-slice_bitcast_fusion.2, pred[512,1024]{1,0:T(8,128)(4,1)S(1)} %broadcast_compare_fusion.5, bf16[1024,12,64]{0,2,1:T(8,128)(2,1)} %get-tuple-element.575, ...), kind=kOutput, calls=%fused_computation.19.clone.1 | convolution fusion | flops 836757504 | bytes 53264388 | tf_op jit(solution)/shard_map/while/body/eval_jaxpr/qhd,khd->hqk/dot_general | solution.py:237
  480.9 22.0 %multiply_convert_fusion.5 = bf16[12,512,1024]{2,1,0:T(8,128)(2,1)} fusion(f32[12,512,1024]{2,1,0:T(8,128)} %get-tuple-element.510, f32[12,512,1024]{2,1,0:T(8,128)} %fusion.129, f32[12,512]{1,0:T(8,128)S(1)} %get-tuple-element.511, f32[12,512]{1,0:T(8,128)S(1)} %dynamic-slice_bitcast_fusion.2, pred[512,1024]{1,0:T(8,128)(4,1)S(1)} %broadcast_compare_fusion.5), kind=kLoop, calls=%fused_computation.18.clone.1 | loop fusion | flops 37748736 | bytes 63488000 | tf_op jit(solution)/shard_map/while/body/eval_jaxpr/convert_element_type | solution.py:241
  502.8 9.5 bitcast_dynamic-update-slice_fusion.5
  512.4 8.6 bitcast_add_fusion.4
  522.5 11.5 fusion.129
  534.0 14.3 %bitcast_add_fusion.5 = f32[1024,12,64]{0,2,1:T(8,128)} fusion(f32[1024,12,64]{0,2,1:T(8,128)} %get-tuple-element.554, f32[12,512,1024]{2,1,0:T(8,128)} %fusion.129, f32[12,512]{1,0:T(8,128)S(1)} %dynamic-slice_bitcast_fusion.2, pred[512,1024]{1,0:T(8,128)(4,1)S(1)} %broadcast_compare_fusion.5, pred[]{:T(512)S(6)} %compare.3, ...), kind=kOutput, calls=%fused_computation.24.clone.1 | convolution fusion | flops 832045056 | bytes 32800772 | tf_op jit(solution)/shard_map/while/body/eval_jaxpr/hqk,qhd->khd/dot_general | solution.py:253
  548.3 18.1 %multiply_reduce_fusion.7 = (f32[12,512]{1,0:T(8,128)S(1)}, f32[12,512,1024]{2,1,0:T(8,128)}) fusion(f32[12,512,1024]{2,1,0:T(8,128)} %fusion.129, f32[12,512]{1,0:T(8,128)S(1)} %dynamic-slice_bitcast_fusion.2, pred[512,1024]{1,0:T(8,128)(4,1)S(1)} %broadcast_compare_fusion.5, bf16[1024,12,64]{0,2,1:T(8,128)(2,1)} %get-tuple-element.575, ...), kind=kOutput, calls=%fused_computation.19.clone.1 | convolution fusion | flops 836757504 | bytes 53264388 | tf_op jit(solution)/shard_map/while/body/eval_jaxpr/qhd,khd->hqk/dot_general | solution.py:237
  566.4 21.2 %multiply_convert_fusion.5 = bf16[12,512,1024]{2,1,0:T(8,128)(2,1)} fusion(f32[12,512,1024]{2,1,0:T(8,128)} %get-tuple-element.510, f32[12,512,1024]{2,1,0:T(8,128)} %fusion.129, f32[12,512]{1,0:T(8,128)S(1)} %get-tuple-element.511, f32[12,512]{1,0:T(8,128)S(1)} %dynamic-slice_bitcast_fusion.2, pred[512,1024]{1,0:T(8,128)(4,1)S(1)} %broadcast_compare_fusion.5), kind=kLoop, calls=%fused_computation.18.clone.1 | loop fusion | flops 37748736 | bytes 63488000 | tf_op jit(solution)/shard_map/while/body/eval_jaxpr/convert_element_type | solution.py:241
  587.7 9.5 bitcast_dynamic-update-slice_fusion.5
  597.1 9.5 bitcast_add_fusion.4
  606.8 3.1 copy.98
  613.0 2.0 copy.112
  615.0 2.2 convert_reduce_fusion.4
  618.4 2.8 convolution_bitcast_fusion
  621.3 3.2 copy.116
  627.9 2.0 copy.114
  630.0 14.3 %fusion.57 = f32[3072,768]{1,0:T(8,128)} fusion(bf16[1024,768]{0,1:T(8,128)(2,1)} %copy-done.23, f32[1024,3072]{1,0:T(8,128)} %fusion.55, f32[3072]{0:T(1024)S(1)} %copy-done.44), kind=kOutput, calls=%fused_computation.110 | convolution fusion | flops 4863295488 | bytes 23605248 | tf_op jit(solution)/shard_map/dot_general | solution.py:21
  644.4 1.8 copy-done.6
  646.2 10.8 fusion.53
  660.5 40.6 %all-reduce.18 = (f32[768]{0:T(1024)S(1)}, f32[768]{0:T(1024)S(1)}, f32[768]{0:T(1024)S(1)}, f32[768]{0:T(1024)S(1)}, f32[768]{0:T(1024)S(1)}, /*index=5*/f32[30...) all-reduce(f32[768]{0:T(1024)S(1)} %reduce_sum.194, ...), channel_id=3, replica_groups=mesh['dp'=4,'fsdp'=8] {'dp','fsdp'}, use_global_device_ids=true, to_apply=%region_19.20.clone | all-reduce | flops 9216 | bytes 73728
  705.8 2.8 fusion.61
  712.8 2.4 copy.103
  715.8 102.0 %reduce-scatter.23.cloned.1.call-done = f32[24,768]{1,0:T(8,128)} async-done(((f32[768,768]{1,0:T(8,128)}), f32[24,768]{1,0:T(8,128)}) %reduce-scatter.23.cloned.1.call-update) | async-done | bytes 73744
  817.7 104.7 %reduce-scatter.21.cloned.1.call-done = f32[24,768]{1,0:T(8,128)} async-done(((f32[768,768]{1,0:T(8,128)}), f32[24,768]{1,0:T(8,128)}) %reduce-scatter.21.cloned.1.call-update) | async-done | bytes 73744
  922.4 141.1 %reduce-scatter.17.cloned.1.call-done = f32[96,768]{1,0:T(8,128)} async-done(((f32[3072,768]{1,0:T(8,128)}), f32[96,768]{1,0:T(8,128)}) %reduce-scatter.17.cloned.1.call-update) | async-done | bytes 294928 | tf_op jit(solution)/shard_map/reduce_scatter | solution.py:99
  1063.5 142.0 %reduce-scatter.15.cloned.1.call-done = f32[24,3072]{1,0:T(8,128)} async-done(((f32[768,3072]{1,0:T(8,128)}), f32[24,3072]{1,0:T(8,128)}) %reduce-scatter.15.cloned.1.call-update) | async-done | bytes 294928 | tf_op jit(solution)/shard_map/reduce_scatter | solution.py:97
  (221 shorter events, 50.1 us)
Async XLA Ops:
  7.2 62.0 %copy-start.16 = (bf16[1024,768]{1,0:T(8,128)(2,1)S(1)}, bf16[1024,768]{1,0:T(8,128)(2,1)}, u32[]{:S(2)}) copy-start(bf16[1024,768]{1,0:T(8,128)(2,1)} %param.22) | copy-start | bytes 4718596
  7.2 63.6 %all-gather.7.cloned.1.call-start = ((), (), s32[]{:S(2)}) async-start(), calls=%async_computation.6 | async-start | bytes 1216512 | tf_op jit(solution)/shard_map/all_gather | solution.py:68
  7.9 116.3 %all-gather.9.cloned.1.call-start = ((), (), s32[]{:S(2)}) async-start(), calls=%async_computation.7 | async-start | bytes 1216512 | tf_op jit(solution)/shard_map/all_gather | solution.py:70
  8.7 171.8 %all-gather.11.cloned.1.call-start = ((), (), s32[]{:S(2)}) async-start(), calls=%async_computation.8 | async-start | bytes 1216512 | tf_op jit(solution)/shard_map/all_gather | solution.py:71
  9.4 250.7 %all-gather.13.cloned.1.call-start = ((), (), s32[]{:S(2)}) async-start(), calls=%async_computation.9 | async-start | bytes 1216512 | tf_op jit(solution)/shard_map/all_gather | solution.py:73
  10.0 292.0 %all-gather.15.cloned.1.call-start = ((), (), s32[]{:S(2)}) async-start(), calls=%async_computation.10 | async-start | bytes 4866048 | tf_op jit(solution)/shard_map/all_gather | solution.py:77
  10.6 356.8 %all-gather.17.cloned.1.call-start = ((), (), s32[]{:S(2)}) async-start(), calls=%async_computation.11 | async-start | bytes 4866048 | tf_op jit(solution)/shard_map/all_gather | solution.py:79
  11.2 704.6 %reduce-scatter.13.cloned.1.call-start = ((), (), s32[]{:S(2)}) async-start(), calls=%async_computation.12 | async-start | bytes 2433024 | tf_op jit(solution)/shard_map/reduce_scatter | solution.py:93
  185.2 23.0 %copy-start.7 = (bf16[1024,12,64]{0,2,1:T(8,128)(2,1)S(1)}, bf16[1024,12,64]{0,2,1:T(8,128)(2,1)}, u32[]{:S(2)}) copy-start(bf16[1024,12,64]{0,2,1:T(8,128)(2,1)} %get-tuple-element.537) | copy-start | bytes 4718596 | tf_op jit(solution)/shard_map/while
  195.9 15.4 %copy-start = (f32[12,512,1024]{2,1,0:T(8,128)S(1)}, f32[12,512,1024]{2,1,0:T(8,128)}, u32[]{:S(2)}) copy-start(f32[12,512,1024]{2,1,0:T(8,128)} %get-tuple-element.497) | copy-start | bytes 75497472 | tf_op jit(solution)/shard_map/while
  220.2 23.1 %copy-start.7 = (bf16[1024,12,64]{0,2,1:T(8,128)(2,1)S(1)}, bf16[1024,12,64]{0,2,1:T(8,128)(2,1)}, u32[]{:S(2)}) copy-start(bf16[1024,12,64]{0,2,1:T(8,128)(2,1)} %get-tuple-element.537) | copy-start | bytes 4718596 | tf_op jit(solution)/shard_map/while
  231.0 15.5 %copy-start = (f32[12,512,1024]{2,1,0:T(8,128)S(1)}, f32[12,512,1024]{2,1,0:T(8,128)}, u32[]{:S(2)}) copy-start(f32[12,512,1024]{2,1,0:T(8,128)} %get-tuple-element.497) | copy-start | bytes 75497472 | tf_op jit(solution)/shard_map/while
  255.5 4.6 copy-start.47
  264.0 1.7 copy-start.4
  264.0 38.0 %copy-start.29 = (f32[768]{0:T(1024)S(1)}, f32[768]{0:T(1024)}, u32[]{:S(2)}) copy-start(f32[768]{0:T(1024)} %convert_element_type.134) | copy-start | bytes 9220
  264.0 38.0 %copy-start.33 = (f32[768]{0:T(1024)S(1)}, f32[768]{0:T(1024)}, u32[]{:S(2)}) copy-start(f32[768]{0:T(1024)} %convert_element_type.135) | copy-start | bytes 9220
  264.1 150.6 %copy-start.27 = (f32[1024]{0:T(1024)}, f32[1024]{0:T(1024)S(1)}, u32[]{:S(2)}) copy-start(f32[1024]{0:T(1024)S(1)} %broadcast_multiply_fusion.5) | copy-start | bytes 12292
  266.1 148.6 %copy-start.31 = (f32[1024]{0:T(1024)}, f32[1024]{0:T(1024)S(1)}, u32[]{:S(2)}) copy-start(f32[1024]{0:T(1024)S(1)} %add_rsqrt_fusion.1) | copy-start | bytes 12292
  266.1 101.3 %copy-start.43 = (f32[3072]{0:T(1024)S(1)}, f32[3072]{0:T(1024)}, u32[]{:S(2)}) copy-start(f32[3072]{0:T(1024)} %convert_element_type.137) | copy-start | bytes 36868
  266.1 101.3 %copy-start.46 = (f32[768]{0:T(1024)S(1)}, f32[768]{0:T(1024)}, u32[]{:S(2)}) copy-start(f32[768]{0:T(1024)} %convert_element_type.139) | copy-start | bytes 9220
  379.5 1.4 copy-start.8
  379.5 5.2 slice-start.2
  380.9 3.9 slice-start.3
  382.8 19.5 %slice-start = ((s8[4718592]{0:T(1024)(128)(4,1)}), s8[4194304]{0:T(1024)(128)(4,1)S(1)}, s32[]{:S(2)}) async-start(s8[4718592]{0:T(1024)(128)(4,1)} %bitcast.149), calls=%async_computation.18 | async-start | bytes 8388608
  384.7 17.6 %copy-start.23 = (bf16[1024,768]{0,1:T(8,128)(2,1)}, bf16[1024,768]{0,1:T(8,128)(2,1)S(1)}, u32[]{:S(2)}) copy-start(bf16[1024,768]{0,1:T(8,128)(2,1)S(1)} %get-tuple-element.369) | copy-start | bytes 4718596
  384.7 17.6 %slice-start.1 = ((s8[4718592]{0:T(1024)(128)(4,1)}), s8[524288]{0:T(1024)(128)(4,1)S(1)}, s32[]{:S(2)}) async-start(s8[4718592]{0:T(1024)(128)(4,1)} %bitcast.149), calls=%async_computation.19 | async-start | bytes 1048576
  402.4 7.6 copy-start.5
  402.4 7.6 copy-start.36
  414.7 3.4 copy-start.22
  416.4 1.7 copy-start.10
  435.2 280.6 %reduce-scatter.19.cloned.1.call-start = ((), (), s32[]{:S(2)}) async-start(), calls=%async_computation.15 | async-start | bytes 2433024
  437.1 11.7 copy-start.9
  502.8 9.5 copy-start.3
  522.5 11.5 copy-start.9
  587.6 9.5 copy-start.3
  606.8 4.8 copy-start.17
  614.9 3.5 copy-start.18
  615.0 202.8 %reduce-scatter.23.cloned.1.call-start = ((), (), s32[]{:S(2)}) async-start(), calls=%async_computation.17 | async-start | bytes 2433024
  621.2 3.3 copy-start.1
  624.5 297.9 %reduce-scatter.21.cloned.1.call-start = ((), (), s32[]{:S(2)}) async-start(), calls=%async_computation.16 | async-start | bytes 2433024
  624.6 2.0 copy-start.19
  627.9 2.1 copy-start.44
  629.9 433.6 %reduce-scatter.17.cloned.1.call-start = ((), (), s32[]{:S(2)}) async-start(), calls=%async_computation.14 | async-start | bytes 9732096 | tf_op jit(solution)/shard_map/reduce_scatter | solution.py:99
  644.3 1.9 copy-start.6
  644.3 1.9 copy-start.28
  644.3 1.9 copy-start.30
  644.3 1.9 copy-start.32
  644.3 1.9 copy-start.34
  644.3 561.2 %reduce-scatter.15.cloned.1.call-start = ((), (), s32[]{:S(2)}) async-start(), calls=%async_computation.13 | async-start | bytes 9732096 | tf_op jit(solution)/shard_map/reduce_scatter | solution.py:97
  657.0 1.4 copy-start.12
  657.0 1.9 copy-start.13
  657.0 3.5 copy-start.37
  657.0 3.5 copy-start.38
  657.0 3.5 copy-start.39
  657.1 3.5 copy-start.40
  657.1 3.5 copy-start.41
  657.1 3.5 copy-start.42
  657.1 3.5 copy-start.45
  658.7 47.1 %copy-start.21 = (bf16[96,8,2,512]{3,1,2,0:T(8,128)(2,1)S(1)}, bf16[96,8,2,512]{3,1,2,0:T(8,128)(2,1)}, u32[]{:S(2)}) copy-start(bf16[96,8,2,512]{3,1,2,0:T(8,128)(2,1)} %copy-done.20) | copy-start | bytes 4718596
  705.8 2.8 copy-start.25
  705.8 2.8 copy-start.48
  708.7 1.9 copy-start.11
  708.7 2.4 copy-start.15
  708.7 2.7 copy-start.26
  (6 other events, 7.2 us)
Sparse Core Ops, SparseCore 0:
  11.1 57.0 all-gather.6
  71.2 53.0 all-gather.8
  127.3 53.1 all-gather.10
  183.3 53.1 all-gather.12
  239.4 62.6 all-gather.14
  304.9 62.4 all-gather.16
  435.3 97.8 reduce-scatter.12
  615.1 98.6 reduce-scatter.18
  719.7 98.0 reduce-scatter.22
  824.3 98.0 reduce-scatter.20
  928.9 134.5 reduce-scatter.16
  1070.9 134.6 reduce-scatter.14
where the time goes:
time: 1220 us; the launch traced here: 1210 us
  waiting for transfers between devices  683 us (56%)
  matrix products  269 us (22%)
  other arithmetic  88.3 us (7%)
  blocking collectives  83.2 us (7%)
  local copies, waits for them, and re-layouts  72.2 us (6%)
  between operations  15.1 us (1%)
    unnamed x15, waiting for transfers between devices  210 us
    reduce_scatter x1, waiting for transfers between devices, spread(): lax.psum_scatter(grads[9], ('dp', 'fsdp'), scatter_dimension=0, tiled=True)  142 us
    reduce_scatter x1, waiting for transfers between devices, spread(): lax.psum_scatter(grads[11], ('dp', 'fsdp'), scatter_dimension=0, tiled=True)  141 us
    unnamed x2, blocking collectives  83.2 us
    all_gather x1, waiting for transfers between devices, collect(): lax.all_gather(params[11], ('dp', 'fsdp'), axis=0, tiled=True)  54.4 us
    all_gather x1, waiting for transfers between devices, collect(): lax.all_gather(params[3], ('dp', 'fsdp'), axis=0, tiled=True)  53 us
    unnamed x133, local copies, waits for them, and re-layouts  46 us
    all_gather x1, waiting for transfers between devices, collect(): lax.all_gather(params[2], ('dp', 'fsdp'), axis=0, tiled=True)  45.9 us
  transfers between devices with their start and end apart: 12, of which 8 were waited for; matrix products, arithmetic and copies ran while one was open for 28% of the time, Pallas kernels for 0%

commit v1 on v0

v1 whole, which is shorter than its diff:
```python
import functools
import math

import jax
import jax.numpy as jnp
from jax import lax
from jax.experimental import pallas as pl
from jax.experimental.pallas import tpu as pltpu
from jax.sharding import PartitionSpec as P

HEAD_DIM = 64
GROUP = 256
PAIR = 128
EPSILON = 1e-06
MASKED = -1e30
LOG2E = 1.4426950408889634
AXES = ("dp", "fsdp")
BF, F32 = jnp.bfloat16, jnp.float32
MIB = 2**20


def dot(a, b, ca=1, cb=0):
    return lax.dot_general(a, b, (((ca,), (cb,)), ((), ())), preferred_element_type=F32)


def call(kernel, cost, vmem=40, **kw):
    return pl.pallas_call(
        kernel,
        compiler_params=pltpu.CompilerParams(vmem_limit_bytes=vmem * MIB),
        cost_estimate=pl.CostEstimate(flops=int(cost * 1e6 * 800), bytes_accessed=0, transcendentals=0),
        **kw,
    )


def seq_ends(len_ref, count):
    ends = [len_ref[0, 0]]
    for j in range(1, count):
        ends.append(ends[-1] + len_ref[0, j])
    return ends


def fill_segments(ends, seg_col, seg_row):
    at_col = lax.broadcasted_iota(jnp.int32, seg_col.shape, 0)
    at_row = lax.broadcasted_iota(jnp.int32, seg_row.shape, 1)
    col, row = jnp.zeros(seg_col.shape, jnp.int32), jnp.zeros(seg_row.shape, jnp.int32)
    for end in ends:
        col = col + (at_col >= end).astype(jnp.int32)
        row = row + (at_row >= end).astype(jnp.int32)
    seg_col[...] = col
    seg_row[...] = row


def key_range(ends, first, last, cases, total):
    low, high = jnp.int32(0), jnp.int32(total)
    for end in ends:
        low = jnp.maximum(low, jnp.where(end <= first, end, 0))
        high = jnp.minimum(high, jnp.where(end > last, end, total))
    start = lax.div(low, 128)
    need = lax.div(high + 127, 128) - start
    case, size = jnp.int32(0), jnp.int32(cases[0])
    for j in range(1, len(cases)):
        more = need > cases[j - 1]
        case = jnp.where(more, j, case)
        size = jnp.where(more, cases[j], size)
    start = jnp.minimum(start, total // 128 - size)
    return pl.multiple_of(start * 128, 128), case


def for_blocks(ends, total, rows_in_block, cases, block):
    cases = tuple(c for c in cases if c < total // 128) + (total // 128,)

    @pl.loop(0, total // rows_in_block)
    def _(i):
        first = i * rows_in_block
        start, case = key_range(ends, first, first + rows_in_block - 1, cases, total)
        for j, n in enumerate(cases):
            pl.when(case == j)(functools.partial(block, pl.multiple_of(first, rows_in_block), n, start))


def attend_kernel(len_ref, tok, w, bias, qkv, ctx, lse, seg_col, seg_row, *, bq, cases, nseq):
    total = tok.shape[0]
    ends = seq_ends(len_ref, nseq)
    fill_segments(ends, seg_col, seg_row)
    for part in range(3):
        cols = pl.ds(part * GROUP, GROUP)
        made = (dot(tok[...], w[:, cols]) + bias[:, cols]).astype(BF)
        qkv[:, cols] = made * BF(1.0 / math.sqrt(HEAD_DIM)) if part == 0 else made

    def block(first, n, start):
        nk = n * 128
        rows, keys = pl.ds(first, bq), pl.ds(start, nk)
        same = jnp.concatenate([seg_col[rows, :]] * n, 1) == seg_row[0:1, keys]
        lane = lax.broadcasted_iota(jnp.int32, (bq, PAIR), 1)
        stats = jnp.zeros((bq, PAIR), F32)
        for pair in range(2):
            q = qkv[rows, pl.ds(pair * PAIR, PAIR)]
            k = qkv[keys, pl.ds(GROUP + pair * PAIR, PAIR)]
            v = qkv[keys, pl.ds(2 * GROUP + pair * PAIR, PAIR)]
            v_ones = jnp.concatenate([v, jnp.ones((nk, PAIR), BF)], 1)
            outs = []
            for h in range(2):
                s = dot(jnp.where((lane < HEAD_DIM) == (h == 0), q, BF(0)), k, 1, 1)
                s = jnp.where(same, s, MASKED)
                top = jnp.max(s, axis=1, keepdims=True)
                o = dot(jnp.exp2((s - top) * LOG2E).astype(BF), v_ones)
                norm = o[:, PAIR:]
                outs.append(o[:, :PAIR] * (1.0 / norm))
                stats = jnp.where(lane == pair * 2 + h, top * LOG2E + jnp.log2(norm), stats)
            ctx[rows, pl.ds(pair * PAIR, PAIR)] = jnp.where(lane < HEAD_DIM, outs[0], outs[1]).astype(BF)
        lse[:, rows] = stats.T[0:8, :]

    for_blocks(ends, total, bq, cases, block)


def attend(lens, tok, w, bias, bq=256, cases=(2, 3, 4, 5, 6)):
    total = tok.shape[0]
    return call(
        functools.partial(attend_kernel, bq=bq, cases=cases, nseq=lens.shape[1]),
        9,
        in_specs=[pl.BlockSpec(memory_space=pltpu.SMEM)] + [pl.BlockSpec(memory_space=pltpu.VMEM)] * 3,
        out_shape=[
            jax.ShapeDtypeStruct((total, 3 * GROUP), BF),
            jax.ShapeDtypeStruct((total, GROUP), BF),
            jax.ShapeDtypeStruct((8, total), F32),
        ],
        scratch_shapes=[pltpu.VMEM((total, 128), jnp.int32), pltpu.VMEM((8, total), jnp.int32)],
        name="attend",
    )(lens, tok, w, bias)


def attend_back_kernel(
    len_ref, tok, w, out_w, qkv, ctx, lse_in, att_back, grad_in, dw, grad_out, sums,
    seg_col, seg_row, key_t, do, dqkv, dk_sum, dv_sum, p_s, ds_s, *, bq, cases, nseq, chunk=2,
):
    total = tok.shape[0]
    ends = seq_ends(len_ref, nseq)
    fill_segments(ends, seg_col, seg_row)
    do[...] = dot(att_back[...], out_w[...], 1, 1).astype(BF)
    key_t[...] = qkv[:, pl.ds(GROUP, GROUP)].T
    dk_sum[...] = jnp.zeros_like(dk_sum)
    dv_sum[...] = jnp.zeros_like(dv_sum)
    head = lax.broadcasted_iota(jnp.int32, (8, GROUP), 1) // HEAD_DIM == lax.broadcasted_iota(jnp.int32, (8, GROUP), 0)
    head = head.astype(BF)

    def block(first, n, start):
        nk = n * 128
        rows, keys = pl.ds(first, bq), pl.ds(start, nk)
        seg_q = seg_row[0:1, rows]
        lane = lax.broadcasted_iota(jnp.int32, (bq, PAIR), 1)
        both = do[rows, :].astype(F32) * ctx[rows, :].astype(F32)
        high = both.astype(BF)
        low = (both - high.astype(F32)).astype(BF)
        delta = dot(head, high, 1, 1) + dot(head, low, 1, 1)
        lse = lse_in[:, rows]
        dqs = []
        for pair in range(2):
            cols = pl.ds(pair * PAIR, PAIR)
            k_cols, v_cols = pl.ds(GROUP + pair * PAIR, PAIR), pl.ds(2 * GROUP + pair * PAIR, PAIR)
            q, g = qkv[rows, cols], do[rows, cols]
            qs, gs = [], []
            for h in range(2):
                head_at = pair * 2 + h
                mine = (lane < HEAD_DIM) == (h == 0)
                qs.append(jnp.where(mine, q, BF(0)))
                gs.append(jnp.where(mine, g, BF(0)))
                for c in range(0, n, chunk):
                    wide = min(chunk, n - c) * 128
                    some = pl.ds(pl.multiple_of(start + c * 128, 128), wide)
                    s = dot(qkv[some, k_cols], qs[h], 1, 1)
                    same = jnp.concatenate([seg_col[some, :]] * (bq // 128), 1) == seg_q
                    p = jnp.exp2(jnp.where(same, s * LOG2E - lse[head_at : head_at + 1, :], MASKED))
                    dp = dot(qkv[some, v_cols], gs[h], 1, 1)
                    p_s[pl.ds(c * 128, wide), pl.ds(h * bq, bq)] = p.astype(BF)
                    ds_s[pl.ds(c * 128, wide), pl.ds(h * bq, bq)] = (p * (dp - delta[head_at : head_at + 1, :])).astype(BF)
            for h in range(2):
                dqs.append(dot(key_t[pl.ds((pair * 2 + h) * HEAD_DIM, HEAD_DIM), keys], ds_s[pl.ds(0, nk), pl.ds(h * bq, bq)]))
            dv_sum[keys, cols] += dot(p_s[pl.ds(0, nk), :], jnp.concatenate(gs, 0))
            dk_sum[keys, cols] += dot(ds_s[pl.ds(0, nk), :], jnp.concatenate(qs, 0))
        dqkv[rows, pl.ds(0, GROUP)] = (jnp.concatenate(dqs, 0).T * (1.0 / math.sqrt(HEAD_DIM))).astype(BF)

    for_blocks(ends, total, bq, cases, block)
    dqkv[:, pl.ds(GROUP, GROUP)] = dk_sum[...].astype(BF)
    dqkv[:, pl.ds(2 * GROUP, GROUP)] = dv_sum[...].astype(BF)
    d = dqkv[...]
    sums[...] = jnp.broadcast_to(jnp.sum(d.astype(F32), axis=0, keepdims=True), sums.shape)
    dw[...] = dot(tok[...], d, 0, 0).astype(BF)
    grad_out[...] = grad_in[...] + dot(d, w[...], 1, 1)


def attend_back(lens, tok, w, out_w, group, qkv, ctx, lse, att_back, grad_in, bq=256, cases=(2, 3, 4, 5, 6)):
    total, width = tok.shape
    vmem = pl.BlockSpec(memory_space=pltpu.VMEM)
    return call(
        functools.partial(attend_back_kernel, bq=bq, cases=cases, nseq=lens.shape[1]),
        12,
        grid=(1,),
        in_specs=[pl.BlockSpec(memory_space=pltpu.SMEM), vmem, vmem, pl.BlockSpec((GROUP, width), lambda _: (group, 0))]
        + [vmem] * 5,
        out_specs=[vmem] * 3,
        out_shape=[
            jax.ShapeDtypeStruct((width, 3 * GROUP), BF),
            jax.ShapeDtypeStruct((total, width), F32),
            jax.ShapeDtypeStruct((8, 3 * GROUP), F32),
        ],
        scratch_shapes=[
            pltpu.VMEM((total, 128), jnp.int32),
            pltpu.VMEM((8, total), jnp.int32),
            pltpu.VMEM((GROUP, total), BF),
            pltpu.VMEM((total, GROUP), BF),
            pltpu.VMEM((total, 3 * GROUP), BF),
            pltpu.VMEM((total, GROUP), F32),
            pltpu.VMEM((total, GROUP), F32),
            pltpu.VMEM((total, 2 * bq), BF),
            pltpu.VMEM((total, 2 * bq), BF),
        ],
        name="attend_back",
    )(lens, tok, w, out_w, qkv, ctx, lse, att_back, grad_in)


def row_mean(value):
    return jnp.sum(value, axis=-1, keepdims=True) * (1.0 / value.shape[-1])


def norm(value):
    center = value - row_mean(value)
    inverse = lax.rsqrt(row_mean(center * center) + EPSILON)
    return center * inverse, inverse


def norm_back(upstream, normed, inverse, gain):
    scaled = upstream * gain
    return inverse * (scaled - row_mean(scaled) - normed * row_mean(scaled * normed))


def add_rows(sums, first, pieces):
    at = lax.broadcasted_iota(jnp.int32, sums.shape, 0)
    made = jnp.zeros(sums.shape, F32)
    for j, piece in enumerate(pieces):
        made = jnp.where(at == j, jnp.sum(piece, axis=0, keepdims=True), made)

    @pl.when(first)
    def _():
        sums[...] = made

    @pl.when(jnp.logical_not(first))
    def _():
        sums[...] += made


def entry_kernel(ctx0, ctx1, ctx2, tok, out_w, vecs, normed, inverse, low):
    ctx = jnp.concatenate([ctx0[...], ctx1[...], ctx2[...]], 1)
    total = tok[...].astype(F32) + (dot(ctx, out_w[...]) + vecs[2:3, :])
    n, r = norm(total)
    normed[...] = n
    inverse[...] = jnp.broadcast_to(r, inverse.shape)
    low[...] = (n * vecs[3:4, :] + vecs[4:5, :]).astype(BF)


def entry(ctxs, tok, out_w, vecs, rows=256):
    total, width = tok.shape
    at = lambda i: (i, 0)
    still = lambda i: (0, 0)
    return call(
        entry_kernel,
        3,
        grid=(total // rows,),
        in_specs=[pl.BlockSpec((rows, GROUP), at)] * 3
        + [pl.BlockSpec((rows, width), at), pl.BlockSpec((width, width), still), pl.BlockSpec(vecs.shape, still)],
        out_specs=[pl.BlockSpec((rows, width), at), pl.BlockSpec((rows, 128), at), pl.BlockSpec((rows, width), at)],
        out_shape=[
            jax.ShapeDtypeStruct((total, width), F32),
            jax.ShapeDtypeStruct((total, 128), F32),
            jax.ShapeDtypeStruct((total, width), BF),
        ],
        name="entry",
    )(*ctxs, tok, out_w, vecs)


ROOT = math.sqrt(2.0 / math.pi)


def expand_kernel(low, up, bias, act, slope, *, rows):
    @pl.loop(0, low.shape[0] // rows)
    def _(i):
        at = pl.ds(pl.multiple_of(i * rows, rows), rows)
        x = dot(low[at, :], up[...]) + bias[...]
        square = x * x
        t = jnp.tanh(x * (ROOT + (ROOT * 0.044715) * square))
        half = 0.5 * x
        act[at, :] = (half + half * t).astype(BF)
        slope[at, :] = (0.5 + 0.5 * t + half * (1.0 - t * t) * (ROOT + (3.0 * ROOT * 0.044715) * square)).astype(BF)


def expand(low, up, bias, wide=512, rows=256):
    total, width = low.shape
    hidden = up.shape[1]
    at = lambda j: (0, j)
    return call(
        functools.partial(expand_kernel, rows=rows),
        7,
        grid=(hidden // wide,),
        in_specs=[pl.BlockSpec((total, width), lambda j: (0, 0)), pl.BlockSpec((width, wide), at), pl.BlockSpec((1, wide), at)],
        out_specs=[pl.BlockSpec((total, wide), at)] * 2,
        out_shape=[jax.ShapeDtypeStruct((total, hidden), BF)] * 2,
        name="expand",
    )(low, up, bias)


def shrink_kernel(act, down, normed, vecs, out_grad, output, back, back_low, sums):
    middle = normed[...] * vecs[3:4, :] + vecs[4:5, :]
    n, r = norm(middle + (dot(act[...], down[...]) + vecs[5:6, :]))
    output[...] = (n * vecs[6:7, :] + vecs[7:8, :]).astype(BF)
    upstream = out_grad[...].astype(F32)
    second = norm_back(upstream, n, r, vecs[6:7, :])
    back[...] = second
    low = second.astype(BF)
    back_low[...] = low
    add_rows(sums, pl.program_id(0) == 0, (upstream * n, upstream, low.astype(F32)))


def shrink(act, down, normed, vecs, out_grad, rows=256):
    total, width = normed.shape
    hidden = act.shape[1]
    at = lambda i: (i, 0)
    still = lambda i: (0, 0)
    block = pl.BlockSpec((rows, width), at)
    return call(
        shrink_kernel,
        7,
        grid=(total // rows,),
        in_specs=[
            pl.BlockSpec((rows, hidden), at),
            pl.BlockSpec((hidden, width), still),
            block,
            pl.BlockSpec(vecs.shape, still),
            block,
        ],
        out_specs=[block, block, block, pl.BlockSpec((8, width), still)],
        out_shape=[
            jax.ShapeDtypeStruct((total, width), BF),
            jax.ShapeDtypeStruct((total, width), F32),
            jax.ShapeDtypeStruct((total, width), BF),
            jax.ShapeDtypeStruct((8, width), F32),
        ],
        name="shrink",
    )(act, down, normed, vecs, out_grad)


def down_grad_kernel(act, back_low, dw):
    dw[...] = dot(act[...], back_low[...], 0, 0).astype(BF)


def down_grad(act, back_low, wide=512):
    total, hidden = act.shape
    width = back_low.shape[1]
    return call(
        down_grad_kernel,
        6,
        grid=(hidden // wide,),
        in_specs=[pl.BlockSpec((total, wide), lambda j: (0, j)), pl.BlockSpec((total, width), lambda j: (0, 0))],
        out_specs=pl.BlockSpec((wide, width), lambda j: (j, 0)),
        out_shape=jax.ShapeDtypeStruct((hidden, width), BF),
        name="down_grad",
    )(act, back_low)


def expand_back_kernel(back_low, down, slope, low, up, dw, back, sums, low_t, ex):
    j = pl.program_id(0)

    @pl.when(j == 0)
    def _():
        low_t[...] = low[...].T
        back[...] = jnp.zeros_like(back)

    ex[...] = (dot(back_low[...], down[...], 1, 1) * slope[...].astype(F32)).astype(BF)
    e = ex[...]
    sums[...] = jnp.broadcast_to(jnp.sum(e.astype(F32), axis=0, keepdims=True), sums.shape)
    dw[...] = dot(low_t[...], e).astype(BF)
    back[...] += dot(e, up[...], 1, 1)


def expand_back(back_low, down, slope, low, up, wide=512):
    total, width = low.shape
    hidden = up.shape[1]
    still = lambda j: (0, 0)
    at = lambda j: (0, j)
    return call(
        expand_back_kernel,
        16,
        grid=(hidden // wide,),
        in_specs=[
            pl.BlockSpec((total, width), still),
            pl.BlockSpec((wide, width), lambda j: (j, 0)),
            pl.BlockSpec((total, wide), at),
            pl.BlockSpec((total, width), still),
            pl.BlockSpec((width, wide), at),
        ],
        out_specs=[pl.BlockSpec((width, wide), at), pl.BlockSpec((total, width), still), pl.BlockSpec((8, wide), at)],
        out_shape=[
            jax.ShapeDtypeStruct((width, hidden), BF),
            jax.ShapeDtypeStruct((total, width), F32),
            jax.ShapeDtypeStruct((8, hidden), F32),
        ],
        scratch_shapes=[pltpu.VMEM((width, total), BF), pltpu.VMEM((total, wide), BF)],
        name="expand_back",
    )(back_low, down, slope, low, up)


def entry_back_kernel(second, expand_part, normed, inverse, ctx0, ctx1, ctx2, vecs, entry_grad, low, dw, sums, *, rows):
    @pl.loop(0, second.shape[0] // rows)
    def _(i):
        at = pl.ds(pl.multiple_of(i * rows, rows), rows)
        upstream = second[at, :] + expand_part[at, :].astype(BF).astype(F32)
        n = normed[at, :]
        made = norm_back(upstream, n, inverse[at, 0:1], vecs[3:4, :])
        entry_grad[at, :] = made
        rounded = made.astype(BF)
        low[at, :] = rounded
        add_rows(sums, i == 0, (upstream * n, upstream, rounded.astype(F32)))

    for g, ctx in enumerate((ctx0, ctx1, ctx2)):
        dw[pl.ds(g * GROUP, GROUP), :] = dot(ctx[...], low[...], 0, 0).astype(BF)


def entry_back(second, expand_part, normed, inverse, ctxs, vecs, rows=128):
    total, width = second.shape
    vmem = pl.BlockSpec(memory_space=pltpu.VMEM)
    return call(
        functools.partial(entry_back_kernel, rows=rows),
        5,
        in_specs=[vmem] * 8,
        out_specs=[vmem] * 4,
        out_shape=[
            jax.ShapeDtypeStruct((total, width), F32),
            jax.ShapeDtypeStruct((total, width), BF),
            jax.ShapeDtypeStruct((width, width), BF),
            jax.ShapeDtypeStruct((8, width), F32),
        ],
        name="entry_back",
    )(second, expand_part, normed, inverse, *ctxs, vecs)


class Cube:
    def __init__(self, mesh):
        self.n_dp, self.n_fsdp = mesh.shape["dp"], mesh.shape["fsdp"]
        self.n = self.n_dp * self.n_fsdp
        self.bits = self.n.bit_length() - 1
        inner = self.n_fsdp.bit_length() - 1
        assert self.n == 1 << self.bits and self.n_fsdp == 1 << inner
        self.near = list(range(1, inner))
        self.far = list(range(inner, self.bits))

    def swap(self, value, bit):
        return lax.ppermute(value, AXES, [(i, i ^ (1 << bit)) for i in range(self.n)])

    def my_bit(self, bit):
        return (lax.axis_index(AXES) >> bit) & 1

    def gather(self, piece, order):
        done = []
        for bit in order:
            other = self.swap(piece, bit)
            at = sum(b > bit for b in done)
            mine_last = self.my_bit(bit) == 1
            piece = jnp.stack([jnp.where(mine_last, other, piece), jnp.where(mine_last, piece, other)], at)
            done.append(bit)
        return piece.reshape(self.n, *piece.shape[self.bits :])

    def scatter(self, whole, order):
        part = whole.reshape((2,) * self.bits + (whole.shape[0] // self.n,) + whole.shape[1:])
        left = list(range(self.bits - 1, -1, -1))
        for bit in order:
            at = left.index(bit)
            left.pop(at)
            mine = self.my_bit(bit)
            keep = lax.dynamic_index_in_dim(part, mine, at, keepdims=False)
            give = lax.dynamic_index_in_dim(part, 1 - mine, at, keepdims=False)
            total = keep.astype(F32) + self.swap(give, bit).astype(F32)
            part = total.astype(BF) if left else total
        return part


def body(cube, *args):
    (
        tokens, seq_lengths, query_weight, query_bias, key_weight, value_weight, value_bias, out_weight, out_bias,
        first_gain, first_shift, up_weight, up_bias, down_weight, down_bias, second_gain, second_shift, out_grad,
    ) = args
    n = cube.n
    width = tokens.shape[1]
    own = width // n
    groups = width // GROUP
    hidden = up_weight.shape[1]
    inward = cube.near[::-1] + cube.far + [0]
    outward = [0] + cube.far + cube.near

    vec_own = jnp.concatenate(
        [query_bias, value_bias, out_bias, first_gain, first_shift, down_bias, second_gain, second_shift, up_bias]
    )
    vec_rows = jnp.pad(vec_own[None], ((0, 7), (0, width - vec_own.shape[0])))
    split = [[m[:, g * GROUP : (g + 1) * GROUP] for g in range(groups)] for m in (query_weight, key_weight, value_weight)]
    packs = [jnp.concatenate([m[g] for m in split], 1) for g in range(groups)]
    first = jnp.concatenate([*packs, vec_rows], 0)
    rest = jnp.concatenate([out_weight, up_weight.reshape(-1, width), down_weight], 0)
    rest_all = lax.all_gather(rest, AXES, axis=0).reshape(n, -1, width)
    first_all = cube.gather(first, inward)
    group_w = [first_all[:, g * own : (g + 1) * own].reshape(width, 3 * GROUP) for g in range(groups)]
    vec_all = first_all[:, groups * own].astype(F32)
    vecs = vec_all[:, : 8 * own].reshape(n, 8, own).transpose(1, 0, 2).reshape(8, width)
    up_b = vec_all[:, 8 * own : 8 * own + hidden // n].reshape(1, hidden)

    zero = jnp.zeros((GROUP,), F32)
    made = []
    for g in range(groups):
        cols = slice(g * GROUP, (g + 1) * GROUP)
        bias = jnp.concatenate([vecs[0, cols], zero, vecs[1, cols]])[None]
        made.append(attend(seq_lengths, tokens, group_w[g], bias))
    ctxs = [m[1] for m in made]
    out_w = rest_all[:, :own].reshape(width, width)
    up = rest_all[:, own : own + own * hidden // width].reshape(width, hidden)
    down = rest_all[:, own + own * hidden // width :].reshape(hidden, width)
    normed, inverse, low = entry(ctxs, tokens, out_w, vecs)
    act, slope = expand(low, up, up_b)
    output, second, back_low, sums_two = shrink(act, down, normed, vecs, out_grad)

    down_dw = down_grad(act, back_low)
    own_down = cube.scatter(down_dw, outward)
    up_dw, expand_part, up_sums = expand_back(back_low, down, slope, low, up)
    own_up = cube.scatter(up_dw, outward)
    grad, att_back, out_dw, sums_one = entry_back(second, expand_part, normed, inverse, ctxs, vecs)
    own_out = cube.scatter(out_dw, outward)
    dws, sums_qkv = [], []
    for g in range(groups):
        qkv, ctx, lse = made[g]
        dw, grad, sums = attend_back(seq_lengths, tokens, group_w[g], out_w, g, qkv, ctx, lse, att_back, grad)
        dws.append(dw.reshape(n, own, 3 * GROUP))
        sums_qkv.append(sums[0])
    query_sum = jnp.concatenate([s[:GROUP] for s in sums_qkv])
    value_sum = jnp.concatenate([s[2 * GROUP :] for s in sums_qkv])
    vec_sums = jnp.stack([query_sum, value_sum, sums_one[2], sums_one[0], sums_one[1], sums_two[2], sums_two[0], sums_two[1]])
    vec_sums = vec_sums.reshape(8, n, own).transpose(1, 0, 2).reshape(n, 8 * own)
    vec_sums = jnp.concatenate([vec_sums, up_sums[0].reshape(n, hidden // n)], 1)
    vec_sums = jnp.pad(vec_sums[:, None], ((0, 0), (0, 7), (0, width - vec_sums.shape[1]))).astype(BF)
    last = jnp.concatenate([*dws, vec_sums], 1)
    own_last = cube.scatter(last.reshape(-1, width), outward)
    own_packs = [own_last[g * own : (g + 1) * own] for g in range(groups)]
    own_q, own_k, own_v = [
        jnp.concatenate([p[:, part * GROUP : (part + 1) * GROUP] for p in own_packs], 1) for part in range(3)
    ]
    own_vec = [own_last[groups * own, j * own : (j + 1) * own] for j in range(8)]
    own_up_b = own_last[groups * own, 8 * own : 8 * own + hidden // n]
    q_b, v_b, out_b, gain_one, shift_one, down_b, gain_two, shift_two = own_vec
    return (
        output, grad, own_q, q_b, own_k, own_v, v_b, own_out, out_b, gain_one, shift_one,
        own_up, own_up_b, own_down, down_b, gain_two, shift_two,
    )


def solution(mesh):
    both = P(AXES)
    rows = P(AXES, None)
    matrix, vector = rows, both
    in_specs = (
        rows, rows, matrix, vector, matrix, matrix, vector, matrix, vector, vector, vector,
        matrix, vector, matrix, vector, vector, vector, rows,
    )
    out_specs = (
        rows, rows, matrix, vector, matrix, matrix, vector, matrix, vector, vector, vector,
        matrix, vector, matrix, vector, vector, vector,
    )
    return jax.shard_map(
        functools.partial(body, Cube(mesh)), mesh=mesh, in_specs=in_specs, out_specs=out_specs, check_vma=False
    )
```

time: 1220 us -> 458 us (0.38)
  waiting for transfers between devices: 683 us -> 145 us
  matrix products: 269 us -> 0 us
  Pallas kernels: 0 us -> 127 us
  blocking collectives: 83.2 us -> 0 us
  other arithmetic: 88.3 us -> 29.9 us
  starting transfers between devices: 0.47 us -> 55.1 us
    reduce_scatter x3 -> x0, waiting for transfers between devices: 283 us -> none  [the longest x1 142 us: spread(): lax.psum_scatter(grads[9], ('dp', 'fsdp'), scatter_dimension=0, tiled=True)]
    dot_general x32 -> x0, matrix products: 269 us -> none  [the longest x4 44.6 us: block_scores(): jnp.einsum('qhd,khd->hqk', query_block, key_heads, preferred_element_type...]
    unnamed x15 -> x1, waiting for transfers between devices: 210 us -> 0.02 us
    all_gather x6 -> x1, waiting for transfers between devices: 189 us -> 0.01 us  [body(): rest_all = lax.all_gather(rest, AXES, axis=0).reshape(n, -1, width)]
    ppermute x0 -> x25, waiting for transfers between devices: none -> 145 us  [swap(): return lax.ppermute(value, AXES, [(i, i ^ 1 << bit) for i in range(self.n)])]
    pallas_call x0 -> x12, Pallas kernels: none -> 127 us  [the longest x3 42.1 us: attend_back(): call(functools.partial(attend_back_kernel, bq=bq, cases=cases, nseq=lens....]
    unnamed x2 -> x0, blocking collectives: 83.2 us -> none
    ppermute x0 -> x25, starting transfers between devices: none -> 55.1 us  [swap(): return lax.ppermute(value, AXES, [(i, i ^ 1 << bit) for i in range(self.n)])]
  transfers between devices with their start and end apart: 12 -> 26, of which waited for: 8 -> 17; matrix products, arithmetic and copies ran while one was open for 28% -> 11% of each run, Pallas kernels for 0% -> 14%
where the time goes in v1:
time: 458 us; the launch traced here: 452 us
  waiting for transfers between devices  145 us (32%)
  Pallas kernels  127 us (28%)
  local copies, waits for them, and re-layouts  79.4 us (17%)
  starting transfers between devices  55.1 us (12%)
  other arithmetic  29.9 us (7%)
  between operations  15.2 us (3%)
    ppermute x25, waiting for transfers between devices, swap(): return lax.ppermute(value, AXES, [(i, i ^ 1 << bit) for i in range(self.n)])  145 us
    ppermute x25, starting transfers between devices, swap(): return lax.ppermute(value, AXES, [(i, i ^ 1 << bit) for i in range(self.n)])  55.1 us
    pallas_call x3, Pallas kernels, attend_back(): call(functools.partial(attend_back_kernel, bq=bq, cases=cases, nseq=lens....  42.1 us
    unnamed x130, local copies, waits for them, and re-layouts  34.3 us
    pallas_call x3, Pallas kernels, attend(): call(functools.partial(attend_kernel, bq=bq, cases=cases, nseq=lens.shape...  22.4 us
    pallas_call x1, Pallas kernels, expand_back(): call(expand_back_kernel, 16, grid=(hidden // wide,), in_specs=[pl.BlockSp...  19.1 us
    pallas_call x1, Pallas kernels, expand(): call(functools.partial(expand_kernel, rows=rows), 7, grid=(hidden // wide...  17.4 us
    convert_element_type x16, other arithmetic, scatter(): part = total.astype(BF) if left else total  14.2 us
  transfers between devices with their start and end apart: 26, of which 17 were waited for; matrix products, arithmetic and copies ran while one was open for 11% of the time, Pallas kernels for 14%

profile of v1, /device:TPU:0, one launch (start us, length us, event | category | flops | bytes accessed | tf_op | source)
XLA Modules:
  0.0 451.7 jit_solution(5464118810918110153)
XLA Ops:
  8.2 1.7 pad_maximum_fusion.5
  9.9 6.1 %concatenate.65 = bf16[288]{0:T(512)(128)(2,1)S(1)} concatenate(bf16[24]{0:T(256)(128)(2,1)} %param.21, bf16[24]{0:T(256)(128)(2,1)} %param.24, bf16[24]{0:T(256)(128)(2,1)} %param.26, bf16[24]{0:T(256)(128)(2,1)} %param.27, bf16[24]{0:T(256)(128)(2,1)} %param.28, bf16[24]{0:T(256)(128)(2,1)} %param.32, bf16[24]{0:T(256)(128)(2,1)} %param.33, bf16[24]{0:T(256)(128)(2,1)} %param.34, ...), dimensions={0} | concatenate | bytes 1152 | tf_op jit(solution)/shard_map/concatenate | solution.py:496
  17.6 4.1 collective-permute-start
  21.7 8.5 %collective-permute-done = bf16[80,768]{1,0:T(8,128)(2,1)S(1)} collective-permute-done((bf16[80,768]{1,0:T(8,128)(2,1)S(1)}, bf16[80,768]{1,0:T(8,128)(2,1)S(1)}, u32[]{:S(2)}, u32[]{:S(2)}) %collective-permute-start) | collective-permute-done | bytes 122912 | tf_op jit(solution)/shard_map/ppermute | solution.py:454
  30.2 3.1 collective-permute-start.1
  33.3 7.4 %collective-permute-done.1 = bf16[2,80,768]{2,1,0:T(8,128)(2,1)S(1)} collective-permute-done((bf16[2,80,768]{2,1,0:T(8,128)(2,1)S(1)}, bf16[2,80,768]{2,1,0:T(8,128)(2,1)S(1)}, u32[]{:S(2)}, u32[]{:S(2)}) %collective-permute-start.1) | collective-permute-done | bytes 245792 | tf_op jit(solution)/shard_map/ppermute | solution.py:454
  42.4 20.3 %collective-permute-done.2 = bf16[2,2,80,768]{3,2,1,0:T(8,128)(2,1)S(1)} collective-permute-done((bf16[2,2,80,768]{3,2,1,0:T(8,128)(2,1)S(1)}, bf16[2,2,80,768]{3,2,1,0:T(8,128)(2,1)S(1)}, u32[]{:S(2)}, u32[]{:S(2)}) %collective-permute-start.2) | collective-permute-done | bytes 491552 | tf_op jit(solution)/shard_map/ppermute | solution.py:454
  64.4 28.3 %collective-permute-done.3 = bf16[2,2,2,80,768]{4,3,2,1,0:T(8,128)(2,1)} collective-permute-done((bf16[2,2,2,80,768]{4,3,2,1,0:T(8,128)(2,1)S(1)}, bf16[2,2,2,80,768]{4,3,2,1,0:T(8,128)(2,1)}, u32[]{:S(2)}, u32[]{:S(2)}) %collective-permute-start.3) | collective-permute-done | bytes 983072 | tf_op jit(solution)/shard_map/ppermute | solution.py:454
  95.5 4.3 collective-permute-done.4
  99.8 1.8 select_bitcast_fusion.1
  101.6 2.3 pad_maximum_fusion
  105.5 2.4 fusion.23
  108.0 7.4 %attend.5 = (bf16[1024,768]{1,0:T(8,128)(2,1)S(1)}, bf16[1024,256]{1,0:T(8,128)(2,1)S(1)}, f32[8,1024]{1,0:T(8,128)S(1)}) custom-call(s32[1,9]{1,0:T(1,128)S(1)} %copy-done.15, bf16[1024,768]{1,0:T(8,128)(2,1)S(1)} %copy-done.12, bf16[768,768]{1,0:T(8,128)(2,1)S(1)} %bitcast.189, f32[1,768]{1,0:T(1,128)S(1)} %broadcast_in_dim.23.bias), custom_call_target="tpu_custom_call" | custom-call | flops 7200000000 | tf_op jit(solution)/shard_map/attend/pallas_call | solution.py:117
  116.8 7.5 %attend.4 = (bf16[1024,768]{1,0:T(8,128)(2,1)S(1)}, bf16[1024,256]{1,0:T(8,128)(2,1)S(1)}, f32[8,1024]{1,0:T(8,128)S(1)}) custom-call(s32[1,9]{1,0:T(1,128)S(1)} %copy-done.15, bf16[1024,768]{1,0:T(8,128)(2,1)S(1)} %copy-done.12, bf16[768,768]{1,0:T(8,128)(2,1)S(1)} %bitcast.191, f32[1,768]{1,0:T(1,128)S(1)} %broadcast_in_dim.22.bias), custom_call_target="tpu_custom_call" | custom-call | flops 7200000000 | tf_op jit(solution)/shard_map/attend/pallas_call | solution.py:117
  126.9 7.6 %attend.3 = (bf16[1024,768]{1,0:T(8,128)(2,1)S(1)}, bf16[1024,256]{1,0:T(8,128)(2,1)S(1)}, f32[8,1024]{1,0:T(8,128)S(1)}) custom-call(s32[1,9]{1,0:T(1,128)S(1)} %copy-done.15, bf16[1024,768]{1,0:T(8,128)(2,1)S(1)} %copy-done.12, bf16[768,768]{1,0:T(8,128)(2,1)S(1)} %bitcast.193, f32[1,768]{1,0:T(1,128)S(1)} %broadcast_in_dim.21.bias), custom_call_target="tpu_custom_call" | custom-call | flops 7200000000 | tf_op jit(solution)/shard_map/attend/pallas_call | solution.py:117
  137.1 2.4 slice.283
  139.5 8.1 %fusion.22 = (bf16[32,96,768]{2,1,0:T(8,128)(2,1)}, bf16[32,96,768]{2,1,0:T(8,128)(2,1)}) fusion(bf16[32,216,768]{2,1,0:T(8,128)(2,1)} %bitcast.204), kind=kLoop, calls=%fused_computation.127 | loop fusion | bytes 18874368 | tf_op jit(solution)/shard_map/slice | solution.py:520
  147.5 8.5 %reshape.167.up = bf16[768,3072]{1,0:T(8,128)(2,1)} reshape(bf16[32,96,768]{2,1,0:T(8,128)(2,1)} %get-tuple-element.92) | data formatting | bytes 9437184 | tf_op jit(solution)/shard_map/reshape | solution.py:519
  161.8 2.9 entry.1
  164.7 1.7 copy-done.17
  167.2 17.4 %expand.1 = (bf16[1024,3072]{1,0:T(8,128)(2,1)S(1)}, bf16[1024,3072]{1,0:T(8,128)(2,1)}) custom-call(bf16[1024,768]{1,0:T(8,128)(2,1)S(1)} %get-tuple-element.54.low, bf16[768,3072]{1,0:T(8,128)(2,1)S(1)} %copy-done.1, f32[1,3072]{1,0:T(1,128)S(1)} %reshape.168.bias), custom_call_target="tpu_custom_call" | custom-call | flops 5600000000 | tf_op jit(solution)/shard_map/expand/pallas_call | solution.py:298
  184.6 2.6 copy-done.21
  187.2 1.9 copy-done.18
  189.1 10.3 %shrink.1 = (bf16[1024,768]{1,0:T(8,128)(2,1)}, f32[1024,768]{1,0:T(8,128)S(1)}, bf16[1024,768]{1,0:T(8,128)(2,1)S(1)}, f32[8,768]{1,0:T(8,128)S(1)}) custom-call(bf16[1024,3072]{1,0:T(8,128)(2,1)} %copy-done.21, bf16[3072,768]{1,0:T(8,128)(2,1)S(1)} %bitcast.188, f32[1024,768]{1,0:T(8,128)S(1)} %copy-done.18, f32[8,768]{1,0:T(8,128)S(1)} %reshape.162.vecs, ...), custom_call_target="tpu_custom_call" | custom-call | flops 5600000000 | tf_op jit(solution)/shard_map/shrink/pallas_call | solution.py:327
  199.4 2.8 copy-done.22
  202.2 6.9 %down_grad.1 = bf16[3072,768]{1,0:T(8,128)(2,1)S(1)} custom-call(bf16[1024,3072]{1,0:T(8,128)(2,1)S(1)} %copy-done.22, bf16[1024,768]{1,0:T(8,128)(2,1)S(1)} %get-tuple-element.61.back_low), custom_call_target="tpu_custom_call" | custom-call | flops 4800000000 | tf_op jit(solution)/shard_map/down_grad/pallas_call | solution.py:356
  209.1 19.1 %expand_back.1 = (bf16[768,3072]{1,0:T(8,128)(2,1)S(1)}, f32[1024,768]{1,0:T(8,128)S(1)}, f32[8,3072]{1,0:T(8,128)S(1)}) custom-call(bf16[1024,768]{1,0:T(8,128)(2,1)S(1)} %get-tuple-element.61.back_low, bf16[3072,768]{1,0:T(8,128)(2,1)} %bitcast.185, bf16[1024,3072]{1,0:T(8,128)(2,1)} %get-tuple-element.62.slope, ...), custom_call_target="tpu_custom_call" | custom-call | flops 12800000000 | tf_op jit(solution)/shard_map/expand_back/pallas_call | solution.py:387
  228.2 2.1 copy-done
  230.3 1.7 copy-done.19
  232.0 1.9 copy-done.20
  233.9 5.8 %entry_back.1 = (f32[1024,768]{1,0:T(8,128)S(1)}, bf16[1024,768]{1,0:T(8,128)(2,1)S(1)}, bf16[768,768]{1,0:T(8,128)(2,1)S(1)}, f32[8,768]{1,0:T(8,128)S(1)}) custom-call(f32[1024,768]{1,0:T(8,128)S(1)} %get-tuple-element.60.second, f32[1024,768]{1,0:T(8,128)S(1)} %copy-done.20, f32[1024,768]{1,0:T(8,128)} %copy-done.17, f32[1024,128]{1,0:T(8,128)S(1)} %copy-done.35, ...), custom_call_target="tpu_custom_call" | custom-call | flops 4000000000 | tf_op jit(solution)/shard_map/entry_back/pallas_call | solution.py:428
  239.8 2.0 constant_dynamic-slice_fusion.1
  243.7 5.0 %collective-permute-start.20 = (bf16[2,2,2,2,96,768]{5,4,2,3,0,1:T(8,128)(2,1)}, bf16[2,2,2,2,96,768]{5,4,2,3,0,1:T(8,128)(2,1)}, u32[]{:S(2)}, u32[]{:S(2)}) collective-permute-start(bf16[2,2,2,2,96,768]{5,4,2,3,0,1:T(8,128)(2,1)} %bitcast.176), channel_id=1, source_target_pairs={{0,1},{1,0},{2,3},{3,2},{4,5},{5,4},{6,7},{7,6},{8,9},{9,8},{10,11... | collective-permute-start | bytes 7077896 | tf_op jit(solution)/shard_map/ppermute | solution.py:454
  250.6 12.8 %attend_back.3 = (bf16[768,768]{1,0:T(8,128)(2,1)S(1)}, f32[1024,768]{1,0:T(8,128)S(1)}, f32[8,768]{1,0:T(8,128)S(1)}) custom-call(s32[1,9]{1,0:T(1,128)S(1)} %copy-done.15, bf16[1024,768]{1,0:T(8,128)(2,1)S(1)} %copy-done.14, bf16[768,768]{1,0:T(8,128)(2,1)S(1)} %bitcast.194, bf16[768,768]{1,0:T(8,128)(2,1)S(1)} %bitcast.196, ...), custom_call_target="tpu_custom_call" | custom-call | flops 9600000000 | tf_op jit(solution)/shard_map/attend_back/pallas_call | solution.py:193
  263.4 1.7 copy-done.36
  265.0 16.4 %attend_back.4 = (bf16[768,768]{1,0:T(8,128)(2,1)S(1)}, f32[1024,768]{1,0:T(8,128)S(1)}, f32[8,768]{1,0:T(8,128)S(1)}) custom-call(s32[1,9]{1,0:T(1,128)S(1)} %copy-done.15, bf16[1024,768]{1,0:T(8,128)(2,1)S(1)} %copy-done.14, bf16[768,768]{1,0:T(8,128)(2,1)S(1)} %bitcast.192, bf16[768,768]{1,0:T(8,128)(2,1)S(1)} %bitcast.197, ...), custom_call_target="tpu_custom_call" | custom-call | flops 9600000000 | tf_op jit(solution)/shard_map/attend_back/pallas_call | solution.py:193
  281.5 1.8 copy-done.24
  283.3 12.9 %attend_back.5 = (bf16[768,768]{1,0:T(8,128)(2,1)S(1)}, f32[1024,768]{1,0:T(8,128)}, f32[8,768]{1,0:T(8,128)S(1)}) custom-call(s32[1,9]{1,0:T(1,128)S(1)} %copy-done.15, bf16[1024,768]{1,0:T(8,128)(2,1)S(1)} %copy-done.14, bf16[768,768]{1,0:T(8,128)(2,1)S(1)} %bitcast.190, bf16[768,768]{1,0:T(8,128)(2,1)S(1)} %bitcast.198, bf16[1024,768]{1,0:T(8,128)(2,1)S(1)} %copy-done.38, ...), custom_call_target="tpu_custom_call" | custom-call | flops 9600000000 | tf_op jit(solution)/shard_map/attend_back/pallas_call | solution.py:193
  300.1 1.6 constant_dynamic-slice_fusion.7
  303.1 4.8 %collective-permute-start.5 = (bf16[2,2,2,2,80,768]{5,4,2,3,0,1:T(8,128)(2,1)}, bf16[2,2,2,2,80,768]{5,4,2,3,0,1:T(8,128)(2,1)}, u32[]{:S(2)}, u32[]{:S(2)}) collective-permute-start(bf16[2,2,2,2,80,768]{5,4,2,3,0,1:T(8,128)(2,1)} %bitcast.178), channel_id=1, source_target_pairs={{0,1},{1,0},{2,3},{3,2},{4,5},{5,4},{6,7},{7,6},{8,9},{9,8},{10,11... | collective-permute-start | bytes 5898248 | tf_op jit(solution)/shard_map/ppermute | solution.py:454
  311.1 2.8 collective-permute-start.11
  313.8 7.7 %collective-permute-done.11 = bf16[2,2,2,24,768]{4,3,1,2,0:T(8,128)(2,1)S(1)} collective-permute-done((bf16[2,2,2,24,768]{4,3,1,2,0:T(8,128)(2,1)S(1)}, bf16[2,2,2,24,768]{4,3,1,2,0:T(8,128)(2,1)S(1)}, u32[]{:S(2)}, u32[]{:S(2)}) %collective-permute-start.11) | collective-permute-done | bytes 294944 | tf_op jit(solution)/shard_map/ppermute | solution.py:454
  323.1 4.2 collective-permute-done.12
  327.5 2.8 fusion.2
  330.4 1.6 collective-permute-start.6
  332.0 2.4 fusion
  336.1 2.6 fusion.1
  341.4 13.7 %collective-permute-done.6 = bf16[2,2,2,80,768]{4,3,1,2,0:T(8,128)(2,1)S(1)} collective-permute-done((bf16[2,2,2,80,768]{4,3,1,2,0:T(8,128)(2,1)S(1)}, bf16[2,2,2,80,768]{4,3,1,2,0:T(8,128)(2,1)S(1)}, u32[]{:S(2)}, u32[]{:S(2)}) %collective-permute-start.6) | collective-permute-done | bytes 983072 | tf_op jit(solution)/shard_map/ppermute | solution.py:454
  357.8 6.9 %collective-permute-start.14 = (bf16[24,768]{1,0:T(8,128)(2,1)S(1)}, bf16[24,768]{1,0:T(8,128)(2,1)S(1)}, u32[]{:S(2)}, u32[]{:S(2)}) collective-permute-start(bf16[24,768]{1,0:T(8,128)(2,1)S(1)} %dynamic-slice_bitcast_fusion.15), channel_id=1, source_target_pairs={{0,4},{1,5},{2,6},{3,7},{4,0},{5,1},{6,2},{7,3},{8,12},{9,13},{10,... | collective-permute-start | bytes 110600 | tf_op jit(solution)/shard_map/ppermute | solution.py:454
  364.8 2.0 collective-permute-done.14
  368.6 2.0 collective-permute-start.8
  370.6 9.9 %collective-permute-done.21 = bf16[2,2,2,96,768]{4,3,1,2,0:T(8,128)(2,1)} collective-permute-done((bf16[2,2,2,96,768]{4,3,1,2,0:T(8,128)(2,1)}, bf16[2,2,2,96,768]{4,3,1,2,0:T(8,128)(2,1)}, u32[]{:S(2)}, u32[]{:S(2)}) %collective-permute-start.21) | collective-permute-done | bytes 1179680 | tf_op jit(solution)/shard_map/ppermute | solution.py:454
  382.1 1.7 collective-permute-start.22
  383.8 20.0 %collective-permute-done.16 = bf16[2,2,2,24,3072]{4,3,1,2,0:T(8,128)(2,1)} collective-permute-done((bf16[2,2,2,24,3072]{4,3,1,2,0:T(8,128)(2,1)}, bf16[2,2,2,24,3072]{4,3,1,2,0:T(8,128)(2,1)}, u32[]{:S(2)}, u32[]{:S(2)}) %collective-permute-start.16) | collective-permute-done | bytes 1179680 | tf_op jit(solution)/shard_map/ppermute | solution.py:454
  403.8 1.7 fusion.4
  405.6 6.5 %collective-permute-start.9 = (bf16[80,768]{1,0:T(8,128)(2,1)S(1)}, bf16[80,768]{1,0:T(8,128)(2,1)S(1)}, u32[]{:S(2)}, u32[]{:S(2)}) collective-permute-start(bf16[80,768]{1,0:T(8,128)(2,1)S(1)} %dynamic-slice_bitcast_fusion.13), channel_id=1, source_target_pairs={{0,4},{1,5},{2,6},{3,7},{4,0},{5,1},{6,2},{7,3},{8,12},{9,13},{10,... | collective-permute-start | bytes 368648 | tf_op jit(solution)/shard_map/ppermute | solution.py:454
  413.4 2.9 collective-permute-done.9
  420.7 4.3 collective-permute-done.17
  426.7 3.1 collective-permute-done.23
  429.9 2.2 collective-permute-start.24
  432.1 2.2 collective-permute-done.18
  434.4 2.3 collective-permute-start.19
  436.7 2.7 collective-permute-done.24
  440.1 3.8 collective-permute-done.19
  (246 shorter events, 57.3 us)
Async XLA Ops:
  7.2 129.9 %all-gather.3.cloned.1.call-start = ((), (), s32[]{:S(2)}) async-start(), calls=%async_computation | async-start | bytes 10948608 | tf_op jit(solution)/shard_map/all_gather | solution.py:504
  17.6 12.6 %collective-permute-start = (bf16[80,768]{1,0:T(8,128)(2,1)S(1)}, bf16[80,768]{1,0:T(8,128)(2,1)S(1)}, u32[]{:S(2)}, u32[]{:S(2)}) collective-permute-start(bf16[80,768]{1,0:T(8,128)(2,1)S(1)} %fusion.17), channel_id=1, source_target_pairs={{0,4},{1,5},{2,6},{3,7},{4,0},{5,1},{6,2},{7,3},{8,12},{9,13},{10,... | collective-permute-start | bytes 368648 | tf_op jit(solution)/shard_map/ppermute | solution.py:454
  30.2 10.4 %collective-permute-start.1 = (bf16[2,80,768]{2,1,0:T(8,128)(2,1)S(1)}, bf16[2,80,768]{2,1,0:T(8,128)(2,1)S(1)}, u32[]{:S(2)}, u32[]{:S(2)}) collective-permute-start(bf16[2,80,768]{2,1,0:T(8,128)(2,1)S(1)} %pad_maximum_fusion.6), channel_id=1, source_target_pairs={{0,2},{1,3},{2,0},{3,1},{4,6},{5,7},{6,4},{7,5},{8,10},{9,11},{10,... | collective-permute-start | bytes 737288 | tf_op jit(solution)/shard_map/ppermute | solution.py:454
  40.8 21.9 %collective-permute-start.2 = (bf16[2,2,80,768]{3,2,1,0:T(8,128)(2,1)S(1)}, bf16[2,2,80,768]{3,2,1,0:T(8,128)(2,1)S(1)}, u32[]{:S(2)}, u32[]{:S(2)}) collective-permute-start(bf16[2,2,80,768]{3,2,1,0:T(8,128)(2,1)S(1)} %pad_maximum_fusion.4), channel_id=1, source_target_pairs={{0,8},{1,9},{2,10},{3,11},{4,12},{5,13},{6,14},{7,15},{8,0},{9,1},... | collective-permute-start | bytes 1474568 | tf_op jit(solution)/shard_map/ppermute | solution.py:454
  62.8 29.9 %collective-permute-start.3 = (bf16[2,2,2,80,768]{4,3,2,1,0:T(8,128)(2,1)S(1)}, bf16[2,2,2,80,768]{4,3,2,1,0:T(8,128)(2,1)}, u32[]{:S(2)}, u32[]{:S(2)}) collective-permute-start(bf16[2,2,2,80,768]{4,3,2,1,0:T(8,128)(2,1)S(1)} %pad_maximum_fusion.3), channel_id=1, source_target_pairs={{0,16},{1,17},{2,18},{3,19},{4,20},{5,21},{6,22},{7,23},{8,24},{9,... | collective-permute-start | bytes 2949128 | tf_op jit(solution)/shard_map/ppermute | solution.py:454
  95.5 4.3 collective-permute-start.4
  105.5 2.5 copy-start.12
  105.5 2.5 copy-start.15
  107.9 8.9 %copy-start.2 = (bf16[32,24,768]{2,1,0:T(8,128)(2,1)}, bf16[32,24,768]{2,1,0:T(8,128)(2,1)S(1)}, u32[]{:S(2)}) copy-start(bf16[32,24,768]{2,1,0:T(8,128)(2,1)S(1)} %get-tuple-element.100) | copy-start | bytes 3538948
  107.9 19.0 %copy-start.4 = (bf16[32,24,768]{2,1,0:T(8,128)(2,1)}, bf16[32,24,768]{2,1,0:T(8,128)(2,1)S(1)}, u32[]{:S(2)}) copy-start(bf16[32,24,768]{2,1,0:T(8,128)(2,1)S(1)} %get-tuple-element.101) | copy-start | bytes 3538948
  116.8 7.5 %copy-start.37 = (bf16[1024,768]{1,0:T(8,128)(2,1)}, bf16[1024,768]{1,0:T(8,128)(2,1)S(1)}, u32[]{:S(2)}) copy-start(bf16[1024,768]{1,0:T(8,128)(2,1)S(1)} %get-tuple-element.58.qkv) | copy-start | bytes 4718596
  161.8 5.4 %copy-start.1 = (bf16[768,3072]{1,0:T(8,128)(2,1)S(1)}, bf16[768,3072]{1,0:T(8,128)(2,1)}, u32[]{:S(2)}) copy-start(bf16[768,3072]{1,0:T(8,128)(2,1)} %reshape.167.up) | copy-start | bytes 14155780
  161.8 25.4 %slice-start.2 = ((s8[4718592]{0:T(1024)(128)(4,1)}), s8[4194304]{0:T(1024)(128)(4,1)S(1)}, s32[]{:S(2)}) async-start(s8[4718592]{0:T(1024)(128)(4,1)} %bitcast.186), calls=%async_computation.3 | async-start | bytes 8388608
  167.2 20.0 %slice-start.3 = ((s8[4718592]{0:T(1024)(128)(4,1)}), s8[524288]{0:T(1024)(128)(4,1)S(1)}, s32[]{:S(2)}) async-start(s8[4718592]{0:T(1024)(128)(4,1)} %bitcast.186), calls=%async_computation.4 | async-start | bytes 1048576
  167.2 20.0 %copy-start.11 = (bf16[1024,768]{1,0:T(8,128)(2,1)S(1)}, bf16[1024,768]{1,0:T(8,128)(2,1)}, u32[]{:S(2)}) copy-start(bf16[1024,768]{1,0:T(8,128)(2,1)} %out_grad.1) | copy-start | bytes 4718596
  184.6 2.6 copy-start.21
  199.4 2.8 copy-start.22
  209.0 23.0 %copy-start.27 = (bf16[1024,256]{1,0:T(8,128)(2,1)S(1)}, bf16[1024,256]{1,0:T(8,128)(2,1)}, u32[]{:S(2)}) copy-start(bf16[1024,256]{1,0:T(8,128)(2,1)} %copy-done.25) | copy-start | bytes 1572868
  209.1 23.0 %copy-start.30 = (bf16[1024,256]{1,0:T(8,128)(2,1)S(1)}, bf16[1024,256]{1,0:T(8,128)(2,1)}, u32[]{:S(2)}) copy-start(bf16[1024,256]{1,0:T(8,128)(2,1)} %copy-done.28) | copy-start | bytes 1572868
  209.1 23.0 %copy-start.33 = (bf16[1024,256]{1,0:T(8,128)(2,1)S(1)}, bf16[1024,256]{1,0:T(8,128)(2,1)}, u32[]{:S(2)}) copy-start(bf16[1024,256]{1,0:T(8,128)(2,1)} %copy-done.31) | copy-start | bytes 1572868
  209.1 22.9 %copy-start.35 = (f32[1024,128]{1,0:T(8,128)S(1)}, f32[1024,128]{1,0:T(8,128)}, u32[]{:S(2)}) copy-start(f32[1024,128]{1,0:T(8,128)} %copy-done.34) | copy-start | bytes 1572868
  239.7 2.4 copy-start.16
  239.7 25.3 %copy-start.23 = (bf16[1024,768]{1,0:T(8,128)(2,1)}, bf16[1024,768]{1,0:T(8,128)(2,1)S(1)}, u32[]{:S(2)}) copy-start(bf16[1024,768]{1,0:T(8,128)(2,1)S(1)} %get-tuple-element.65.att_back) | copy-start | bytes 4718596
  239.7 2.4 copy-start.55
  242.1 8.4 %copy-start.14 = (bf16[1024,768]{1,0:T(8,128)(2,1)S(1)}, bf16[1024,768]{1,0:T(8,128)(2,1)}, u32[]{:S(2)}) copy-start(bf16[1024,768]{1,0:T(8,128)(2,1)} %tok.13) | copy-start | bytes 4718596
  242.1 8.4 %copy-start.42 = (bf16[1024,768]{1,0:T(8,128)(2,1)S(1)}, bf16[1024,768]{1,0:T(8,128)(2,1)}, u32[]{:S(2)}) copy-start(bf16[1024,768]{1,0:T(8,128)(2,1)} %copy-done.41) | copy-start | bytes 4718596
  243.7 6.9 %copy-start.5 = (bf16[32,24,768]{2,1,0:T(8,128)(2,1)S(1)}, bf16[32,24,768]{2,1,0:T(8,128)(2,1)}, u32[]{:S(2)}) copy-start(bf16[32,24,768]{2,1,0:T(8,128)(2,1)} %copy-done.4) | copy-start | bytes 3538948
  243.7 6.9 %copy-start.7 = (bf16[32,24,768]{2,1,0:T(8,128)(2,1)S(1)}, bf16[32,24,768]{2,1,0:T(8,128)(2,1)}, u32[]{:S(2)}) copy-start(bf16[32,24,768]{2,1,0:T(8,128)(2,1)} %slice.283) | copy-start | bytes 3538948
  243.7 6.9 %copy-start.48 = (f32[8,1024]{1,0:T(8,128)S(1)}, f32[8,1024]{1,0:T(8,128)}, u32[]{:S(2)}) copy-start(f32[8,1024]{1,0:T(8,128)} %copy-done.47) | copy-start | bytes 98308
  243.7 88.3 %collective-permute-start.20 = (bf16[2,2,2,2,96,768]{5,4,2,3,0,1:T(8,128)(2,1)}, bf16[2,2,2,2,96,768]{5,4,2,3,0,1:T(8,128)(2,1)}, u32[]{:S(2)}, u32[]{:S(2)}) collective-permute-start(bf16[2,2,2,2,96,768]{5,4,2,3,0,1:T(8,128)(2,1)} %bitcast.176), channel_id=1, source_target_pairs={{0,1},{1,0},{2,3},{3,2},{4,5},{5,4},{6,7},{7,6},{8,9},{9,8},{10,11... | collective-permute-start | bytes 7077896 | tf_op jit(solution)/shard_map/ppermute | solution.py:454
  250.5 59.3 %collective-permute-start.10 = (bf16[2,2,2,2,24,768]{5,4,2,3,0,1:T(8,128)(2,1)}, bf16[2,2,2,2,24,768]{5,4,2,3,0,1:T(8,128)(2,1)}, u32[]{:S(2)}, u32[]{:S(2)}) collective-permute-start(bf16[2,2,2,2,24,768]{5,4,2,3,0,1:T(8,128)(2,1)} %bitcast.179), channel_id=1, source_target_pairs={{0,1},{1,0},{2,3},{3,2},{4,5},{5,4},{6,7},{7,6},{8,9},{9,8},{10,11... | collective-permute-start | bytes 1769480 | tf_op jit(solution)/shard_map/ppermute | solution.py:454
  250.5 14.5 %copy-start.3 = (bf16[32,24,768]{2,1,0:T(8,128)(2,1)S(1)}, bf16[32,24,768]{2,1,0:T(8,128)(2,1)}, u32[]{:S(2)}) copy-start(bf16[32,24,768]{2,1,0:T(8,128)(2,1)} %copy-done.2) | copy-start | bytes 3538948
  250.5 14.5 %copy-start.40 = (bf16[1024,768]{1,0:T(8,128)(2,1)S(1)}, bf16[1024,768]{1,0:T(8,128)(2,1)}, u32[]{:S(2)}) copy-start(bf16[1024,768]{1,0:T(8,128)(2,1)} %copy-done.39) | copy-start | bytes 4718596
  250.5 14.5 %copy-start.46 = (f32[8,1024]{1,0:T(8,128)S(1)}, f32[8,1024]{1,0:T(8,128)}, u32[]{:S(2)}) copy-start(f32[8,1024]{1,0:T(8,128)} %copy-done.45) | copy-start | bytes 98308
  265.0 16.5 %copy-start.38 = (bf16[1024,768]{1,0:T(8,128)(2,1)S(1)}, bf16[1024,768]{1,0:T(8,128)(2,1)}, u32[]{:S(2)}) copy-start(bf16[1024,768]{1,0:T(8,128)(2,1)} %copy-done.37) | copy-start | bytes 4718596
  265.0 16.5 %copy-start.44 = (f32[8,1024]{1,0:T(8,128)S(1)}, f32[8,1024]{1,0:T(8,128)}, u32[]{:S(2)}) copy-start(f32[8,1024]{1,0:T(8,128)} %copy-done.43) | copy-start | bytes 98308
  281.5 14.8 %copy-start.8 = (bf16[768,768]{1,0:T(8,128)(2,1)}, bf16[768,768]{1,0:T(8,128)(2,1)S(1)}, u32[]{:S(2)}) copy-start(bf16[768,768]{1,0:T(8,128)(2,1)S(1)} %get-tuple-element.75) | copy-start | bytes 3538948
  283.3 14.4 %slice-start.4 = ((bf16[8,768]{1,0:T(8,128)(2,1)}), bf16[2,768]{1,0:T(2,128)(2,1)S(1)}, s32[]{:S(2)}) async-start(bf16[8,768]{1,0:T(8,128)(2,1)} %copy-done.55), calls=%async_computation.5 | async-start | bytes 6144 | tf_op jit(solution)/shard_map/slice | solution.py:539
  283.3 14.6 %slice-start.5 = ((bf16[8,768]{1,0:T(8,128)(2,1)}), bf16[2,768]{1,0:T(2,128)(2,1)S(1)}, s32[]{:S(2)}) async-start(bf16[8,768]{1,0:T(8,128)(2,1)} %copy-done.56), calls=%async_computation.6 | async-start | bytes 6144 | tf_op jit(solution)/shard_map/slice | solution.py:539
  298.6 9.3 %slice-start = ((s8[4718592]{0:T(1024)(128)(4,1)}), s8[4194304]{0:T(1024)(128)(4,1)S(1)}, s32[]{:S(2)}) async-start(s8[4718592]{0:T(1024)(128)(4,1)} %bitcast.181), calls=%async_computation.1 | async-start | bytes 8388608
  300.1 7.8 %slice-start.1 = ((s8[4718592]{0:T(1024)(128)(4,1)}), s8[524288]{0:T(1024)(128)(4,1)S(1)}, s32[]{:S(2)}) async-start(s8[4718592]{0:T(1024)(128)(4,1)} %bitcast.181), calls=%async_computation.2 | async-start | bytes 1048576
  303.1 24.3 %collective-permute-start.5 = (bf16[2,2,2,2,80,768]{5,4,2,3,0,1:T(8,128)(2,1)}, bf16[2,2,2,2,80,768]{5,4,2,3,0,1:T(8,128)(2,1)}, u32[]{:S(2)}, u32[]{:S(2)}) collective-permute-start(bf16[2,2,2,2,80,768]{5,4,2,3,0,1:T(8,128)(2,1)} %bitcast.178), channel_id=1, source_target_pairs={{0,1},{1,0},{2,3},{3,2},{4,5},{5,4},{6,7},{7,6},{8,9},{9,8},{10,11... | collective-permute-start | bytes 5898248 | tf_op jit(solution)/shard_map/ppermute | solution.py:454
  309.8 26.3 %collective-permute-start.15 = (bf16[2,2,2,2,24,3072]{5,4,2,3,0,1:T(8,128)(2,1)}, bf16[2,2,2,2,24,3072]{5,4,2,3,0,1:T(8,128)(2,1)}, u32[]{:S(2)}, u32[]{:S(2)}) collective-permute-start(bf16[2,2,2,2,24,3072]{5,4,2,3,0,1:T(8,128)(2,1)} %bitcast.177), channel_id=1, source_target_pairs={{0,1},{1,0},{2,3},{3,2},{4,5},{5,4},{6,7},{7,6},{8,9},{9,8},{10,11... | collective-permute-start | bytes 7077896 | tf_op jit(solution)/shard_map/ppermute | solution.py:454
  311.1 10.4 %collective-permute-start.11 = (bf16[2,2,2,24,768]{4,3,1,2,0:T(8,128)(2,1)S(1)}, bf16[2,2,2,24,768]{4,3,1,2,0:T(8,128)(2,1)S(1)}, u32[]{:S(2)}, u32[]{:S(2)}) collective-permute-start(bf16[2,2,2,24,768]{4,3,1,2,0:T(8,128)(2,1)S(1)} %dynamic-slice_bitcast_fusion.8), channel_id=1, source_target_pairs={{0,8},{1,9},{2,10},{3,11},{4,12},{5,13},{6,14},{7,15},{8,0},{9,1},... | collective-permute-start | bytes 884744 | tf_op jit(solution)/shard_map/ppermute | solution.py:454
  321.6 5.7 %collective-permute-start.12 = (bf16[2,2,24,768]{3,2,0,1:T(8,128)(2,1)S(1)}, bf16[2,2,24,768]{3,2,0,1:T(8,128)(2,1)S(1)}, u32[]{:S(2)}, u32[]{:S(2)}) collective-permute-start(bf16[2,2,24,768]{3,2,0,1:T(8,128)(2,1)S(1)} %dynamic-slice_bitcast_fusion.12), channel_id=1, source_target_pairs={{0,16},{1,17},{2,18},{3,19},{4,20},{5,21},{6,22},{7,23},{8,24},{9,... | collective-permute-start | bytes 442376 | tf_op jit(solution)/shard_map/ppermute | solution.py:454
  327.4 30.4 %collective-permute-start.13 = (bf16[2,24,768]{2,1,0:T(8,128)(2,1)S(1)}, bf16[2,24,768]{2,1,0:T(8,128)(2,1)S(1)}, u32[]{:S(2)}, u32[]{:S(2)}) collective-permute-start(bf16[2,24,768]{2,1,0:T(8,128)(2,1)S(1)} %dynamic-slice_bitcast_fusion.14), channel_id=1, source_target_pairs={{0,2},{1,3},{2,0},{3,1},{4,6},{5,7},{6,4},{7,5},{8,10},{9,11},{10,... | collective-permute-start | bytes 221192 | tf_op jit(solution)/shard_map/ppermute | solution.py:454
  327.5 4.5 copy-start.49
  330.4 24.8 %collective-permute-start.6 = (bf16[2,2,2,80,768]{4,3,1,2,0:T(8,128)(2,1)S(1)}, bf16[2,2,2,80,768]{4,3,1,2,0:T(8,128)(2,1)S(1)}, u32[]{:S(2)}, u32[]{:S(2)}) collective-permute-start(bf16[2,2,2,80,768]{4,3,1,2,0:T(8,128)(2,1)S(1)} %dynamic-slice_bitcast_fusion.2), channel_id=1, source_target_pairs={{0,8},{1,9},{2,10},{3,11},{4,12},{5,13},{6,14},{7,15},{8,0},{9,1},... | collective-permute-start | bytes 2949128 | tf_op jit(solution)/shard_map/ppermute | solution.py:454
  334.3 4.3 copy-start.50
  335.6 44.9 %collective-permute-start.21 = (bf16[2,2,2,96,768]{4,3,1,2,0:T(8,128)(2,1)}, bf16[2,2,2,96,768]{4,3,1,2,0:T(8,128)(2,1)}, u32[]{:S(2)}, u32[]{:S(2)}) collective-permute-start(bf16[2,2,2,96,768]{4,3,1,2,0:T(8,128)(2,1)} %dynamic-slice_bitcast_fusion), channel_id=1, source_target_pairs={{0,8},{1,9},{2,10},{3,11},{4,12},{5,13},{6,14},{7,15},{8,0},{9,1},... | collective-permute-start | bytes 3538952 | tf_op jit(solution)/shard_map/ppermute | solution.py:454
  338.6 16.7 %copy-start.52 = (bf16[2,2,2,2,24,3072]{5,4,2,3,0,1:T(8,128)(2,1)}, bf16[2,2,2,2,24,3072]{5,4,2,3,0,1:T(8,128)(2,1)S(1)}, u32[]{:S(2)}) copy-start(bf16[2,2,2,2,24,3072]{5,4,2,3,0,1:T(8,128)(2,1)S(1)} %fusion.1) | copy-start | bytes 7077892
  339.9 63.9 %collective-permute-start.16 = (bf16[2,2,2,24,3072]{4,3,1,2,0:T(8,128)(2,1)}, bf16[2,2,2,24,3072]{4,3,1,2,0:T(8,128)(2,1)}, u32[]{:S(2)}, u32[]{:S(2)}) collective-permute-start(bf16[2,2,2,24,3072]{4,3,1,2,0:T(8,128)(2,1)} %dynamic-slice_bitcast_fusion.1), channel_id=1, source_target_pairs={{0,8},{1,9},{2,10},{3,11},{4,12},{5,13},{6,14},{7,15},{8,0},{9,1},... | collective-permute-start | bytes 3538952 | tf_op jit(solution)/shard_map/ppermute | solution.py:454
  355.4 25.1 %copy-start.51 = (bf16[2,2,2,2,96,768]{5,4,2,3,0,1:T(8,128)(2,1)S(1)}, bf16[2,2,2,2,96,768]{5,4,2,3,0,1:T(8,128)(2,1)}, u32[]{:S(2)}) copy-start(bf16[2,2,2,2,96,768]{5,4,2,3,0,1:T(8,128)(2,1)} %copy-done.50) | copy-start | bytes 7077892
  356.2 11.2 %collective-permute-start.7 = (bf16[2,2,80,768]{3,2,0,1:T(8,128)(2,1)}, bf16[2,2,80,768]{3,2,0,1:T(8,128)(2,1)}, u32[]{:S(2)}, u32[]{:S(2)}) collective-permute-start(bf16[2,2,80,768]{3,2,0,1:T(8,128)(2,1)} %dynamic-slice_bitcast_fusion.5), channel_id=1, source_target_pairs={{0,16},{1,17},{2,18},{3,19},{4,20},{5,21},{6,22},{7,23},{8,24},{9,... | collective-permute-start | bytes 1474568 | tf_op jit(solution)/shard_map/ppermute | solution.py:454
  357.8 9.0 %collective-permute-start.14 = (bf16[24,768]{1,0:T(8,128)(2,1)S(1)}, bf16[24,768]{1,0:T(8,128)(2,1)S(1)}, u32[]{:S(2)}, u32[]{:S(2)}) collective-permute-start(bf16[24,768]{1,0:T(8,128)(2,1)S(1)} %dynamic-slice_bitcast_fusion.15), channel_id=1, source_target_pairs={{0,4},{1,5},{2,6},{3,7},{4,0},{5,1},{6,2},{7,3},{8,12},{9,13},{10,... | collective-permute-start | bytes 110600 | tf_op jit(solution)/shard_map/ppermute | solution.py:454
  368.6 35.2 %copy-start.53 = (bf16[2,2,2,2,24,3072]{5,4,2,3,0,1:T(8,128)(2,1)S(1)}, bf16[2,2,2,2,24,3072]{5,4,2,3,0,1:T(8,128)(2,1)}, u32[]{:S(2)}) copy-start(bf16[2,2,2,2,24,3072]{5,4,2,3,0,1:T(8,128)(2,1)} %copy-done.52) | copy-start | bytes 7077892
  368.6 36.8 %collective-permute-start.8 = (bf16[2,80,768]{2,1,0:T(8,128)(2,1)S(1)}, bf16[2,80,768]{2,1,0:T(8,128)(2,1)S(1)}, u32[]{:S(2)}, u32[]{:S(2)}) collective-permute-start(bf16[2,80,768]{2,1,0:T(8,128)(2,1)S(1)} %dynamic-slice_bitcast_fusion.9), channel_id=1, source_target_pairs={{0,2},{1,3},{2,0},{3,1},{4,6},{5,7},{6,4},{7,5},{8,10},{9,11},{10,... | collective-permute-start | bytes 737288 | tf_op jit(solution)/shard_map/ppermute | solution.py:454
  382.1 37.3 %collective-permute-start.22 = (bf16[2,2,96,768]{3,2,0,1:T(8,128)(2,1)S(1)}, bf16[2,2,96,768]{3,2,0,1:T(8,128)(2,1)S(1)}, u32[]{:S(2)}, u32[]{:S(2)}) collective-permute-start(bf16[2,2,96,768]{3,2,0,1:T(8,128)(2,1)S(1)} %dynamic-slice_bitcast_fusion.3), channel_id=1, source_target_pairs={{0,16},{1,17},{2,18},{3,19},{4,20},{5,21},{6,22},{7,23},{8,24},{9,... | collective-permute-start | bytes 1769480 | tf_op jit(solution)/shard_map/ppermute | solution.py:454
  405.6 10.7 %collective-permute-start.9 = (bf16[80,768]{1,0:T(8,128)(2,1)S(1)}, bf16[80,768]{1,0:T(8,128)(2,1)S(1)}, u32[]{:S(2)}, u32[]{:S(2)}) collective-permute-start(bf16[80,768]{1,0:T(8,128)(2,1)S(1)} %dynamic-slice_bitcast_fusion.13), channel_id=1, source_target_pairs={{0,4},{1,5},{2,6},{3,7},{4,0},{5,1},{6,2},{7,3},{8,12},{9,13},{10,... | collective-permute-start | bytes 368648 | tf_op jit(solution)/shard_map/ppermute | solution.py:454
  412.1 12.9 %collective-permute-start.17 = (bf16[2,2,24,3072]{3,2,0,1:T(8,128)(2,1)S(1)}, bf16[2,2,24,3072]{3,2,0,1:T(8,128)(2,1)S(1)}, u32[]{:S(2)}, u32[]{:S(2)}) collective-permute-start(bf16[2,2,24,3072]{3,2,0,1:T(8,128)(2,1)S(1)} %dynamic-slice_bitcast_fusion.4), channel_id=1, source_target_pairs={{0,16},{1,17},{2,18},{3,19},{4,20},{5,21},{6,22},{7,23},{8,24},{9,... | collective-permute-start | bytes 1769480 | tf_op jit(solution)/shard_map/ppermute | solution.py:454
  419.6 10.2 %collective-permute-start.23 = (bf16[2,96,768]{2,1,0:T(8,128)(2,1)S(1)}, bf16[2,96,768]{2,1,0:T(8,128)(2,1)S(1)}, u32[]{:S(2)}, u32[]{:S(2)}) collective-permute-start(bf16[2,96,768]{2,1,0:T(8,128)(2,1)S(1)} %dynamic-slice_bitcast_fusion.6), channel_id=1, source_target_pairs={{0,2},{1,3},{2,0},{3,1},{4,6},{5,7},{6,4},{7,5},{8,10},{9,11},{10,... | collective-permute-start | bytes 884744 | tf_op jit(solution)/shard_map/ppermute | solution.py:454
  425.2 9.1 %collective-permute-start.18 = (bf16[2,24,3072]{2,1,0:T(8,128)(2,1)S(1)}, bf16[2,24,3072]{2,1,0:T(8,128)(2,1)S(1)}, u32[]{:S(2)}, u32[]{:S(2)}) collective-permute-start(bf16[2,24,3072]{2,1,0:T(8,128)(2,1)S(1)} %dynamic-slice_bitcast_fusion.7), channel_id=1, source_target_pairs={{0,2},{1,3},{2,0},{3,1},{4,6},{5,7},{6,4},{7,5},{8,10},{9,11},{10,... | collective-permute-start | bytes 884744 | tf_op jit(solution)/shard_map/ppermute | solution.py:454
  429.9 9.5 %collective-permute-start.24 = (bf16[96,768]{1,0:T(8,128)(2,1)S(1)}, bf16[96,768]{1,0:T(8,128)(2,1)S(1)}, u32[]{:S(2)}, u32[]{:S(2)}) collective-permute-start(bf16[96,768]{1,0:T(8,128)(2,1)S(1)} %dynamic-slice_bitcast_fusion.10), channel_id=1, source_target_pairs={{0,4},{1,5},{2,6},{3,7},{4,0},{5,1},{6,2},{7,3},{8,12},{9,13},{10,... | collective-permute-start | bytes 442376 | tf_op jit(solution)/shard_map/ppermute | solution.py:454
  434.4 9.5 %collective-permute-start.19 = (bf16[24,3072]{1,0:T(8,128)(2,1)S(1)}, bf16[24,3072]{1,0:T(8,128)(2,1)S(1)}, u32[]{:S(2)}, u32[]{:S(2)}) collective-permute-start(bf16[24,3072]{1,0:T(8,128)(2,1)S(1)} %dynamic-slice_bitcast_fusion.11), channel_id=1, source_target_pairs={{0,4},{1,5},{2,6},{3,7},{4,0},{5,1},{6,2},{7,3},{8,12},{9,13},{10,... | collective-permute-start | bytes 442376 | tf_op jit(solution)/shard_map/ppermute | solution.py:454
  (25 other events, 32.1 us)
Sparse Core Ops, SparseCore 0:
  11.6 107.6 all-gather.2

commit v2 on v1

v2 whole, which is shorter than its diff:
```python
import functools
import math

import jax
import jax.numpy as jnp
from jax import lax
from jax.experimental import pallas as pl
from jax.experimental.pallas import tpu as pltpu
from jax.sharding import PartitionSpec as P

HEAD_DIM = 64
GROUP = 256
PAIR = 128
EPSILON = 1e-06
MASKED = -1e30
LOG2E = 1.4426950408889634
AXES = ("dp", "fsdp")
BF, F32 = jnp.bfloat16, jnp.float32
MIB = 2**20
SCALE = 1
UP_AT_ONCE = False
PLACED = 2**17


def dot(a, b, ca=1, cb=0):
    return lax.dot_general(a, b, (((ca,), (cb,)), ((), ())), preferred_element_type=F32)


def call(kernel, cost, after=(), vmem=40, placed=False, **kw):
    after = tuple(after)
    kw["in_specs"] = list(kw["in_specs"]) + [pl.BlockSpec(memory_space=pl.ANY)] * len(after)
    taken = len(kw["in_specs"]) - len(after)

    def run(*refs):
        kernel(*refs[:taken], *refs[taken + len(after) :])

    made = pl.pallas_call(
        run,
        compiler_params=pltpu.CompilerParams(vmem_limit_bytes=vmem * MIB),
        cost_estimate=pl.CostEstimate(flops=int(cost * 1e6 * SCALE), bytes_accessed=0, transcendentals=0),
        **kw,
    )
    def place(operand):
        small = operand.size * operand.dtype.itemsize < PLACED
        return operand if small or not placed else pltpu.with_memory_space_constraint(operand, pltpu.HBM)

    return lambda *operands: made(*map(place, operands), *after)


def shares(rows, cols, n, dtype=BF):
    own = rows // n
    if own % 8:
        return [jax.ShapeDtypeStruct((rows, cols), dtype)]
    return [jax.ShapeDtypeStruct((n // 2, own, cols), dtype)] * 2


def put_shares(value, core, refs, cols=slice(None)):
    if len(refs) == 1:
        refs[0][:, cols] = value.astype(BF)
        return
    pairs, own = refs[0].shape[:2]
    value = value.reshape(pairs, 2, own, value.shape[-1])
    even, odd = value[:, 0], value[:, 1]
    mine = core == 0
    refs[0][:, :, cols] = jnp.where(mine, even, odd).astype(BF)
    refs[1][:, :, cols] = jnp.where(mine, odd, even).astype(BF)


def seq_ends(len_ref, count):
    ends = [len_ref[0, 0]]
    for j in range(1, count):
        ends.append(ends[-1] + len_ref[0, j])
    return ends


def fill_segments(ends, seg_col, seg_row):
    at_col = lax.broadcasted_iota(jnp.int32, seg_col.shape, 0)
    at_row = lax.broadcasted_iota(jnp.int32, seg_row.shape, 1)
    col, row = jnp.zeros(seg_col.shape, jnp.int32), jnp.zeros(seg_row.shape, jnp.int32)
    for end in ends:
        col = col + (at_col >= end).astype(jnp.int32)
        row = row + (at_row >= end).astype(jnp.int32)
    seg_col[...] = col
    seg_row[...] = row


def key_range(ends, first, last, cases, total):
    low, high = jnp.int32(0), jnp.int32(total)
    for end in ends:
        low = jnp.maximum(low, jnp.where(end <= first, end, 0))
        high = jnp.minimum(high, jnp.where(end > last, end, total))
    start = lax.div(low, 128)
    need = lax.div(high + 127, 128) - start
    case, size = jnp.int32(0), jnp.int32(cases[0])
    for j in range(1, len(cases)):
        more = need > cases[j - 1]
        case = jnp.where(more, j, case)
        size = jnp.where(more, cases[j], size)
    start = jnp.minimum(start, total // 128 - size)
    return pl.multiple_of(start * 128, 128), case


def for_blocks(ends, total, rows_in_block, cases, block):
    cases = tuple(c for c in cases if c < total // 128) + (total // 128,)

    @pl.loop(0, total // rows_in_block)
    def _(i):
        first = i * rows_in_block
        start, case = key_range(ends, first, first + rows_in_block - 1, cases, total)
        for j, n in enumerate(cases):
            pl.when(case == j)(functools.partial(block, pl.multiple_of(first, rows_in_block), n, start))


def attend_kernel(len_ref, tok, w, vecs, qkv, ctx, lse, seg_col, seg_row, *, group, bq, cases, nseq):
    total = tok.shape[0]
    ends = seq_ends(len_ref, nseq)
    fill_segments(ends, seg_col, seg_row)
    for part in range(3):
        cols = pl.ds(part * GROUP, GROUP)
        made = dot(tok[...], w[:, cols])
        if part != 1:
            made = made + vecs[part // 2 : part // 2 + 1, pl.ds(group * GROUP, GROUP)]
        made = made.astype(BF)
        qkv[:, cols] = made * BF(1.0 / math.sqrt(HEAD_DIM)) if part == 0 else made

    def block(first, n, start):
        nk = n * 128
        rows, keys = pl.ds(first, bq), pl.ds(start, nk)
        same = jnp.concatenate([seg_col[rows, :]] * n, 1) == seg_row[0:1, keys]
        lane = lax.broadcasted_iota(jnp.int32, (bq, PAIR), 1)
        stats = jnp.zeros((bq, PAIR), F32)
        for pair in range(2):
            q = qkv[rows, pl.ds(pair * PAIR, PAIR)]
            k = qkv[keys, pl.ds(GROUP + pair * PAIR, PAIR)]
            v = qkv[keys, pl.ds(2 * GROUP + pair * PAIR, PAIR)]
            v_ones = jnp.concatenate([v, jnp.ones((nk, PAIR), BF)], 1)
            outs = []
            for h in range(2):
                s = dot(jnp.where((lane < HEAD_DIM) == (h == 0), q, BF(0)), k, 1, 1)
                s = jnp.where(same, s, MASKED)
                top = jnp.max(s, axis=1, keepdims=True)
                o = dot(jnp.exp2((s - top) * LOG2E).astype(BF), v_ones)
                norm = o[:, PAIR:]
                outs.append(o[:, :PAIR] * (1.0 / norm))
                stats = jnp.where(lane == pair * 2 + h, top * LOG2E + jnp.log2(norm), stats)
            ctx[rows, pl.ds(pair * PAIR, PAIR)] = jnp.where(lane < HEAD_DIM, outs[0], outs[1]).astype(BF)
        lse[:, rows] = stats.T[0:8, :]

    for_blocks(ends, total, bq, cases, block)


def attend(lens, tok, packed, group, vecs, after=(), bq=256, cases=(2, 3, 4, 5, 6)):
    total, width = tok.shape
    vmem = pl.BlockSpec(memory_space=pltpu.VMEM)
    return call(
        functools.partial(attend_kernel, group=group, bq=bq, cases=cases, nseq=lens.shape[1]),
        9,
        after,
        grid=(1,),
        in_specs=[
            pl.BlockSpec(memory_space=pltpu.SMEM),
            vmem,
            pl.BlockSpec((width, 3 * GROUP), lambda _: (0, group)),
            vmem,
        ],
        out_specs=[vmem] * 3,
        out_shape=[
            jax.ShapeDtypeStruct((total, 3 * GROUP), BF),
            jax.ShapeDtypeStruct((total, GROUP), BF),
            jax.ShapeDtypeStruct((8, total), F32),
        ],
        scratch_shapes=[pltpu.VMEM((total, 128), jnp.int32), pltpu.VMEM((8, total), jnp.int32)],
        name="attend",
    )(lens, tok, packed, vecs)


def attend_back_kernel(
    len_ref, core_ref, tok_t, w, out_w, qkv, ctx, lse_in, att_back, grad_in, *refs, extra, carry, n_dw, bq, cases, nseq, chunk=2
):
    extras, carried, refs = refs[:extra], refs[extra : extra + carry], refs[extra + carry :]
    dw, (grad_out, sums) = refs[:n_dw], refs[n_dw : n_dw + 2]
    seg_col, seg_row, key_t, do, dqkv, dk_sum, dv_sum, p_s, ds_s = refs[n_dw + 2 :]
    width, total = tok_t.shape
    ends = seq_ends(len_ref, nseq)
    fill_segments(ends, seg_col, seg_row)
    do[...] = dot(att_back[...], out_w[...], 1, 1).astype(BF)
    key_t[...] = qkv[:, pl.ds(GROUP, GROUP)].T
    dk_sum[...] = jnp.zeros_like(dk_sum)
    dv_sum[...] = jnp.zeros_like(dv_sum)
    head = lax.broadcasted_iota(jnp.int32, (8, GROUP), 1) // HEAD_DIM == lax.broadcasted_iota(jnp.int32, (8, GROUP), 0)
    head = head.astype(BF)

    def block(first, n, start):
        nk = n * 128
        rows, keys = pl.ds(first, bq), pl.ds(start, nk)
        seg_q = seg_row[0:1, rows]
        lane = lax.broadcasted_iota(jnp.int32, (bq, PAIR), 1)
        both = do[rows, :].astype(F32) * ctx[rows, :].astype(F32)
        high = both.astype(BF)
        low = (both - high.astype(F32)).astype(BF)
        delta = dot(head, high, 1, 1) + dot(head, low, 1, 1)
        lse = lse_in[:, rows]
        dqs = []
        for pair in range(2):
            cols = pl.ds(pair * PAIR, PAIR)
            k_cols, v_cols = pl.ds(GROUP + pair * PAIR, PAIR), pl.ds(2 * GROUP + pair * PAIR, PAIR)
            q, g = qkv[rows, cols], do[rows, cols]
            qs, gs = [], []
            for h in range(2):
                head_at = pair * 2 + h
                mine = (lane < HEAD_DIM) == (h == 0)
                qs.append(jnp.where(mine, q, BF(0)))
                gs.append(jnp.where(mine, g, BF(0)))
                for c in range(0, n, chunk):
                    wide = min(chunk, n - c) * 128
                    some = pl.ds(pl.multiple_of(start + c * 128, 128), wide)
                    s = dot(qkv[some, k_cols], qs[h], 1, 1)
                    same = jnp.concatenate([seg_col[some, :]] * (bq // 128), 1) == seg_q
                    p = jnp.exp2(jnp.where(same, s * LOG2E - lse[head_at : head_at + 1, :], MASKED))
                    dp = dot(qkv[some, v_cols], gs[h], 1, 1)
                    p_s[pl.ds(c * 128, wide), pl.ds(h * bq, bq)] = p.astype(BF)
                    ds_s[pl.ds(c * 128, wide), pl.ds(h * bq, bq)] = (p * (dp - delta[head_at : head_at + 1, :])).astype(BF)
            for h in range(2):
                dqs.append(dot(key_t[pl.ds((pair * 2 + h) * HEAD_DIM, HEAD_DIM), keys], ds_s[pl.ds(0, nk), pl.ds(h * bq, bq)]))
            dv_sum[keys, cols] += dot(p_s[pl.ds(0, nk), :], jnp.concatenate(gs, 0))
            dk_sum[keys, cols] += dot(ds_s[pl.ds(0, nk), :], jnp.concatenate(qs, 0))
        dqkv[rows, pl.ds(0, GROUP)] = (jnp.concatenate(dqs, 0).T * (1.0 / math.sqrt(HEAD_DIM))).astype(BF)

    for_blocks(ends, total, bq, cases, block)
    dqkv[:, pl.ds(GROUP, GROUP)] = dk_sum[...].astype(BF)
    dqkv[:, pl.ds(2 * GROUP, GROUP)] = dv_sum[...].astype(BF)
    d = dqkv[...]
    bias_sums = jnp.sum(d.astype(F32), axis=0, keepdims=True)
    sums[...] = jnp.broadcast_to(bias_sums, sums.shape)
    put_shares(dot(tok_t[...], d), core_ref[0, 0], dw, pl.ds(0, 3 * GROUP))
    grad_out[...] = grad_in[...] + dot(d, w[...], 1, 1)
    for source, target in zip(carried, dw):
        target[..., pl.ds(3 * GROUP, width)] = source[...]
    if extra:
        *before, sums_one, sums_two, up_sums = extras
        query = jnp.concatenate([b[0:1, :GROUP] for b in before] + [bias_sums[:, :GROUP]], 1)
        value = jnp.concatenate([b[0:1, 2 * GROUP :] for b in before] + [bias_sums[:, 2 * GROUP :]], 1)
        rows = [query, value, sums_one[2:3], sums_one[0:1], sums_one[1:2], sums_two[2:3], sums_two[0:1], sums_two[1:2]]
        at = lax.broadcasted_iota(jnp.int32, (128, width), 0)
        table = jnp.zeros((128, width), F32)
        for j, row in enumerate([*rows, *(up_sums[j : j + 1] for j in range(4))]):
            table = jnp.where(at == j, row, table)
        put_shares(table.T, core_ref[0, 0], dw, pl.ds(3 * GROUP, 128))


def attend_back(
    lens, core, tok_t, packed, out_up, group, qkv, ctx, lse, att_back, grad_in, n, extras=(), carried=(), after=(), bq=256,
    cases=(2, 3, 4, 5, 6),
):
    width, total = tok_t.shape
    vmem, smem = pl.BlockSpec(memory_space=pltpu.VMEM), pl.BlockSpec(memory_space=pltpu.SMEM)
    dw = shares(width, 3 * GROUP + (128 if extras else 0) + (width if carried else 0), n)
    return call(
        functools.partial(
            attend_back_kernel, extra=len(extras), carry=len(carried), n_dw=len(dw), bq=bq, cases=cases, nseq=lens.shape[1]
        ),
        15,
        after,
        grid=(1,),
        in_specs=[
            smem,
            smem,
            vmem,
            pl.BlockSpec((width, 3 * GROUP), lambda _: (0, group)),
            pl.BlockSpec((GROUP, width), lambda _: (group, 0)),
        ]
        + [vmem] * (5 + len(extras) + len(carried)),
        out_specs=[vmem] * (len(dw) + 2),
        out_shape=[
            *dw,
            jax.ShapeDtypeStruct((total, width), F32),
            jax.ShapeDtypeStruct((8, 3 * GROUP), F32),
        ],
        scratch_shapes=[
            pltpu.VMEM((total, 128), jnp.int32),
            pltpu.VMEM((8, total), jnp.int32),
            pltpu.VMEM((GROUP, total), BF),
            pltpu.VMEM((total, GROUP), BF),
            pltpu.VMEM((total, 3 * GROUP), BF),
            pltpu.VMEM((total, GROUP), F32),
            pltpu.VMEM((total, GROUP), F32),
            pltpu.VMEM((total, 2 * bq), BF),
            pltpu.VMEM((total, 2 * bq), BF),
        ],
        name="attend_back",
    )(lens, core, tok_t, packed, out_up, qkv, ctx, lse, att_back, grad_in, *extras, *carried)


def row_mean(value):
    return jnp.sum(value, axis=-1, keepdims=True) * (1.0 / value.shape[-1])


def norm(value):
    center = value - row_mean(value)
    inverse = lax.rsqrt(row_mean(center * center) + EPSILON)
    return center * inverse, inverse


def norm_back(upstream, normed, inverse, gain):
    scaled = upstream * gain
    return inverse * (scaled - row_mean(scaled) - normed * row_mean(scaled * normed))


def add_rows(sums, first, pieces):
    at = lax.broadcasted_iota(jnp.int32, sums.shape, 0)
    made = jnp.zeros(sums.shape, F32)
    for j, piece in enumerate(pieces):
        made = jnp.where(at == j, jnp.sum(piece, axis=0, keepdims=True), made)

    @pl.when(first)
    def _():
        sums[...] = made

    @pl.when(jnp.logical_not(first))
    def _():
        sums[...] += made


ROOT = math.sqrt(2.0 / math.pi)


def lay_down(core, pieces, whole):
    if len(pieces) == 1:
        whole[...] = pieces[0][...]
        return
    half = len(pieces) // 2
    pairs, each = pieces[0].shape[:2]
    first = 0
    for mine, other in zip(pieces[:half], pieces[half:]):
        cols = pl.ds(first, mine.shape[-1])
        for e in range(pairs):
            a, b = mine[e], other[e]
            whole[pl.ds(2 * e * each, each), cols] = jnp.where(core == 0, a, b)
            whole[pl.ds((2 * e + 1) * each, each), cols] = jnp.where(core == 0, b, a)
        first += mine.shape[-1]


def down_specs(pieces, parts, at):
    if len(pieces) == 1:
        hidden, width = pieces[0].shape
        return [pl.BlockSpec((hidden // parts, width), lambda j: (at(j), 0))]
    return [pl.BlockSpec((p.shape[0] // parts, *p.shape[1:]), lambda j: (at(j), 0, 0)) for p in pieces]


def forward_kernel(core_ref, ctx0, ctx1, ctx2, tok, out_w, up, bias, vecs, out_grad, *refs, rows, parts, n_down, n_dw):
    pieces, dw, refs = refs[:n_down], refs[n_down : n_down + n_dw], refs[n_down + n_dw :]
    output, normed, inverse, low, slope, second, back_low, sums, act, total, down = refs
    j = pl.program_id(0)
    width = tok.shape[1]
    blocks = tok.shape[0] // rows

    @pl.when(j == 0)
    def _():
        @pl.loop(0, blocks)
        def _(i):
            at = pl.ds(pl.multiple_of(i * rows, rows), rows)
            ctx = jnp.concatenate([ctx0[at, :], ctx1[at, :], ctx2[at, :]], 1)
            n, r = norm(tok[at, :].astype(F32) + (dot(ctx, out_w[...]) + vecs[2:3, :]))
            normed[at, :] = n
            inverse[at, :] = jnp.broadcast_to(r, (rows, inverse.shape[1]))
            middle = n * vecs[3:4, :] + vecs[4:5, :]
            low[at, :] = middle.astype(BF)
            total[at, :] = middle + vecs[5:6, :]

    @pl.when(j < parts)
    def _():
        x = dot(low[...], up[...]) + bias[...]
        w = ROOT + (ROOT * 0.044715) * (x * x)
        gate = 0.5 + 0.5 * jnp.tanh(x * w)
        made = x * gate
        slope[...] = (gate + made * (1.0 - gate) * (6.0 * w - 4.0 * ROOT)).astype(BF)
        act[j] = made.astype(BF)
        lay_down(core_ref[0, 0], pieces, down)
        total[...] += dot(act[j], down[...])

    @pl.when(j == parts - 1)
    def _():
        @pl.loop(0, blocks)
        def _(i):
            at = pl.ds(pl.multiple_of(i * rows, rows), rows)
            n, r = norm(total[at, :])
            output[at, :] = (n * vecs[6:7, :] + vecs[7:8, :]).astype(BF)
            upstream = out_grad[at, :].astype(F32)
            made = norm_back(upstream, n, r, vecs[6:7, :])
            second[at, :] = made
            rounded = made.astype(BF)
            back_low[at, :] = rounded
            add_rows(sums, i == 0, (upstream * n, upstream, rounded.astype(F32)))

    @pl.when(j >= parts)
    def _():
        put_shares(dot(act[j - parts], back_low[...], 0, 0), core_ref[0, 0], dw)


def forward(core, ctxs, tok, out_up, up_bias, down, vecs, out_grad, n, rows=256):
    total, width = tok.shape
    hidden = up_bias.shape[1]
    parts = hidden // width
    vmem = pl.BlockSpec(memory_space=pltpu.VMEM)
    first = lambda j: jnp.minimum(j, parts - 1)
    last = lambda j: jnp.maximum(j - parts, 0)
    dw = shares(hidden, width, n)
    return call(
        functools.partial(forward_kernel, rows=rows, parts=parts, n_down=len(down), n_dw=len(dw)),
        32,
        vmem=48,
        placed=True,
        grid=(2 * parts,),
        in_specs=[pl.BlockSpec(memory_space=pltpu.SMEM)]
        + [vmem] * 4
        + [
            pl.BlockSpec((width, width), lambda j: (0, 0)),
            pl.BlockSpec((width, width), lambda j: (0, first(j) + 1)),
            pl.BlockSpec((1, width), lambda j: (0, first(j))),
            vmem,
            vmem,
            *down_specs(down, parts, first),
        ],
        out_specs=down_specs(dw, parts, last)
        + [vmem] * 4
        + [pl.BlockSpec((total, width), lambda j: (0, first(j))), vmem, vmem, vmem],
        out_shape=[
            *dw,
            jax.ShapeDtypeStruct((total, width), BF),
            jax.ShapeDtypeStruct((total, width), F32),
            jax.ShapeDtypeStruct((total, 128), F32),
            jax.ShapeDtypeStruct((total, width), BF),
            jax.ShapeDtypeStruct((total, hidden), BF),
            jax.ShapeDtypeStruct((total, width), F32),
            jax.ShapeDtypeStruct((total, width), BF),
            jax.ShapeDtypeStruct((8, width), F32),
        ],
        scratch_shapes=[
            pltpu.VMEM((parts, total, width), BF),
            pltpu.VMEM((total, width), F32),
            pltpu.VMEM((width, width), BF),
        ],
        name="forward",
    )(core, *ctxs, tok, out_up, out_up, up_bias, vecs, out_grad, *down)


def backward_kernel(
    core_ref, back_low, slope, low, up, second, normed, inverse, ctx0, ctx1, ctx2, vecs, *refs, rows, n_dw, n_down
):
    pieces, refs = refs[:n_down], refs[n_down:]
    dw, out_dw, refs = refs[: n_dw[0]], refs[n_dw[0] : sum(n_dw)], refs[sum(n_dw) :]
    up_sums, entry_grad, att_back, sums, low_t, back, ex, down = refs
    j = pl.program_id(0)
    blocks = low.shape[0] // rows

    @pl.when(j == 0)
    def _():
        low_t[...] = low[...].T
        back[...] = jnp.zeros_like(back)

    lay_down(core_ref[0, 0], pieces, down)
    ex[...] = (dot(back_low[...], down[...], 1, 1) * slope[...].astype(F32)).astype(BF)
    up_sums[...] = jnp.broadcast_to(jnp.sum(ex[...].astype(F32), axis=0, keepdims=True), up_sums.shape)
    back[...] += dot(ex[...], up[...], 1, 1)
    put_shares(dot(low_t[...], ex[...]), core_ref[0, 0], dw)

    @pl.when(j == pl.num_programs(0) - 1)
    def _():
        @pl.loop(0, blocks)
        def _(i):
            at = pl.ds(pl.multiple_of(i * rows, rows), rows)
            upstream = second[at, :] + back[at, :].astype(BF).astype(F32)
            n = normed[at, :]
            made = norm_back(upstream, n, inverse[at, 0:1], vecs[3:4, :])
            entry_grad[at, :] = made
            rounded = made.astype(BF)
            att_back[at, :] = rounded
            add_rows(sums, i == 0, (upstream * n, upstream, rounded.astype(F32)))

        ctx = jnp.concatenate([ctx0[...], ctx1[...], ctx2[...]], 1)
        put_shares(dot(ctx, att_back[...], 0, 0), core_ref[0, 0], out_dw)


def backward(core, back_low, down, slope, low, out_up, second, normed, inverse, ctxs, vecs, n, after=(), rows=256):
    total, width = low.shape
    hidden = slope.shape[1]
    vmem = pl.BlockSpec(memory_space=pltpu.VMEM)
    dw = [jax.ShapeDtypeStruct((width, hidden), BF)] if UP_AT_ONCE else shares(width, hidden, n)
    out_dw = shares(width, width, n)
    lead = (0,) * (len(dw[0].shape) - 1)
    return call(
        functools.partial(backward_kernel, rows=rows, n_dw=(len(dw), len(out_dw)), n_down=len(down)),
        26,
        after,
        vmem=44,
        placed=True,
        grid=(hidden // width,),
        in_specs=[
            pl.BlockSpec(memory_space=pltpu.SMEM),
            vmem,
            pl.BlockSpec((total, width), lambda j: (0, j)),
            vmem,
            pl.BlockSpec((width, width), lambda j: (0, j + 1)),
        ]
        + [vmem] * 7
        + down_specs(down, hidden // width, lambda j: j),
        out_specs=[pl.BlockSpec((*d.shape[:-1], width), lambda j: (*lead, j)) for d in dw]
        + [vmem] * len(out_dw)
        + [pl.BlockSpec((8, width), lambda j: (0, j))]
        + [vmem] * 3,
        out_shape=[
            *dw,
            *out_dw,
            jax.ShapeDtypeStruct((8, hidden), F32),
            jax.ShapeDtypeStruct((total, width), F32),
            jax.ShapeDtypeStruct((total, width), BF),
            jax.ShapeDtypeStruct((8, width), F32),
        ],
        scratch_shapes=[
            pltpu.VMEM((width, total), BF),
            pltpu.VMEM((total, width), F32),
            pltpu.VMEM((total, width), BF),
            pltpu.VMEM((width, width), BF),
        ],
        name="backward",
    )(core, back_low, slope, low, out_up, second, normed, inverse, *ctxs, vecs, *down)


def pack_kernel(query, key, value, table, packed):
    own, width = query.shape
    for g in range(width // GROUP):
        for part, matrix in enumerate((query, key, value)):
            packed[:, pl.ds((3 * g + part) * GROUP, GROUP)] = matrix[:, pl.ds(g * GROUP, GROUP)]
    packed[:, pl.ds(3 * width, 128)] = table[...].astype(F32).T[:own, :].astype(BF)


def pack(query, key, value, rows):
    own, width = query.shape
    table = jnp.pad(rows, ((0, 128 - rows.shape[0]), (0, 128 - own)))
    vmem = pl.BlockSpec(memory_space=pltpu.VMEM)
    return call(
        pack_kernel,
        1,
        in_specs=[vmem] * 4,
        out_specs=vmem,
        out_shape=jax.ShapeDtypeStruct((own, 3 * width + 128), BF),
        name="pack",
    )(query, key, value, table)


def turn_kernel(packed, vecs):
    vecs[...] = packed[...].astype(F32).T[: vecs.shape[0], :]


def turn(packed, first):
    width = packed.shape[0]
    return call(
        turn_kernel,
        1,
        grid=(1,),
        in_specs=[pl.BlockSpec((width, 128), lambda _: (0, first // 128))],
        out_specs=pl.BlockSpec(memory_space=pltpu.VMEM),
        out_shape=jax.ShapeDtypeStruct((16, width), F32),
        name="turn",
    )(packed)


class Cube:
    def __init__(self, mesh):
        self.n_dp, self.n_fsdp = mesh.shape["dp"], mesh.shape["fsdp"]
        self.n = self.n_dp * self.n_fsdp
        self.bits = self.n.bit_length() - 1
        inner = self.n_fsdp.bit_length() - 1
        assert self.n == 1 << self.bits and self.n_fsdp == 1 << inner
        self.near = list(range(1, inner))
        self.far = list(range(inner, self.bits))

    def swap(self, value, bit):
        return lax.ppermute(value, AXES, [(i, i ^ (1 << bit)) for i in range(self.n)])

    def my_bit(self, bit):
        return (lax.axis_index(AXES) >> bit) & 1

    def join(self, mine, other, bit, done):
        at = sum(b > bit for b in done)
        last = self.my_bit(bit) == 1
        return jnp.stack([jnp.where(last, other, mine), jnp.where(last, mine, other)], at)

    def gather_near(self, piece, step, done):
        bit = self.near[::-1][step]
        return self.join(piece, self.swap(piece, bit), bit, done), [*done, bit]

    def halve(self, piece):
        half = piece.shape[-1] // 256 * 128
        return [piece[..., :half], piece[..., half:]]

    def gather_far(self, parts, step, done):
        orders = [self.far[::-1], self.far[:1] + self.far[:0:-1]]
        bits = [order[step] for order in orders]
        before = [[*done, *order[:step]] for order in orders]
        return [self.join(p, self.swap(p, bit), bit, d) for p, bit, d in zip(parts, bits, before)]

    def gather_core(self, parts, others):
        done = self.near + self.far
        whole = jnp.concatenate([self.join(p, o, 0, done) for p, o in zip(parts, others)], -1)
        return whole.reshape(-1, whole.shape[-1])

    def fold(self, part, left, bit):
        at = left.index(bit)
        rest = left[:at] + left[at + 1 :]
        mine = self.my_bit(bit)
        keep = lax.dynamic_index_in_dim(part, mine, at, keepdims=False)
        give = lax.dynamic_index_in_dim(part, 1 - mine, at, keepdims=False)
        total = keep.astype(F32) + self.swap(give, bit).astype(F32)
        return (total.astype(BF) if rest else total), rest

    def scatter_core(self, given):
        left = list(range(self.bits - 1, -1, -1))
        if len(given) == 2:
            keep, give = given
            part = (keep.astype(F32) + self.swap(give, 0).astype(F32)).astype(BF)
            part = part.reshape((2,) * (self.bits - 1) + part.shape[1:])
        else:
            whole = given[0].reshape((2,) * self.bits + (-1, given[0].shape[-1]))
            part, _ = self.fold(whole, left, 0)
        return part

    def scatter_far(self, parts, step):
        made = []
        for part, order in zip(parts, (self.far, self.far[1:] + self.far[:1])):
            left = [b for b in range(self.bits - 1, 0, -1) if b not in order[:step]]
            made.append(self.fold(part, left, order[step])[0])
        return made


class Flow:
    def __init__(self, cube, parts):
        self.cube, self.parts, self.left = cube, list(parts), list(range(cube.bits - 1, 0, -1))
        self.todo = [("far", i) for i in range(len(cube.far))] + [("near", bit) for bit in cube.near]

    def step(self, *after):
        if not self.todo:
            return
        (where, i), *self.todo = self.todo
        parts = [tie(p, *after) for p in self.parts] if after else self.parts
        if where == "far":
            self.parts = self.cube.scatter_far(parts, i)
        else:
            part = jnp.concatenate(parts, -1) if len(parts) > 1 else parts[0]
            left = [b for b in self.cube.near if b >= i][::-1]
            self.parts = [self.cube.fold(part, left, i)[0]]

    def finish(self):
        while self.todo:
            self.step()
        return self.parts[0]


def tie(value, *others):
    return lax.optimization_barrier((value, *others))[0]


def body(cube, *args):
    (
        tokens, seq_lengths, query_weight, query_bias, key_weight, value_weight, value_bias, out_weight, out_bias,
        first_gain, first_shift, up_weight, up_bias, down_weight, down_bias, second_gain, second_shift, out_grad,
    ) = args
    n = cube.n
    width = tokens.shape[1]
    own = width // n
    groups = width // GROUP
    hidden = up_weight.shape[1]
    each = hidden // width
    core = cube.my_bit(0).astype(jnp.int32).reshape(1, 1)

    vectors = (query_bias, value_bias, out_bias, first_gain, first_shift, down_bias, second_gain, second_shift)
    rows = jnp.concatenate([jnp.stack(vectors), up_bias.reshape(each, own)])
    piece, done = pack(query_weight, key_weight, value_weight, rows), []
    out_up = lax.all_gather(jnp.concatenate([out_weight, up_weight], 1), AXES, axis=0, tiled=True)
    down_piece, down_done = down_weight, []
    steps_near, steps_far = len(cube.near), len(cube.far)
    for step in range(steps_near):
        piece, done = cube.gather_near(piece, step, done)
    parts = cube.halve(piece)
    for step in range(max(steps_far, steps_near)):
        if step < steps_near:
            down_piece = tie(down_piece, *parts)
        if step < steps_far:
            parts = cube.gather_far(parts, step, done)
        if step < steps_near:
            down_piece, down_done = cube.gather_near(down_piece, step, down_done)
    packed = cube.gather_core(parts, [cube.swap(p, 0) for p in parts])
    vecs = turn(packed, 3 * GROUP * groups)
    up_b = vecs[8 : 8 + each].reshape(each, n, own).transpose(1, 0, 2).reshape(1, hidden)
    tok_t = tokens.T

    down_parts = [tie(p, packed) for p in cube.halve(down_piece)]
    made, wait = [], [tok_t, up_b]
    for g in range(groups):
        if g < steps_far:
            down_parts = cube.gather_far(down_parts, g, down_done)
        made.append(attend(seq_lengths, tokens, packed, g, vecs, wait))
        wait = [made[-1][2], *down_parts]
        down_parts = [tie(p, made[-1][2]) for p in down_parts] if g < steps_far else down_parts
    for step in range(groups, steps_far):
        down_parts = cube.gather_far(down_parts, step, down_done)
    ctxs = [m[1] for m in made]
    down_others = [cube.swap(p, 0) for p in down_parts]
    if hidden // n % 16:
        down = [cube.gather_core(down_parts, down_others)]
    else:
        down = [p.reshape(-1, *p.shape[-2:]) for p in (*down_parts, *down_others)]
    *down_dw, output, normed, inverse, low, slope, second, back_low, sums_two = forward(
        core, ctxs, tokens, out_up, up_b, down, vecs, out_grad, n
    )
    flows = [Flow(cube, cube.halve(cube.scatter_core(down_dw)))]

    *dws, up_sums, grad, att_back, sums_one = backward(
        core, back_low, down, slope, low, out_up, second, normed, inverse, ctxs, vecs, n
    )
    half = 1 if UP_AT_ONCE else len(dws) // 2
    out_dw = dws[half:]
    wait = flows[0].parts
    flows[0].step(sums_one)
    if UP_AT_ONCE:
        own_up = lax.psum_scatter(dws[0], AXES, scatter_dimension=0, tiled=True).astype(F32)
    else:
        flows.append(Flow(cube, cube.halve(cube.scatter_core(dws[:half]))))
    up_sums = up_sums[0].reshape(width, each).T
    later, sums_qkv = [], []
    for g in range(groups):
        qkv, ctx, lse = made[g]
        extras = (*sums_qkv, sums_one, sums_two, up_sums) if g == groups - 1 else ()
        *dw, grad, sums = attend_back(
            seq_lengths, core, tok_t, packed, out_up, g, qkv, ctx, lse, att_back, grad, n, extras, out_dw if g == 0 else (),
            wait,
        )
        sums_qkv.append(sums)
        wait = [p for flow in flows for p in flow.parts]
        for flow in flows:
            flow.step(sums)
        if g == 0:
            flows.append(Flow(cube, cube.halve(cube.scatter_core(dw))))
        else:
            later.append(cube.scatter_core(dw))
    own_down, *own_up_too, first = [flow.finish() for flow in flows]
    if own_up_too:
        (own_up,) = own_up_too
    both = Flow(cube, later).finish()
    owned = [first]
    owned += [both[:, g * 3 * GROUP : (g + 1) * 3 * GROUP + (128 if g == groups - 2 else 0)] for g in range(groups - 1)]
    own_out = owned[0][:, 3 * GROUP :]
    own_q, own_k, own_v = [
        jnp.concatenate([p[:, part * GROUP : (part + 1) * GROUP] for p in owned], 1) for part in range(3)
    ]
    own_vec = owned[-1][:, 3 * GROUP :]
    q_b, v_b, out_b, gain_one, shift_one, down_b, gain_two, shift_two = [own_vec[:, j] for j in range(8)]
    own_up_b = own_vec[:, 8 : 8 + each].reshape(-1)
    return (
        output, grad, own_q, q_b, own_k, own_v, v_b, own_out, out_b, gain_one, shift_one,
        own_up, own_up_b, own_down, down_b, gain_two, shift_two,
    )


def solution(mesh):
    both = P(AXES)
    rows = P(AXES, None)
    matrix, vector = rows, both
    in_specs = (
        rows, rows, matrix, vector, matrix, matrix, vector, matrix, vector, vector, vector,
        matrix, vector, matrix, vector, vector, vector, rows,
    )
    out_specs = (
        rows, rows, matrix, vector, matrix, matrix, vector, matrix, vector, vector, vector,
        matrix, vector, matrix, vector, vector, vector,
    )
    return jax.shard_map(
        functools.partial(body, Cube(mesh)), mesh=mesh, in_specs=in_specs, out_specs=out_specs, check_vma=False
    )
```

time: 458 us -> 331 us (0.72)
  waiting for transfers between devices: 145 us -> 74.6 us
  local copies, waits for them, and re-layouts: 79.4 us -> 31.3 us
  other arithmetic: 29.9 us -> 22.4 us
    ppermute x25 -> x45, waiting for transfers between devices: 145 us -> 74.5 us  [swap(): return lax.ppermute(value, AXES, [(i, i ^ 1 << bit) for i in range(self.n)])]
    unnamed x130 -> x67, local copies, waits for them, and re-layouts: 34.3 us -> 18.5 us
    slice x18 -> x8, local copies, waits for them, and re-layouts: 14.7 us -> 2.36 us  [the longest x1 0.82 us: body(): own_vec[:, j]]
    dynamic_slice x7 -> x4, local copies, waits for them, and re-layouts: 8.82 us -> 0.16 us  [the longest x2 0.11 us: fold(): keep = lax.dynamic_index_in_dim(part, mine, at, keepdims=False)]
    reshape x6 -> x4, local copies, waits for them, and re-layouts: 9.87 us -> 1.58 us  [the longest x1 0.74 us: body(): rows = jnp.concatenate([jnp.stack(vectors), up_bias.reshape(each, own)])]
    convert_element_type x17 -> x25, other arithmetic: 15.2 us -> 7.86 us  [the longest x5 6.21 us: scatter_core(): part = (keep.astype(F32) + self.swap(give, 0).astype(F32)).astype(BF)]
    ppermute x25 -> x45, starting transfers between devices: 55.1 us -> 56.1 us  [swap(): return lax.ppermute(value, AXES, [(i, i ^ 1 << bit) for i in range(self.n)])]
    pallas_call x12 -> x10, Pallas kernels: 127 us -> 128 us  [call(): return lambda *operands: made(*map(place, operands), *after)]
  transfers between devices with their start and end apart: 26 -> 46, of which waited for: 17 -> 22; matrix products, arithmetic and copies ran while one was open for 11% -> 9% of each run, Pallas kernels for 14% -> 28%
where the time goes in v2:
time: 331 us; the launch traced here: 327 us
  Pallas kernels  128 us (39%)
  waiting for transfers between devices  74.6 us (23%)
  starting transfers between devices  56.1 us (17%)
  local copies, waits for them, and re-layouts  31.3 us (9%)
  other arithmetic  22.4 us (7%)
  between operations  15.2 us (5%)
    pallas_call x10, Pallas kernels, call(): return lambda *operands: made(*map(place, operands), *after)  128 us
    ppermute x45, waiting for transfers between devices, swap(): return lax.ppermute(value, AXES, [(i, i ^ 1 << bit) for i in range(self.n)])  74.5 us
    ppermute x45, starting transfers between devices, swap(): return lax.ppermute(value, AXES, [(i, i ^ 1 << bit) for i in range(self.n)])  56.1 us
    unnamed x67, local copies, waits for them, and re-layouts  18.5 us
    another operation x25, other arithmetic, join(): jnp.stack([jnp.where(last, other, mine), jnp.where(last, mine, other)], at)  8.63 us
  transfers between devices with their start and end apart: 46, of which 22 were waited for; matrix products, arithmetic and copies ran while one was open for 9% of the time, Pallas kernels for 28%

profile of v2, /device:TPU:0, one launch (start us, length us, event | category | flops | bytes accessed | tf_op | source)
XLA Modules:
  0.0 327.2 jit_solution(8833046084770092932)
XLA Ops:
  11.2 4.1 %collective-permute-start = (bf16[24,2432]{1,0:T(8,128)(2,1)S(1)}, bf16[24,2432]{1,0:T(8,128)(2,1)S(1)}, u32[]{:S(2)}, u32[]{:S(2)}) collective-permute-start(bf16[24,2432]{1,0:T(8,128)(2,1)S(1)} %pack.1), channel_id=1, source_target_pairs={{0,4},{1,5},{2,6},{3,7},{4,0},{5,1},{6,2},{7,3},{8,12},{9,13},{10,... | collective-permute-start | bytes 350216 | tf_op jit(solution)/shard_map/ppermute | solution.py:579
  15.2 1.6 pad_maximum_fusion.13
  16.9 4.0 %collective-permute-done = bf16[24,2432]{1,0:T(8,128)(2,1)S(1)} collective-permute-done((bf16[24,2432]{1,0:T(8,128)(2,1)S(1)}, bf16[24,2432]{1,0:T(8,128)(2,1)S(1)}, u32[]{:S(2)}, u32[]{:S(2)}) %collective-permute-start) | collective-permute-done | bytes 116768 | tf_op jit(solution)/shard_map/ppermute | solution.py:579
  21.8 6.4 %collective-permute-done.1 = bf16[2,24,2432]{2,1,0:T(8,128)(2,1)S(1)} collective-permute-done((bf16[2,24,2432]{2,1,0:T(8,128)(2,1)S(1)}, bf16[2,24,2432]{2,1,0:T(8,128)(2,1)S(1)}, u32[]{:S(2)}, u32[]{:S(2)}) %collective-permute-start.1) | collective-permute-done | bytes 233504 | tf_op jit(solution)/shard_map/ppermute | solution.py:579
  28.4 4.2 %collective-permute-start.8 = (bf16[96,768]{1,0:T(8,128)(2,1)S(1)}, bf16[96,768]{1,0:T(8,128)(2,1)S(1)}, u32[]{:S(2)}, u32[]{:S(2)}) collective-permute-start(bf16[96,768]{1,0:T(8,128)(2,1)S(1)} %copy-done.31), channel_id=1, source_target_pairs={{0,4},{1,5},{2,6},{3,7},{4,0},{5,1},{6,2},{7,3},{8,12},{9,13},{10,... | collective-permute-start | bytes 442376 | tf_op jit(solution)/shard_map/ppermute | solution.py:579
  32.5 1.5 collective-permute-start.2
  34.1 1.5 collective-permute-start.5
  35.5 5.3 %collective-permute-done.8 = bf16[96,768]{1,0:T(8,128)(2,1)S(1)} collective-permute-done((bf16[96,768]{1,0:T(8,128)(2,1)S(1)}, bf16[96,768]{1,0:T(8,128)(2,1)S(1)}, u32[]{:S(2)}, u32[]{:S(2)}) %collective-permute-start.8) | collective-permute-done | bytes 147488 | tf_op jit(solution)/shard_map/ppermute | solution.py:579
  41.1 1.6 collective-permute-start.3
  42.8 1.6 collective-permute-start.6
  44.5 13.2 %collective-permute-done.3 = bf16[2,2,2,24,1152]{4,3,1,2,0:T(8,128)(2,1)S(1)} collective-permute-done((bf16[2,2,2,24,1152]{4,3,1,2,0:T(8,128)(2,1)S(1)}, bf16[2,2,2,24,1152]{4,3,1,2,0:T(8,128)(2,1)S(1)}, u32[]{:S(2)}, u32[]{:S(2)}) %collective-permute-start.3) | collective-permute-done | bytes 442400 | tf_op jit(solution)/shard_map/ppermute | solution.py:579
  61.5 1.4 select_bitcast_fusion.3
  62.9 1.3 select_bitcast_fusion.1
  65.1 2.1 copy.50
  67.2 1.6 collective-permute-start.11
  68.7 1.8 collective-permute-start.10
  71.3 2.1 copy-done
  74.0 2.1 copy-done.1
  76.1 7.4 %attend.3 = (bf16[1024,768]{1,0:T(8,128)(2,1)S(1)}, bf16[1024,256]{1,0:T(8,128)(2,1)S(1)}, f32[8,1024]{1,0:T(8,128)S(1)}) custom-call(s32[1,9]{1,0:T(1,128)S(1)} %copy-done.30, bf16[1024,768]{1,0:T(8,128)(2,1)S(1)} %copy-done.2, bf16[768,2432]{1,0:T(8,128)(2,1)S(1)} %bitcast.216, f32[16,768]{1,0:T(8,128)S(1)} %turn.1.refs_3_.refs_8_.refs_11_, ...), custom_call_target="tpu_custom_call" | custom-call | flops 9000000 | tf_op jit(solution)/shard_map/attend/pallas_call | solution.py:47
  83.6 1.5 select_bitcast_fusion.13
  86.4 1.6 collective-permute-start.13
  88.0 1.3 collective-permute-start.12
  89.2 7.5 %attend.4 = (bf16[1024,768]{1,0:T(8,128)(2,1)S(1)}, bf16[1024,256]{1,0:T(8,128)(2,1)S(1)}, f32[8,1024]{1,0:T(8,128)S(1)}) custom-call(s32[1,9]{1,0:T(1,128)S(1)} %copy-done.30, bf16[1024,768]{1,0:T(8,128)(2,1)S(1)} %copy-done.2, bf16[768,2432]{1,0:T(8,128)(2,1)S(1)} %bitcast.217, f32[16,768]{1,0:T(8,128)S(1)} %turn.1.refs_3_.refs_8_.refs_11_, ...), custom_call_target="tpu_custom_call" | custom-call | flops 9000000 | tf_op jit(solution)/shard_map/attend/pallas_call | solution.py:47
  96.8 4.7 %collective-permute-done.13 = bf16[2,2,2,96,384]{4,3,2,1,0:T(8,128)(2,1)S(1)} collective-permute-done((bf16[2,2,2,96,384]{4,3,2,1,0:T(8,128)(2,1)S(1)}, bf16[2,2,2,96,384]{4,3,2,1,0:T(8,128)(2,1)S(1)}, u32[]{:S(2)}, u32[]{:S(2)}) %collective-permute-start.13) | collective-permute-done | bytes 589856 | tf_op jit(solution)/shard_map/ppermute | solution.py:579
  101.8 1.2 collective-permute-done.12
  103.8 1.2 copy.55
  105.1 7.3 %attend.5 = (bf16[1024,768]{1,0:T(8,128)(2,1)S(1)}, bf16[1024,256]{1,0:T(8,128)(2,1)S(1)}, f32[8,1024]{1,0:T(8,128)S(1)}) custom-call(s32[1,9]{1,0:T(1,128)S(1)} %copy-done.30, bf16[1024,768]{1,0:T(8,128)(2,1)S(1)} %copy-done.2, bf16[768,2432]{1,0:T(8,128)(2,1)S(1)} %bitcast.218, f32[16,768]{1,0:T(8,128)S(1)} %turn.1.refs_3_.refs_8_.refs_11_, ...), custom_call_target="tpu_custom_call" | custom-call | flops 9000000 | tf_op jit(solution)/shard_map/attend/pallas_call | solution.py:47
  113.2 1.2 copy-done.14
  115.5 35.8 %forward.1 = (bf16[16,96,768]{2,1,0:T(8,128)(2,1)S(1)}, bf16[16,96,768]{2,1,0:T(8,128)(2,1)}, bf16[1024,768]{1,0:T(8,128)(2,1)}, f32[1024,768]{1,0:T(8,128)}, f3...) custom-call(s32[1,1]{1,0:T(1,128)} %bitcast.refs_0_.refs_1_, ...), custom_call_target="tpu_custom_call" | custom-call | flops 32000000 | tf_op jit(solution)/shard_map/forward/pallas_call | solution.py:47
  151.3 1.4 copy-done.13
  152.7 1.2 copy-done.20
  153.9 1.2 copy-done.21
  155.9 28.4 %backward.1 = (bf16[16,24,3072]{2,1,0:T(8,128)(2,1)S(1)}, bf16[16,24,3072]{2,1,0:T(8,128)(2,1)}, bf16[16,24,768]{2,1,0:T(8,128)(2,1)S(1)}, bf16[16,24,768]{2,1,0...) custom-call(s32[1,1]{1,0:T(1,128)} %bitcast.refs_0_.refs_1_, ...), custom_call_target="tpu_custom_call" | custom-call | flops 26000000 | tf_op jit(solution)/shard_map/backward/pallas_call | solution.py:47
  184.3 1.4 copy-done.11
  187.8 1.2 reshape_squeeze.3
  190.1 3.1 add_convert_fusion.1
  193.7 1.9 collective-permute-start.18
  195.6 2.5 add_convert_fusion
  198.7 1.6 collective-permute-start.17
  200.4 13.6 %attend_back.3 = (bf16[16,24,1536]{2,1,0:T(8,128)(2,1)S(1)}, bf16[16,24,1536]{2,1,0:T(8,128)(2,1)S(1)}, f32[1024,768]{1,0:T(8,128)S(1)}, f32[8,768]{1,0:T(8,128)S(1)}) custom-call(s32[1,9]{1,0:T(1,128)S(1)} %copy-done.30, s32[1,1]{1,0:T(1,128)} %bitcast.refs_0_.refs_1_, bf16[768,1024]{1,0:T(8,128)(2,1)S(1)} %bitcast.220, bf16[768,2432]{1,0:T(8,128)(2,1)} %bitcast.212, ...), custom_call_target="tpu_custom_call" | custom-call | flops 15000000 | tf_op jit(solution)/shard_map/attend_back/pallas_call | solution.py:47
  214.3 3.3 collective-permute-start.23
  217.8 1.2 collective-permute-start.22
  220.8 13.3 %attend_back.4 = (bf16[16,24,768]{2,1,0:T(8,128)(2,1)S(1)}, bf16[16,24,768]{2,1,0:T(8,128)(2,1)S(1)}, f32[1024,768]{1,0:T(8,128)S(1)}, f32[8,768]{1,0:T(8,128)S(1)}) custom-call(s32[1,9]{1,0:T(1,128)S(1)} %copy-done.30, s32[1,1]{1,0:T(1,128)} %bitcast.refs_0_.refs_1_, bf16[768,1024]{1,0:T(8,128)(2,1)S(1)} %bitcast.221, bf16[768,2432]{1,0:T(8,128)(2,1)} %bitcast.213, ...), custom_call_target="tpu_custom_call" | custom-call | flops 15000000 | tf_op jit(solution)/shard_map/attend_back/pallas_call | solution.py:47
  234.4 1.8 collective-permute-start.40
  236.4 2.9 collective-permute-start.39
  240.7 4.7 %collective-permute-done.40 = bf16[2,2,24,1536]{3,2,1,0:T(8,128)(2,1)S(1)} collective-permute-done((bf16[2,2,24,1536]{3,2,1,0:T(8,128)(2,1)S(1)}, bf16[2,2,24,1536]{3,2,1,0:T(8,128)(2,1)S(1)}, u32[]{:S(2)}, u32[]{:S(2)}) %collective-permute-start.40) | collective-permute-done | bytes 294944 | tf_op jit(solution)/shard_map/ppermute | solution.py:579
  247.5 1.6 collective-permute-done.43
  251.0 14.1 %attend_back.5 = (bf16[16,24,896]{2,1,0:T(8,128)(2,1)S(1)}, bf16[16,24,896]{2,1,0:T(8,128)(2,1)S(1)}, f32[1024,768]{1,0:T(8,128)}, f32[8,768]{1,0:T(8,128)}) custom-call(s32[1,9]{1,0:T(1,128)S(1)} %copy-done.30, s32[1,1]{1,0:T(1,128)} %bitcast.refs_0_.refs_1_, bf16[768,1024]{1,0:T(8,128)(2,1)S(1)} %bitcast.222, bf16[768,2432]{1,0:T(8,128)(2,1)} %bitcast.214, ...), custom_call_target="tpu_custom_call" | custom-call | flops 15000000 | tf_op jit(solution)/shard_map/attend_back/pallas_call | solution.py:47
  265.1 2.2 collective-permute-start.44
  267.4 3.9 %collective-permute-start.41 = (bf16[2,24,3072]{2,1,0:T(8,128)(2,1)S(1)}, bf16[2,24,3072]{2,1,0:T(8,128)(2,1)S(1)}, u32[]{:S(2)}, u32[]{:S(2)}) collective-permute-start(bf16[2,24,3072]{2,1,0:T(8,128)(2,1)S(1)} %dynamic-slice_bitcast_fusion.5), channel_id=1, source_target_pairs={{0,2},{1,3},{2,0},{3,1},{4,6},{5,7},{6,4},{7,5},{8,10},{9,11},{10,... | collective-permute-start | bytes 884744 | tf_op jit(solution)/shard_map/ppermute | solution.py:579
  273.2 2.6 collective-permute-done.44
  276.8 1.5 collective-permute-start.33
  278.3 1.7 collective-permute-done.41
  280.8 1.3 collective-permute-start.28
  283.1 2.9 collective-permute-done.28
  286.1 1.3 collective-permute-done.26
  287.5 1.9 collective-permute-start.29
  291.2 1.5 collective-permute-done.29
  292.8 6.9 %collective-permute-done.35 = bf16[2,2,2,24,896]{4,3,1,2,0:T(8,128)(2,1)S(1)} collective-permute-done((bf16[2,2,2,24,896]{4,3,1,2,0:T(8,128)(2,1)S(1)}, bf16[2,2,2,24,896]{4,3,1,2,0:T(8,128)(2,1)S(1)}, u32[]{:S(2)}, u32[]{:S(2)}) %collective-permute-start.35) | collective-permute-done | bytes 344096 | tf_op jit(solution)/shard_map/ppermute | solution.py:579
  300.2 1.2 collective-permute-start.30
  301.4 3.9 %collective-permute-done.36 = bf16[2,2,24,896]{3,2,0,1:T(8,128)(2,1)S(1)} collective-permute-done((bf16[2,2,24,896]{3,2,0,1:T(8,128)(2,1)S(1)}, bf16[2,2,24,896]{3,2,0,1:T(8,128)(2,1)S(1)}, u32[]{:S(2)}, u32[]{:S(2)}) %collective-permute-start.36) | collective-permute-done | bytes 172064 | tf_op jit(solution)/shard_map/ppermute | solution.py:579
  306.1 4.6 %collective-permute-done.37 = bf16[2,24,1664]{2,1,0:T(8,128)(2,1)S(1)} collective-permute-done((bf16[2,24,1664]{2,1,0:T(8,128)(2,1)S(1)}, bf16[2,24,1664]{2,1,0:T(8,128)(2,1)S(1)}, u32[]{:S(2)}, u32[]{:S(2)}) %collective-permute-start.37) | collective-permute-done | bytes 159776 | tf_op jit(solution)/shard_map/ppermute | solution.py:579
  310.8 1.3 collective-permute-start.38
  312.7 4.0 %collective-permute-done.38 = bf16[24,1664]{1,0:T(8,128)(2,1)S(1)} collective-permute-done((bf16[24,1664]{1,0:T(8,128)(2,1)S(1)}, bf16[24,1664]{1,0:T(8,128)(2,1)S(1)}, u32[]{:S(2)}, u32[]{:S(2)}) %collective-permute-start.38) | collective-permute-done | bytes 79904 | tf_op jit(solution)/shard_map/ppermute | solution.py:579
  (220 shorter events, 41.0 us)
Async XLA Ops:
  7.2 108.3 %all-gather.2.cloned.1.call-start = ((), (), s32[]{:S(2)}) async-start(), calls=%async_computation | async-start | bytes 6082560 | tf_op jit(solution)/shard_map/all_gather | solution.py:679
  11.2 9.8 %collective-permute-start = (bf16[24,2432]{1,0:T(8,128)(2,1)S(1)}, bf16[24,2432]{1,0:T(8,128)(2,1)S(1)}, u32[]{:S(2)}, u32[]{:S(2)}) collective-permute-start(bf16[24,2432]{1,0:T(8,128)(2,1)S(1)} %pack.1), channel_id=1, source_target_pairs={{0,4},{1,5},{2,6},{3,7},{4,0},{5,1},{6,2},{7,3},{8,12},{9,13},{10,... | collective-permute-start | bytes 350216 | tf_op jit(solution)/shard_map/ppermute | solution.py:579
  16.9 11.5 %copy-start.31 = (bf16[96,768]{1,0:T(8,128)(2,1)S(1)}, bf16[96,768]{1,0:T(8,128)(2,1)}, u32[]{:S(2)}) copy-start(bf16[96,768]{1,0:T(8,128)(2,1)} %param.31) | copy-start | bytes 442372
  21.0 7.2 %collective-permute-start.1 = (bf16[2,24,2432]{2,1,0:T(8,128)(2,1)S(1)}, bf16[2,24,2432]{2,1,0:T(8,128)(2,1)S(1)}, u32[]{:S(2)}, u32[]{:S(2)}) collective-permute-start(bf16[2,24,2432]{2,1,0:T(8,128)(2,1)S(1)} %pad_maximum_fusion.11), channel_id=1, source_target_pairs={{0,2},{1,3},{2,0},{3,1},{4,6},{5,7},{6,4},{7,5},{8,10},{9,11},{10,... | collective-permute-start | bytes 700424 | tf_op jit(solution)/shard_map/ppermute | solution.py:579
  28.4 12.5 %collective-permute-start.8 = (bf16[96,768]{1,0:T(8,128)(2,1)S(1)}, bf16[96,768]{1,0:T(8,128)(2,1)S(1)}, u32[]{:S(2)}, u32[]{:S(2)}) collective-permute-start(bf16[96,768]{1,0:T(8,128)(2,1)S(1)} %copy-done.31), channel_id=1, source_target_pairs={{0,4},{1,5},{2,6},{3,7},{4,0},{5,1},{6,2},{7,3},{8,12},{9,13},{10,... | collective-permute-start | bytes 442376 | tf_op jit(solution)/shard_map/ppermute | solution.py:579
  32.5 8.4 %collective-permute-start.2 = (bf16[2,2,24,1152]{3,2,0,1:T(8,128)(2,1)S(1)}, bf16[2,2,24,1152]{3,2,0,1:T(8,128)(2,1)S(1)}, u32[]{:S(2)}, u32[]{:S(2)}) collective-permute-start(bf16[2,2,24,1152]{3,2,0,1:T(8,128)(2,1)S(1)} %pad_maximum_fusion.12), channel_id=1, source_target_pairs={{0,16},{1,17},{2,18},{3,19},{4,20},{5,21},{6,22},{7,23},{8,24},{9,... | collective-permute-start | bytes 663560 | tf_op jit(solution)/shard_map/ppermute | solution.py:579
  34.1 8.6 %collective-permute-start.5 = (bf16[2,2,24,1280]{3,2,0,1:T(8,128)(2,1)S(1)}, bf16[2,2,24,1280]{3,2,0,1:T(8,128)(2,1)S(1)}, u32[]{:S(2)}, u32[]{:S(2)}) collective-permute-start(bf16[2,2,24,1280]{3,2,0,1:T(8,128)(2,1)S(1)} %pad_maximum_fusion.10), channel_id=1, source_target_pairs={{0,8},{1,9},{2,10},{3,11},{4,12},{5,13},{6,14},{7,15},{8,0},{9,1},... | collective-permute-start | bytes 737288 | tf_op jit(solution)/shard_map/ppermute | solution.py:579
  41.1 16.6 %collective-permute-start.3 = (bf16[2,2,2,24,1152]{4,3,1,2,0:T(8,128)(2,1)S(1)}, bf16[2,2,2,24,1152]{4,3,1,2,0:T(8,128)(2,1)S(1)}, u32[]{:S(2)}, u32[]{:S(2)}) collective-permute-start(bf16[2,2,2,24,1152]{4,3,1,2,0:T(8,128)(2,1)S(1)} %pad_maximum_fusion.7), channel_id=1, source_target_pairs={{0,8},{1,9},{2,10},{3,11},{4,12},{5,13},{6,14},{7,15},{8,0},{9,1},... | collective-permute-start | bytes 1327112 | tf_op jit(solution)/shard_map/ppermute | solution.py:579
  42.8 15.9 %collective-permute-start.6 = (bf16[2,2,2,24,1280]{4,3,1,2,0:T(8,128)(2,1)S(1)}, bf16[2,2,2,24,1280]{4,3,1,2,0:T(8,128)(2,1)S(1)}, u32[]{:S(2)}, u32[]{:S(2)}) collective-permute-start(bf16[2,2,2,24,1280]{4,3,1,2,0:T(8,128)(2,1)S(1)} %pad_maximum_fusion.6), channel_id=1, source_target_pairs={{0,16},{1,17},{2,18},{3,19},{4,20},{5,21},{6,22},{7,23},{8,24},{9,... | collective-permute-start | bytes 1474568 | tf_op jit(solution)/shard_map/ppermute | solution.py:579
  44.5 15.1 %collective-permute-start.9 = (bf16[2,96,768]{2,1,0:T(8,128)(2,1)S(1)}, bf16[2,96,768]{2,1,0:T(8,128)(2,1)S(1)}, u32[]{:S(2)}, u32[]{:S(2)}) collective-permute-start(bf16[2,96,768]{2,1,0:T(8,128)(2,1)S(1)} %pad_maximum_fusion.9), channel_id=1, source_target_pairs={{0,2},{1,3},{2,0},{3,1},{4,6},{5,7},{6,4},{7,5},{8,10},{9,11},{10,... | collective-permute-start | bytes 884744 | tf_op jit(solution)/shard_map/ppermute | solution.py:579
  58.8 2.8 collective-permute-start.4
  58.9 3.9 %collective-permute-start.7 = (bf16[2,2,2,2,24,1280]{5,4,2,3,1,0:T(8,128)(2,1)S(1)}, bf16[2,2,2,2,24,1280]{5,4,2,3,1,0:T(8,128)(2,1)}, u32[]{:S(2)}, u32[]{:S(2)}) collective-permute-start(bf16[2,2,2,2,24,1280]{5,4,2,3,1,0:T(8,128)(2,1)S(1)} %pad_maximum_fusion.2), channel_id=1, source_target_pairs={{0,1},{1,0},{2,3},{3,2},{4,5},{5,4},{6,7},{7,6},{8,9},{9,8},{10,11... | collective-permute-start | bytes 2949128 | tf_op jit(solution)/shard_map/ppermute | solution.py:579
  65.1 5.4 %copy-start.2 = (bf16[1024,768]{1,0:T(8,128)(2,1)S(1)}, bf16[1024,768]{1,0:T(8,128)(2,1)}, u32[]{:S(2)}) copy-start(bf16[1024,768]{1,0:T(8,128)(2,1)} %refs_4_.1) | copy-start | bytes 4718596
  67.2 16.4 %collective-permute-start.11 = (bf16[2,2,96,384]{3,2,1,0:T(8,128)(2,1)}, bf16[2,2,96,384]{3,2,1,0:T(8,128)(2,1)}, u32[]{:S(2)}, u32[]{:S(2)}) collective-permute-start(bf16[2,2,96,384]{3,2,1,0:T(8,128)(2,1)} %get-tuple-element.86), channel_id=1, source_target_pairs={{0,8},{1,9},{2,10},{3,11},{4,12},{5,13},{6,14},{7,15},{8,0},{9,1},... | collective-permute-start | bytes 884744 | tf_op jit(solution)/shard_map/ppermute | solution.py:579
  68.7 16.4 %collective-permute-start.10 = (bf16[2,2,96,384]{3,2,1,0:T(8,128)(2,1)}, bf16[2,2,96,384]{3,2,1,0:T(8,128)(2,1)}, u32[]{:S(2)}, u32[]{:S(2)}) collective-permute-start(bf16[2,2,96,384]{3,2,1,0:T(8,128)(2,1)} %get-tuple-element.85), channel_id=1, source_target_pairs={{0,16},{1,17},{2,18},{3,19},{4,20},{5,21},{6,22},{7,23},{8,24},{9,... | collective-permute-start | bytes 884744 | tf_op jit(solution)/shard_map/ppermute | solution.py:579
  71.3 2.1 copy-start
  74.0 2.1 copy-start.1
  83.5 2.7 copy-start.8
  83.5 2.9 copy-start.18
  86.4 15.1 %collective-permute-start.13 = (bf16[2,2,2,96,384]{4,3,2,1,0:T(8,128)(2,1)S(1)}, bf16[2,2,2,96,384]{4,3,2,1,0:T(8,128)(2,1)S(1)}, u32[]{:S(2)}, u32[]{:S(2)}) collective-permute-start(bf16[2,2,2,96,384]{4,3,2,1,0:T(8,128)(2,1)S(1)} %get-tuple-element.90.refs_6_), channel_id=1, source_target_pairs={{0,16},{1,17},{2,18},{3,19},{4,20},{5,21},{6,22},{7,23},{8,24},{9,... | collective-permute-start | bytes 1769480 | tf_op jit(solution)/shard_map/ppermute | solution.py:579
  88.0 15.0 %collective-permute-start.12 = (bf16[2,2,2,96,384]{4,3,2,1,0:T(8,128)(2,1)S(1)}, bf16[2,2,2,96,384]{4,3,2,1,0:T(8,128)(2,1)S(1)}, u32[]{:S(2)}, u32[]{:S(2)}) collective-permute-start(bf16[2,2,2,96,384]{4,3,2,1,0:T(8,128)(2,1)S(1)} %get-tuple-element.89.refs_5_), channel_id=1, source_target_pairs={{0,8},{1,9},{2,10},{3,11},{4,12},{5,13},{6,14},{7,15},{8,0},{9,1},... | collective-permute-start | bytes 1769480 | tf_op jit(solution)/shard_map/ppermute | solution.py:579
  96.7 4.9 %copy-start.16 = (bf16[1024,768]{1,0:T(8,128)(2,1)}, bf16[1024,768]{1,0:T(8,128)(2,1)S(1)}, u32[]{:S(2)}) copy-start(bf16[1024,768]{1,0:T(8,128)(2,1)S(1)} %get-tuple-element.104.refs_5_) | copy-start | bytes 4718596
  96.7 5.0 %copy-start.6 = (bf16[1024,256]{1,0:T(8,128)(2,1)}, bf16[1024,256]{1,0:T(8,128)(2,1)S(1)}, u32[]{:S(2)}) copy-start(bf16[1024,256]{1,0:T(8,128)(2,1)S(1)} %get-tuple-element.87.refs_2_.refs_9_.refs_6_) | copy-start | bytes 1572868
  101.8 3.3 %copy-start.3 = (bf16[2,2,2,2,96,384]{5,4,3,2,1,0:T(8,128)(2,1)}, bf16[2,2,2,2,96,384]{5,4,3,2,1,0:T(8,128)(2,1)S(1)}, u32[]{:S(2)}) copy-start(bf16[2,2,2,2,96,384]{5,4,3,2,1,0:T(8,128)(2,1)S(1)} %pad_maximum_fusion.1.refs_6_) | copy-start | bytes 3538948
  103.2 11.1 %collective-permute-start.14 = (bf16[2,2,2,2,96,384]{5,4,3,2,0,1:T(8,128)(2,1)S(1)}, bf16[2,2,2,2,96,384]{5,4,3,2,0,1:T(8,128)(2,1)S(1)}, u32[]{:S(2)}, u32[]{:S(2)}) collective-permute-start(bf16[2,2,2,2,96,384]{5,4,3,2,0,1:T(8,128)(2,1)S(1)} %pad_maximum_fusion), channel_id=1, source_target_pairs={{0,1},{1,0},{2,3},{3,2},{4,5},{5,4},{6,7},{7,6},{8,9},{9,8},{10,11... | collective-permute-start | bytes 3538952 | tf_op jit(solution)/shard_map/ppermute | solution.py:579
  103.3 12.2 %collective-permute-start.15 = (bf16[2,2,2,2,96,384]{5,4,3,2,1,0:T(8,128)(2,1)S(1)}, bf16[2,2,2,2,96,384]{5,4,3,2,1,0:T(8,128)(2,1)}, u32[]{:S(2)}, u32[]{:S(2)}) collective-permute-start(bf16[2,2,2,2,96,384]{5,4,3,2,1,0:T(8,128)(2,1)S(1)} %pad_maximum_fusion.1.refs_6_), channel_id=1, source_target_pairs={{0,1},{1,0},{2,3},{3,2},{4,5},{5,4},{6,7},{7,6},{8,9},{9,8},{10,11... | collective-permute-start | bytes 3538952 | tf_op jit(solution)/shard_map/ppermute | solution.py:579
  155.8 34.3 %collective-permute-start.16 = (bf16[16,96,768]{2,1,0:T(8,128)(2,1)}, bf16[16,96,768]{2,1,0:T(8,128)(2,1)}, u32[]{:S(2)}, u32[]{:S(2)}) collective-permute-start(bf16[16,96,768]{2,1,0:T(8,128)(2,1)} %get-tuple-element.110), channel_id=1, source_target_pairs={{0,1},{1,0},{2,3},{3,2},{4,5},{5,4},{6,7},{7,6},{8,9},{9,8},{10,11... | collective-permute-start | bytes 7077896 | tf_op jit(solution)/shard_map/ppermute | solution.py:579
  187.4 8.3 %collective-permute-start.19 = (bf16[16,24,3072]{2,1,0:T(8,128)(2,1)}, bf16[16,24,3072]{2,1,0:T(8,128)(2,1)}, u32[]{:S(2)}, u32[]{:S(2)}) collective-permute-start(bf16[16,24,3072]{2,1,0:T(8,128)(2,1)} %get-tuple-element.116), channel_id=1, source_target_pairs={{0,1},{1,0},{2,3},{3,2},{4,5},{5,4},{6,7},{7,6},{8,9},{9,8},{10,11... | collective-permute-start | bytes 7077896 | tf_op jit(solution)/shard_map/ppermute | solution.py:579
  193.2 2.4 copy-start.12
  193.7 25.2 %collective-permute-start.18 = (bf16[2,2,2,96,384]{4,3,2,1,0:T(8,128)(2,1)S(1)}, bf16[2,2,2,96,384]{4,3,2,1,0:T(8,128)(2,1)S(1)}, u32[]{:S(2)}, u32[]{:S(2)}) collective-permute-start(bf16[2,2,2,96,384]{4,3,2,1,0:T(8,128)(2,1)S(1)} %dynamic-slice_bitcast_fusion.2), channel_id=1, source_target_pairs={{0,16},{1,17},{2,18},{3,19},{4,20},{5,21},{6,22},{7,23},{8,24},{9,... | collective-permute-start | bytes 1769480 | tf_op jit(solution)/shard_map/ppermute | solution.py:579
  198.5 1.9 copy-start.9
  198.5 1.8 copy-start.19
  198.5 1.8 copy-start.23
  198.5 1.9 copy-start.25
  198.7 21.4 %collective-permute-start.17 = (bf16[2,2,2,96,384]{4,3,2,1,0:T(8,128)(2,1)S(1)}, bf16[2,2,2,96,384]{4,3,2,1,0:T(8,128)(2,1)S(1)}, u32[]{:S(2)}, u32[]{:S(2)}) collective-permute-start(bf16[2,2,2,96,384]{4,3,2,1,0:T(8,128)(2,1)S(1)} %dynamic-slice_bitcast_fusion.3), channel_id=1, source_target_pairs={{0,8},{1,9},{2,10},{3,11},{4,12},{5,13},{6,14},{7,15},{8,0},{9,1},... | collective-permute-start | bytes 1769480 | tf_op jit(solution)/shard_map/ppermute | solution.py:579
  214.0 3.7 %copy-start.10 = (f32[1024,768]{1,0:T(8,128)}, f32[1024,768]{1,0:T(8,128)S(1)}, u32[]{:S(2)}) copy-start(f32[1024,768]{1,0:T(8,128)S(1)} %get-tuple-element.111.refs_9_) | copy-start | bytes 9437188
  214.0 35.2 %collective-permute-start.24 = (bf16[16,24,1536]{2,1,0:T(8,128)(2,1)S(1)}, bf16[16,24,1536]{2,1,0:T(8,128)(2,1)S(1)}, u32[]{:S(2)}, u32[]{:S(2)}) collective-permute-start(bf16[16,24,1536]{2,1,0:T(8,128)(2,1)S(1)} %get-tuple-element.127), channel_id=1, source_target_pairs={{0,1},{1,0},{2,3},{3,2},{4,5},{5,4},{6,7},{7,6},{8,9},{9,8},{10,11... | collective-permute-start | bytes 3538952 | tf_op jit(solution)/shard_map/ppermute | solution.py:579
  214.3 19.8 %collective-permute-start.23 = (bf16[2,2,2,24,1536]{4,3,2,1,0:T(8,128)(2,1)S(1)}, bf16[2,2,2,24,1536]{4,3,2,1,0:T(8,128)(2,1)S(1)}, u32[]{:S(2)}, u32[]{:S(2)}) collective-permute-start(bf16[2,2,2,24,1536]{4,3,2,1,0:T(8,128)(2,1)S(1)} %dynamic-slice_bitcast_fusion), channel_id=1, source_target_pairs={{0,16},{1,17},{2,18},{3,19},{4,20},{5,21},{6,22},{7,23},{8,24},{9,... | collective-permute-start | bytes 1769480 | tf_op jit(solution)/shard_map/ppermute | solution.py:579
  217.8 18.4 %collective-permute-start.22 = (bf16[2,2,2,24,1536]{4,3,2,1,0:T(8,128)(2,1)S(1)}, bf16[2,2,2,24,1536]{4,3,2,1,0:T(8,128)(2,1)S(1)}, u32[]{:S(2)}, u32[]{:S(2)}) collective-permute-start(bf16[2,2,2,24,1536]{4,3,2,1,0:T(8,128)(2,1)S(1)} %dynamic-slice_bitcast_fusion.1), channel_id=1, source_target_pairs={{0,8},{1,9},{2,10},{3,11},{4,12},{5,13},{6,14},{7,15},{8,0},{9,1},... | collective-permute-start | bytes 1769480 | tf_op jit(solution)/shard_map/ppermute | solution.py:579
  219.1 1.7 copy-start.7
  219.1 1.7 copy-start.17
  219.2 20.9 %collective-permute-start.21 = (bf16[2,2,96,384]{3,2,1,0:T(8,128)(2,1)S(1)}, bf16[2,2,96,384]{3,2,1,0:T(8,128)(2,1)S(1)}, u32[]{:S(2)}, u32[]{:S(2)}) collective-permute-start(bf16[2,2,96,384]{3,2,1,0:T(8,128)(2,1)S(1)} %dynamic-slice_bitcast_fusion.10), channel_id=1, source_target_pairs={{0,8},{1,9},{2,10},{3,11},{4,12},{5,13},{6,14},{7,15},{8,0},{9,1},... | collective-permute-start | bytes 884744 | tf_op jit(solution)/shard_map/ppermute | solution.py:579
  220.3 18.9 %collective-permute-start.20 = (bf16[2,2,96,384]{3,2,1,0:T(8,128)(2,1)S(1)}, bf16[2,2,96,384]{3,2,1,0:T(8,128)(2,1)S(1)}, u32[]{:S(2)}, u32[]{:S(2)}) collective-permute-start(bf16[2,2,96,384]{3,2,1,0:T(8,128)(2,1)S(1)} %dynamic-slice_bitcast_fusion.11), channel_id=1, source_target_pairs={{0,16},{1,17},{2,18},{3,19},{4,20},{5,21},{6,22},{7,23},{8,24},{9,... | collective-permute-start | bytes 884744 | tf_op jit(solution)/shard_map/ppermute | solution.py:579
  234.4 11.1 %collective-permute-start.40 = (bf16[2,2,24,1536]{3,2,1,0:T(8,128)(2,1)S(1)}, bf16[2,2,24,1536]{3,2,1,0:T(8,128)(2,1)S(1)}, u32[]{:S(2)}, u32[]{:S(2)}) collective-permute-start(bf16[2,2,24,1536]{3,2,1,0:T(8,128)(2,1)S(1)} %dynamic-slice_bitcast_fusion.6), channel_id=1, source_target_pairs={{0,8},{1,9},{2,10},{3,11},{4,12},{5,13},{6,14},{7,15},{8,0},{9,1},... | collective-permute-start | bytes 884744 | tf_op jit(solution)/shard_map/ppermute | solution.py:579
  236.4 9.8 %collective-permute-start.39 = (bf16[2,2,24,1536]{3,2,1,0:T(8,128)(2,1)S(1)}, bf16[2,2,24,1536]{3,2,1,0:T(8,128)(2,1)S(1)}, u32[]{:S(2)}, u32[]{:S(2)}) collective-permute-start(bf16[2,2,24,1536]{3,2,1,0:T(8,128)(2,1)S(1)} %dynamic-slice_bitcast_fusion.7), channel_id=1, source_target_pairs={{0,16},{1,17},{2,18},{3,19},{4,20},{5,21},{6,22},{7,23},{8,24},{9,... | collective-permute-start | bytes 884744 | tf_op jit(solution)/shard_map/ppermute | solution.py:579
  239.3 7.0 %collective-permute-start.31 = (bf16[16,24,768]{2,1,0:T(8,128)(2,1)S(1)}, bf16[16,24,768]{2,1,0:T(8,128)(2,1)S(1)}, u32[]{:S(2)}, u32[]{:S(2)}) collective-permute-start(bf16[16,24,768]{2,1,0:T(8,128)(2,1)S(1)} %get-tuple-element.135), channel_id=1, source_target_pairs={{0,1},{1,0},{2,3},{3,2},{4,5},{5,4},{6,7},{7,6},{8,9},{9,8},{10,11... | collective-permute-start | bytes 1769480 | tf_op jit(solution)/shard_map/ppermute | solution.py:579
  240.3 8.8 %collective-permute-start.43 = (bf16[2,96,768]{2,1,0:T(8,128)(2,1)S(1)}, bf16[2,96,768]{2,1,0:T(8,128)(2,1)S(1)}, u32[]{:S(2)}, u32[]{:S(2)}) collective-permute-start(bf16[2,96,768]{2,1,0:T(8,128)(2,1)S(1)} %dynamic-slice_bitcast_fusion.4), channel_id=1, source_target_pairs={{0,2},{1,3},{2,0},{3,1},{4,6},{5,7},{6,4},{7,5},{8,10},{9,11},{10,... | collective-permute-start | bytes 884744 | tf_op jit(solution)/shard_map/ppermute | solution.py:579
  246.5 30.2 %collective-permute-start.32 = (bf16[2,2,2,24,768]{4,3,1,2,0:T(8,128)(2,1)S(1)}, bf16[2,2,2,24,768]{4,3,1,2,0:T(8,128)(2,1)S(1)}, u32[]{:S(2)}, u32[]{:S(2)}) collective-permute-start(bf16[2,2,2,24,768]{4,3,1,2,0:T(8,128)(2,1)S(1)} %bitcast.236), channel_id=1, source_target_pairs={{0,8},{1,9},{2,10},{3,11},{4,12},{5,13},{6,14},{7,15},{8,0},{9,1},... | collective-permute-start | bytes 884744 | tf_op jit(solution)/shard_map/ppermute | solution.py:579
  249.5 1.6 copy-start.15
  265.1 10.7 %collective-permute-start.44 = (bf16[96,768]{1,0:T(8,128)(2,1)S(1)}, bf16[96,768]{1,0:T(8,128)(2,1)S(1)}, u32[]{:S(2)}, u32[]{:S(2)}) collective-permute-start(bf16[96,768]{1,0:T(8,128)(2,1)S(1)} %dynamic-slice_bitcast_fusion.13), channel_id=1, source_target_pairs={{0,4},{1,5},{2,6},{3,7},{4,0},{5,1},{6,2},{7,3},{8,12},{9,13},{10,... | collective-permute-start | bytes 442376 | tf_op jit(solution)/shard_map/ppermute | solution.py:579
  267.4 12.6 %collective-permute-start.41 = (bf16[2,24,3072]{2,1,0:T(8,128)(2,1)S(1)}, bf16[2,24,3072]{2,1,0:T(8,128)(2,1)S(1)}, u32[]{:S(2)}, u32[]{:S(2)}) collective-permute-start(bf16[2,24,3072]{2,1,0:T(8,128)(2,1)S(1)} %dynamic-slice_bitcast_fusion.5), channel_id=1, source_target_pairs={{0,2},{1,3},{2,0},{3,1},{4,6},{5,7},{6,4},{7,5},{8,10},{9,11},{10,... | collective-permute-start | bytes 884744 | tf_op jit(solution)/shard_map/ppermute | solution.py:579
  271.3 9.4 %collective-permute-start.27 = (bf16[2,2,2,24,768]{4,3,2,1,0:T(8,128)(2,1)S(1)}, bf16[2,2,2,24,768]{4,3,2,1,0:T(8,128)(2,1)S(1)}, u32[]{:S(2)}, u32[]{:S(2)}) collective-permute-start(bf16[2,2,2,24,768]{4,3,2,1,0:T(8,128)(2,1)S(1)} %dynamic-slice_bitcast_fusion.8), channel_id=1, source_target_pairs={{0,16},{1,17},{2,18},{3,19},{4,20},{5,21},{6,22},{7,23},{8,24},{9,... | collective-permute-start | bytes 884744 | tf_op jit(solution)/shard_map/ppermute | solution.py:579
  272.3 9.8 %collective-permute-start.25 = (bf16[2,2,2,24,768]{4,3,2,1,0:T(8,128)(2,1)S(1)}, bf16[2,2,2,24,768]{4,3,2,1,0:T(8,128)(2,1)S(1)}, u32[]{:S(2)}, u32[]{:S(2)}) collective-permute-start(bf16[2,2,2,24,768]{4,3,2,1,0:T(8,128)(2,1)S(1)} %dynamic-slice_bitcast_fusion.9), channel_id=1, source_target_pairs={{0,8},{1,9},{2,10},{3,11},{4,12},{5,13},{6,14},{7,15},{8,0},{9,1},... | collective-permute-start | bytes 884744 | tf_op jit(solution)/shard_map/ppermute | solution.py:579
  275.9 14.3 %collective-permute-start.34 = (bf16[16,24,896]{2,1,0:T(8,128)(2,1)S(1)}, bf16[16,24,896]{2,1,0:T(8,128)(2,1)S(1)}, u32[]{:S(2)}, u32[]{:S(2)}) collective-permute-start(bf16[16,24,896]{2,1,0:T(8,128)(2,1)S(1)} %get-tuple-element.137), channel_id=1, source_target_pairs={{0,1},{1,0},{2,3},{3,2},{4,5},{5,4},{6,7},{7,6},{8,9},{9,8},{10,11... | collective-permute-start | bytes 2064392 | tf_op jit(solution)/shard_map/ppermute | solution.py:579
  276.8 6.3 %collective-permute-start.33 = (bf16[2,2,24,768]{3,2,0,1:T(8,128)(2,1)S(1)}, bf16[2,2,24,768]{3,2,0,1:T(8,128)(2,1)S(1)}, u32[]{:S(2)}, u32[]{:S(2)}) collective-permute-start(bf16[2,2,24,768]{3,2,0,1:T(8,128)(2,1)S(1)} %dynamic-slice_bitcast_fusion.15), channel_id=1, source_target_pairs={{0,16},{1,17},{2,18},{3,19},{4,20},{5,21},{6,22},{7,23},{8,24},{9,... | collective-permute-start | bytes 442376 | tf_op jit(solution)/shard_map/ppermute | solution.py:579
  280.1 9.3 %collective-permute-start.42 = (bf16[24,3072]{1,0:T(8,128)(2,1)S(1)}, bf16[24,3072]{1,0:T(8,128)(2,1)S(1)}, u32[]{:S(2)}, u32[]{:S(2)}) collective-permute-start(bf16[24,3072]{1,0:T(8,128)(2,1)S(1)} %dynamic-slice_bitcast_fusion.14), channel_id=1, source_target_pairs={{0,4},{1,5},{2,6},{3,7},{4,0},{5,1},{6,2},{7,3},{8,12},{9,13},{10,... | collective-permute-start | bytes 442376 | tf_op jit(solution)/shard_map/ppermute | solution.py:579
  280.8 5.2 %collective-permute-start.28 = (bf16[2,2,24,768]{3,2,1,0:T(8,128)(2,1)S(1)}, bf16[2,2,24,768]{3,2,1,0:T(8,128)(2,1)S(1)}, u32[]{:S(2)}, u32[]{:S(2)}) collective-permute-start(bf16[2,2,24,768]{3,2,1,0:T(8,128)(2,1)S(1)} %dynamic-slice_bitcast_fusion.16), channel_id=1, source_target_pairs={{0,8},{1,9},{2,10},{3,11},{4,12},{5,13},{6,14},{7,15},{8,0},{9,1},... | collective-permute-start | bytes 442376 | tf_op jit(solution)/shard_map/ppermute | solution.py:579
  282.2 5.2 %collective-permute-start.26 = (bf16[2,2,24,768]{3,2,1,0:T(8,128)(2,1)S(1)}, bf16[2,2,24,768]{3,2,1,0:T(8,128)(2,1)S(1)}, u32[]{:S(2)}, u32[]{:S(2)}) collective-permute-start(bf16[2,2,24,768]{3,2,1,0:T(8,128)(2,1)S(1)} %dynamic-slice_bitcast_fusion.17), channel_id=1, source_target_pairs={{0,16},{1,17},{2,18},{3,19},{4,20},{5,21},{6,22},{7,23},{8,24},{9,... | collective-permute-start | bytes 442376 | tf_op jit(solution)/shard_map/ppermute | solution.py:579
  287.5 5.2 %collective-permute-start.29 = (bf16[2,24,1536]{2,1,0:T(8,128)(2,1)S(1)}, bf16[2,24,1536]{2,1,0:T(8,128)(2,1)S(1)}, u32[]{:S(2)}, u32[]{:S(2)}) collective-permute-start(bf16[2,24,1536]{2,1,0:T(8,128)(2,1)S(1)} %fusion.26), channel_id=1, source_target_pairs={{0,2},{1,3},{2,0},{3,1},{4,6},{5,7},{6,4},{7,5},{8,10},{9,11},{10,... | collective-permute-start | bytes 442376 | tf_op jit(solution)/shard_map/ppermute | solution.py:579
  290.5 9.2 %collective-permute-start.35 = (bf16[2,2,2,24,896]{4,3,1,2,0:T(8,128)(2,1)S(1)}, bf16[2,2,2,24,896]{4,3,1,2,0:T(8,128)(2,1)S(1)}, u32[]{:S(2)}, u32[]{:S(2)}) collective-permute-start(bf16[2,2,2,24,896]{4,3,1,2,0:T(8,128)(2,1)S(1)} %bitcast.235), channel_id=1, source_target_pairs={{0,16},{1,17},{2,18},{3,19},{4,20},{5,21},{6,22},{7,23},{8,24},{9,... | collective-permute-start | bytes 1032200 | tf_op jit(solution)/shard_map/ppermute | solution.py:579
  299.8 5.5 %collective-permute-start.36 = (bf16[2,2,24,896]{3,2,0,1:T(8,128)(2,1)S(1)}, bf16[2,2,24,896]{3,2,0,1:T(8,128)(2,1)S(1)}, u32[]{:S(2)}, u32[]{:S(2)}) collective-permute-start(bf16[2,2,24,896]{3,2,0,1:T(8,128)(2,1)S(1)} %dynamic-slice_bitcast_fusion.12), channel_id=1, source_target_pairs={{0,8},{1,9},{2,10},{3,11},{4,12},{5,13},{6,14},{7,15},{8,0},{9,1},... | collective-permute-start | bytes 516104 | tf_op jit(solution)/shard_map/ppermute | solution.py:579
  300.2 5.9 %collective-permute-start.30 = (bf16[24,1536]{1,0:T(8,128)(2,1)S(1)}, bf16[24,1536]{1,0:T(8,128)(2,1)S(1)}, u32[]{:S(2)}, u32[]{:S(2)}) collective-permute-start(bf16[24,1536]{1,0:T(8,128)(2,1)S(1)} %dynamic-slice_bitcast_fusion.19), channel_id=1, source_target_pairs={{0,4},{1,5},{2,6},{3,7},{4,0},{5,1},{6,2},{7,3},{8,12},{9,13},{10,... | collective-permute-start | bytes 221192 | tf_op jit(solution)/shard_map/ppermute | solution.py:579
  305.4 5.3 %collective-permute-start.37 = (bf16[2,24,1664]{2,1,0:T(8,128)(2,1)S(1)}, bf16[2,24,1664]{2,1,0:T(8,128)(2,1)S(1)}, u32[]{:S(2)}, u32[]{:S(2)}) collective-permute-start(bf16[2,24,1664]{2,1,0:T(8,128)(2,1)S(1)} %fusion.22), channel_id=1, source_target_pairs={{0,2},{1,3},{2,0},{3,1},{4,6},{5,7},{6,4},{7,5},{8,10},{9,11},{10,... | collective-permute-start | bytes 479240 | tf_op jit(solution)/shard_map/ppermute | solution.py:579
  310.8 5.9 %collective-permute-start.38 = (bf16[24,1664]{1,0:T(8,128)(2,1)S(1)}, bf16[24,1664]{1,0:T(8,128)(2,1)S(1)}, u32[]{:S(2)}, u32[]{:S(2)}) collective-permute-start(bf16[24,1664]{1,0:T(8,128)(2,1)S(1)} %dynamic-slice_bitcast_fusion.18), channel_id=1, source_target_pairs={{0,4},{1,5},{2,6},{3,7},{4,0},{5,1},{6,2},{7,3},{8,12},{9,13},{10,... | collective-permute-start | bytes 239624 | tf_op jit(solution)/shard_map/ppermute | solution.py:579
  (14 other events, 13.6 us)
Sparse Core Ops, SparseCore 0:
  17.0 78.9 all-gather.1

commit v3 on v2

--- a/solution.py
+++ b/solution.py
@@ -18,7 +18,6 @@
 BF, F32 = jnp.bfloat16, jnp.float32
 MIB = 2**20
 SCALE = 1
-UP_AT_ONCE = False
 PLACED = 2**17
 
 
@@ -26,10 +25,17 @@
     return lax.dot_general(a, b, (((ca,), (cb,)), ((), ())), preferred_element_type=F32)
 
 
-def call(kernel, cost, after=(), vmem=40, placed=False, **kw):
+def large(array):
+    return math.prod(array.shape) * jnp.dtype(array.dtype).itemsize >= PLACED
+
+
+def call(kernel, cost, after=(), vmem=40, placed=False, pinned=False, **kw):
     after = tuple(after)
     kw["in_specs"] = list(kw["in_specs"]) + [pl.BlockSpec(memory_space=pl.ANY)] * len(after)
     taken = len(kw["in_specs"]) - len(after)
+
+    if pinned:
+        kw["out_shape"] = [pltpu.HBM(s.shape, s.dtype) if large(s) else s for s in kw["out_shape"]]
 
     def run(*refs):
         kernel(*refs[:taken], *refs[taken + len(after) :])
@@ -41,8 +47,7 @@
         **kw,
     )
     def place(operand):
-        small = operand.size * operand.dtype.itemsize < PLACED
-        return operand if small or not placed else pltpu.with_memory_space_constraint(operand, pltpu.HBM)
+        return operand if not placed or not large(operand) else pltpu.with_memory_space_constraint(operand, pltpu.HBM)
 
     return lambda *operands: made(*map(place, operands), *after)
 
@@ -175,11 +180,11 @@
 
 
 def attend_back_kernel(
-    len_ref, core_ref, tok_t, w, out_w, qkv, ctx, lse_in, att_back, grad_in, *refs, extra, carry, n_dw, bq, cases, nseq, chunk=2
+    len_ref, core_ref, tok_t, out_w, qkv, ctx, lse_in, att_back, *refs, extra, carry, n_dw, bq, cases, nseq, chunk=2
 ):
     extras, carried, refs = refs[:extra], refs[extra : extra + carry], refs[extra + carry :]
-    dw, (grad_out, sums) = refs[:n_dw], refs[n_dw : n_dw + 2]
-    seg_col, seg_row, key_t, do, dqkv, dk_sum, dv_sum, p_s, ds_s = refs[n_dw + 2 :]
+    dw, (dqkv, sums) = refs[:n_dw], refs[n_dw : n_dw + 2]
+    seg_col, seg_row, key_t, do, dk_sum, dv_sum, p_s, ds_s = refs[n_dw + 2 :]
     width, total = tok_t.shape
     ends = seq_ends(len_ref, nseq)
     fill_segments(ends, seg_col, seg_row)
@@ -233,7 +238,6 @@
     bias_sums = jnp.sum(d.astype(F32), axis=0, keepdims=True)
     sums[...] = jnp.broadcast_to(bias_sums, sums.shape)
     put_shares(dot(tok_t[...], d), core_ref[0, 0], dw, pl.ds(0, 3 * GROUP))
-    grad_out[...] = grad_in[...] + dot(d, w[...], 1, 1)
     for source, target in zip(carried, dw):
         target[..., pl.ds(3 * GROUP, width)] = source[...]
     if extra:
@@ -249,7 +253,7 @@
 
 
 def attend_back(
-    lens, core, tok_t, packed, out_up, group, qkv, ctx, lse, att_back, grad_in, n, extras=(), carried=(), after=(), bq=256,
+    lens, core, tok_t, out_up, group, qkv, ctx, lse, att_back, n, extras=(), carried=(), after=(), bq=256,
     cases=(2, 3, 4, 5, 6),
 ):
     width, total = tok_t.shape
@@ -261,19 +265,19 @@
         ),
         15,
         after,
+        pinned=True,
         grid=(1,),
         in_specs=[
             smem,
             smem,
             vmem,
-            pl.BlockSpec((width, 3 * GROUP), lambda _: (0, group)),
             pl.BlockSpec((GROUP, width), lambda _: (group, 0)),
         ]
-        + [vmem] * (5 + len(extras) + len(carried)),
+        + [vmem] * (4 + len(extras) + len(carried)),
         out_specs=[vmem] * (len(dw) + 2),
         out_shape=[
             *dw,
-            jax.ShapeDtypeStruct((total, width), F32),
+            jax.ShapeDtypeStruct((total, 3 * GROUP), BF),
             jax.ShapeDtypeStruct((8, 3 * GROUP), F32),
         ],
         scratch_shapes=[
@@ -281,14 +285,36 @@
             pltpu.VMEM((8, total), jnp.int32),
             pltpu.VMEM((GROUP, total), BF),
             pltpu.VMEM((total, GROUP), BF),
-            pltpu.VMEM((total, 3 * GROUP), BF),
             pltpu.VMEM((total, GROUP), F32),
             pltpu.VMEM((total, GROUP), F32),
             pltpu.VMEM((total, 2 * bq), BF),
             pltpu.VMEM((total, 2 * bq), BF),
         ],
         name="attend_back",
-    )(lens, core, tok_t, packed, out_up, qkv, ctx, lse, att_back, grad_in, *extras, *carried)
+    )(lens, core, tok_t, out_up, qkv, ctx, lse, att_back, *extras, *carried)
+
+
+def tokens_back_kernel(grad_in, w, *refs):
+    *ds, grad = refs
+    d = jnp.concatenate([r[...] for r in ds], 1)
+    grad[...] = grad_in[...] + dot(d, w[:, : d.shape[1]], 1, 1)
+
+
+def tokens_back(grad, packed, ds, after=(), rows=256):
+    total, width = grad.shape
+    at = lambda i: (i, 0)
+    return call(
+        tokens_back_kernel,
+        8,
+        after,
+        placed=True,
+        grid=(total // rows,),
+        in_specs=[pl.BlockSpec((rows, width), at), pl.BlockSpec(packed.shape, lambda i: (0, 0))]
+        + [pl.BlockSpec((rows, 3 * GROUP), at)] * len(ds),
+        out_specs=pl.BlockSpec((rows, width), at),
+        out_shape=jax.ShapeDtypeStruct((total, width), F32),
+        name="tokens_back",
+    )(grad, packed, *ds)
 
 
 def row_mean(value):
@@ -347,15 +373,20 @@
     return [pl.BlockSpec((p.shape[0] // parts, *p.shape[1:]), lambda j: (at(j), 0, 0)) for p in pieces]
 
 
-def forward_kernel(core_ref, ctx0, ctx1, ctx2, tok, out_w, up, bias, vecs, out_grad, *refs, rows, parts, n_down, n_dw):
+def forward_kernel(core_ref, ctx0, ctx1, ctx2, tok, out_w, up, bias, vecs, out_grad_far, *refs, rows, parts, n_down, n_dw):
     pieces, dw, refs = refs[:n_down], refs[n_down : n_down + n_dw], refs[n_down + n_dw :]
-    output, normed, inverse, low, slope, second, back_low, sums, act, total, down = refs
+    far, (slope, sums, act, total, down), near, (out_grad, sems) = refs[:6], refs[6:11], refs[11:17], refs[17:]
+    normed, inverse, low, output, second, back_low = near
+    bring = pltpu.make_async_copy(out_grad_far, out_grad, sems.at[6])
+    take = [pltpu.make_async_copy(near[i], far[i], sems.at[i]) for i in range(6)]
     j = pl.program_id(0)
     width = tok.shape[1]
     blocks = tok.shape[0] // rows
 
     @pl.when(j == 0)
     def _():
+        bring.start()
+
         @pl.loop(0, blocks)
         def _(i):
             at = pl.ds(pl.multiple_of(i * rows, rows), rows)
@@ -367,6 +398,9 @@
             low[at, :] = middle.astype(BF)
             total[at, :] = middle + vecs[5:6, :]
 
+        for copy in take[:3]:
+            copy.start()
+
     @pl.when(j < parts)
     def _():
         x = dot(low[...], up[...]) + bias[...]
@@ -380,6 +414,8 @@
 
     @pl.when(j == parts - 1)
     def _():
+        bring.wait()
+
         @pl.loop(0, blocks)
         def _(i):
             at = pl.ds(pl.multiple_of(i * rows, rows), rows)
@@ -392,9 +428,17 @@
             back_low[at, :] = rounded
             add_rows(sums, i == 0, (upstream * n, upstream, rounded.astype(F32)))
 
+        for copy in take[3:]:
+            copy.start()
+
     @pl.when(j >= parts)
     def _():
         put_shares(dot(act[j - parts], back_low[...], 0, 0), core_ref[0, 0], dw)
+
+    @pl.when(j == 2 * parts - 1)
+    def _():
+        for copy in take:
+            copy.wait()
 
 
 def forward(core, ctxs, tok, out_up, up_bias, down, vecs, out_grad, n, rows=256):
@@ -405,11 +449,15 @@
     first = lambda j: jnp.minimum(j, parts - 1)
     last = lambda j: jnp.maximum(j - parts, 0)
     dw = shares(hidden, width, n)
+    hbm = pl.BlockSpec(memory_space=pl.ANY)
+    wide = (total, width)
+    kept = [(wide, F32), ((total, 128), F32), (wide, BF), (wide, BF), (wide, F32), (wide, BF)]
     return call(
         functools.partial(forward_kernel, rows=rows, parts=parts, n_down=len(down), n_dw=len(dw)),
         32,
         vmem=48,
         placed=True,
+        pinned=True,
         grid=(2 * parts,),
         in_specs=[pl.BlockSpec(memory_space=pltpu.SMEM)]
         + [vmem] * 4
@@ -418,43 +466,48 @@
             pl.BlockSpec((width, width), lambda j: (0, first(j) + 1)),
             pl.BlockSpec((1, width), lambda j: (0, first(j))),
             vmem,
-            vmem,
+            hbm,
             *down_specs(down, parts, first),
         ],
         out_specs=down_specs(dw, parts, last)
-        + [vmem] * 4
-        + [pl.BlockSpec((total, width), lambda j: (0, first(j))), vmem, vmem, vmem],
+        + [hbm] * len(kept)
+        + [pl.BlockSpec((total, width), lambda j: (0, first(j))), vmem],
         out_shape=[
             *dw,
-            jax.ShapeDtypeStruct((total, width), BF),
-            jax.ShapeDtypeStruct((total, width), F32),
-            jax.ShapeDtypeStruct((total, 128), F32),
-            jax.ShapeDtypeStruct((total, width), BF),
+            *(jax.ShapeDtypeStruct(*k) for k in kept),
             jax.ShapeDtypeStruct((total, hidden), BF),
-            jax.ShapeDtypeStruct((total, width), F32),
-            jax.ShapeDtypeStruct((total, width), BF),
             jax.ShapeDtypeStruct((8, width), F32),
         ],
         scratch_shapes=[
             pltpu.VMEM((parts, total, width), BF),
             pltpu.VMEM((total, width), F32),
             pltpu.VMEM((width, width), BF),
+            *(pltpu.VMEM(*k) for k in kept),
+            pltpu.VMEM((total, width), BF),
+            pltpu.SemaphoreType.DMA((7,)),
         ],
         name="forward",
     )(core, *ctxs, tok, out_up, out_up, up_bias, vecs, out_grad, *down)
 
 
 def backward_kernel(
-    core_ref, back_low, slope, low, up, second, normed, inverse, ctx0, ctx1, ctx2, vecs, *refs, rows, n_dw, n_down
+    core_ref, back_low, slope, low, up, vecs, *refs, rows, n_dw, n_down
 ):
-    pieces, refs = refs[:n_down], refs[n_down:]
+    far, pieces, refs = refs[:6], refs[6 : 6 + n_down], refs[6 + n_down :]
     dw, out_dw, refs = refs[: n_dw[0]], refs[n_dw[0] : sum(n_dw)], refs[sum(n_dw) :]
-    up_sums, entry_grad, att_back, sums, low_t, back, ex, down = refs
+    (up_sums, sums), out_far, (low_t, back, ex, down), near, (entry_grad, att_back, sems) = (
+        refs[:2], refs[2:4], refs[4:8], refs[8:14], refs[14:]
+    )
+    second, normed, inverse, ctx0, ctx1, ctx2 = near
+    bring = [pltpu.make_async_copy(far[i], near[i], sems.at[i]) for i in range(6)]
+    take = [pltpu.make_async_copy(a, b, sems.at[6 + i]) for i, (a, b) in enumerate(zip((entry_grad, att_back), out_far))]
     j = pl.program_id(0)
     blocks = low.shape[0] // rows
 
     @pl.when(j == 0)
     def _():
+        for copy in bring:
+            copy.start()
         low_t[...] = low[...].T
         back[...] = jnp.zeros_like(back)
 
@@ -466,6 +519,9 @@
 
     @pl.when(j == pl.num_programs(0) - 1)
     def _():
+        for copy in bring:
+            copy.wait()
+
         @pl.loop(0, blocks)
         def _(i):
             at = pl.ds(pl.multiple_of(i * rows, rows), rows)
@@ -477,16 +533,20 @@
             att_back[at, :] = rounded
             add_rows(sums, i == 0, (upstream * n, upstream, rounded.astype(F32)))
 
+        for copy in take:
+            copy.start()
         ctx = jnp.concatenate([ctx0[...], ctx1[...], ctx2[...]], 1)
         put_shares(dot(ctx, att_back[...], 0, 0), core_ref[0, 0], out_dw)
+        for copy in take:
+            copy.wait()
 
 
 def backward(core, back_low, down, slope, low, out_up, second, normed, inverse, ctxs, vecs, n, after=(), rows=256):
     total, width = low.shape
     hidden = slope.shape[1]
     vmem = pl.BlockSpec(memory_space=pltpu.VMEM)
-    dw = [jax.ShapeDtypeStruct((width, hidden), BF)] if UP_AT_ONCE else shares(width, hidden, n)
-    out_dw = shares(width, width, n)
+    dw, out_dw = shares(width, hidden, n), shares(width, width, n)
+    hbm = pl.BlockSpec(memory_space=pl.ANY)
     lead = (0,) * (len(dw[0].shape) - 1)
     return call(
         functools.partial(backward_kernel, rows=rows, n_dw=(len(dw), len(out_dw)), n_down=len(down)),
@@ -494,6 +554,7 @@
         after,
         vmem=44,
         placed=True,
+        pinned=True,
         grid=(hidden // width,),
         in_specs=[
             pl.BlockSpec(memory_space=pltpu.SMEM),
@@ -501,29 +562,36 @@
             pl.BlockSpec((total, width), lambda j: (0, j)),
             vmem,
             pl.BlockSpec((width, width), lambda j: (0, j + 1)),
+            vmem,
         ]
-        + [vmem] * 7
+        + [hbm] * 6
         + down_specs(down, hidden // width, lambda j: j),
         out_specs=[pl.BlockSpec((*d.shape[:-1], width), lambda j: (*lead, j)) for d in dw]
         + [vmem] * len(out_dw)
-        + [pl.BlockSpec((8, width), lambda j: (0, j))]
-        + [vmem] * 3,
+        + [pl.BlockSpec((8, width), lambda j: (0, j)), vmem, hbm, hbm],
         out_shape=[
             *dw,
             *out_dw,
             jax.ShapeDtypeStruct((8, hidden), F32),
+            jax.ShapeDtypeStruct((8, width), F32),
             jax.ShapeDtypeStruct((total, width), F32),
             jax.ShapeDtypeStruct((total, width), BF),
-            jax.ShapeDtypeStruct((8, width), F32),
         ],
         scratch_shapes=[
             pltpu.VMEM((width, total), BF),
             pltpu.VMEM((total, width), F32),
             pltpu.VMEM((total, width), BF),
             pltpu.VMEM((width, width), BF),
+            pltpu.VMEM((total, width), F32),
+            pltpu.VMEM((total, width), F32),
+            pltpu.VMEM((total, 128), F32),
+            *[pltpu.VMEM((total, GROUP), BF)] * 3,
+            pltpu.VMEM((total, width), F32),
+            pltpu.VMEM((total, width), BF),
+            pltpu.SemaphoreType.DMA((8,)),
         ],
         name="backward",
-    )(core, back_low, slope, low, out_up, second, normed, inverse, *ctxs, vecs, *down)
+    )(core, back_low, slope, low, out_up, vecs, second, normed, inverse, *ctxs, *down)
 
 
 def pack_kernel(query, key, value, table, packed):
@@ -682,6 +750,7 @@
     for step in range(steps_near):
         piece, done = cube.gather_near(piece, step, done)
     parts = cube.halve(piece)
+    tok_t = tie(tokens, piece).T
     for step in range(max(steps_far, steps_near)):
         if step < steps_near:
             down_piece = tie(down_piece, *parts)
@@ -692,7 +761,6 @@
     packed = cube.gather_core(parts, [cube.swap(p, 0) for p in parts])
     vecs = turn(packed, 3 * GROUP * groups)
     up_b = vecs[8 : 8 + each].reshape(each, n, own).transpose(1, 0, 2).reshape(1, hidden)
-    tok_t = tokens.T
 
     down_parts = [tie(p, packed) for p in cube.halve(down_piece)]
     made, wait = [], [tok_t, up_b]
@@ -710,43 +778,47 @@
         down = [cube.gather_core(down_parts, down_others)]
     else:
         down = [p.reshape(-1, *p.shape[-2:]) for p in (*down_parts, *down_others)]
-    *down_dw, output, normed, inverse, low, slope, second, back_low, sums_two = forward(
+    *down_dw, normed, inverse, low, output, second, back_low, slope, sums_two = forward(
         core, ctxs, tokens, out_up, up_b, down, vecs, out_grad, n
     )
-    flows = [Flow(cube, cube.halve(cube.scatter_core(down_dw)))]
-
-    *dws, up_sums, grad, att_back, sums_one = backward(
+    down_flow = Flow(cube, cube.halve(cube.scatter_core(down_dw)))
+
+    *dws, up_sums, sums_one, grad, att_back = backward(
         core, back_low, down, slope, low, out_up, second, normed, inverse, ctxs, vecs, n
     )
-    half = 1 if UP_AT_ONCE else len(dws) // 2
+    half = len(dws) // 2
     out_dw = dws[half:]
-    wait = flows[0].parts
-    flows[0].step(sums_one)
-    if UP_AT_ONCE:
-        own_up = lax.psum_scatter(dws[0], AXES, scatter_dimension=0, tiled=True).astype(F32)
-    else:
-        flows.append(Flow(cube, cube.halve(cube.scatter_core(dws[:half]))))
     up_sums = up_sums[0].reshape(width, each).T
-    later, sums_qkv = [], []
+    wait = down_flow.parts
+    down_flow.step(sums_one)
+    flows = [down_flow, Flow(cube, cube.halve(cube.scatter_core(dws[:half])))]
+    later, sums_qkv, ds = [], [], []
     for g in range(groups):
         qkv, ctx, lse = made[g]
         extras = (*sums_qkv, sums_one, sums_two, up_sums) if g == groups - 1 else ()
-        *dw, grad, sums = attend_back(
-            seq_lengths, core, tok_t, packed, out_up, g, qkv, ctx, lse, att_back, grad, n, extras, out_dw if g == 0 else (),
-            wait,
+        *dw, d, sums = attend_back(
+            seq_lengths, core, tok_t, out_up, g, qkv, ctx, lse, att_back, n, extras, out_dw if g == 0 else (), wait
         )
+        ds.append(d)
         sums_qkv.append(sums)
         wait = [p for flow in flows for p in flow.parts]
-        for flow in flows:
-            flow.step(sums)
+        if g < groups - 1:
+            for flow in flows:
+                flow.step(sums)
+        if g == groups - 1:
+            dw = [tie(p, *(p for flow in flows for p in flow.parts)) for p in dw]
         if g == 0:
-            flows.append(Flow(cube, cube.halve(cube.scatter_core(dw))))
+            flows.append(Flow(cube, [cube.scatter_core(dw)]))
         else:
             later.append(cube.scatter_core(dw))
-    own_down, *own_up_too, first = [flow.finish() for flow in flows]
-    if own_up_too:
-        (own_up,) = own_up_too
-    both = Flow(cube, later).finish()
+    both = Flow(cube, later)
+    grad = tokens_back(grad, packed, ds, later[-1:])
+    while both.todo or any(flow.todo for flow in flows):
+        before = [p for flow in (both, *flows) for p in flow.parts]
+        for flow in (both, *flows):
+            flow.step(*before)
+    own_down, own_up, first = [flow.parts[0] for flow in flows]
+    both = both.parts[0]
     owned = [first]
     owned += [both[:, g * 3 * GROUP : (g + 1) * 3 * GROUP + (128 if g == groups - 2 else 0)] for g in range(groups - 1)]
     own_out = owned[0][:, 3 * GROUP :]

time: 331 us -> 308 us (0.931)
  local copies, waits for them, and re-layouts: 31.3 us -> 18.8 us
  waiting for transfers between devices: 74.6 us -> 64 us
    unnamed x67 -> x63, local copies, waits for them, and re-layouts: 18.5 us -> 7.25 us
    ppermute x45 -> x43, waiting for transfers between devices: 74.5 us -> 64 us  [swap(): return lax.ppermute(value, AXES, [(i, i ^ 1 << bit) for i in range(self.n)])]
    ppermute x45 -> x43, starting transfers between devices: 56.1 us -> 55 us  [swap(): return lax.ppermute(value, AXES, [(i, i ^ 1 << bit) for i in range(self.n)])]
    pallas_call x10 -> x11, Pallas kernels: 128 us -> 127 us  [call(): return lambda *operands: made(*map(place, operands), *after)]
    another operation x25 -> x26, other arithmetic: 8.63 us -> 8.58 us  [join(): jnp.stack([jnp.where(last, other, mine), jnp.where(last, mine, other)], at)]
  transfers between devices with their start and end apart: 46 -> 44, of which waited for: 22 -> 16; matrix products, arithmetic and copies ran while one was open for 9% -> 10% of each run, Pallas kernels for 28% -> 31%
where the time goes in v3:
time: 308 us; the launch traced here: 305 us
  Pallas kernels  127 us (41%)
  waiting for transfers between devices  64 us (21%)
  starting transfers between devices  55 us (18%)
  other arithmetic  24.3 us (8%)
  local copies, waits for them, and re-layouts  18.8 us (6%)
  between operations  15.5 us (5%)
    pallas_call x11, Pallas kernels, call(): return lambda *operands: made(*map(place, operands), *after)  127 us
    ppermute x43, waiting for transfers between devices, swap(): return lax.ppermute(value, AXES, [(i, i ^ 1 << bit) for i in range(self.n)])  64 us
    ppermute x43, starting transfers between devices, swap(): return lax.ppermute(value, AXES, [(i, i ^ 1 << bit) for i in range(self.n)])  55 us
    another operation x26, other arithmetic, join(): jnp.stack([jnp.where(last, other, mine), jnp.where(last, mine, other)], at)  8.58 us
    convert_element_type x5, other arithmetic, scatter_core(): part = (keep.astype(F32) + self.swap(give, 0).astype(F32)).astype(BF)  8.43 us
    unnamed x63, local copies, waits for them, and re-layouts  7.25 us
  transfers between devices with their start and end apart: 44, of which 16 were waited for; matrix products, arithmetic and copies ran while one was open for 10% of the time, Pallas kernels for 31%

profile of v3, /device:TPU:0, one launch (start us, length us, event | category | flops | bytes accessed | tf_op | source)
XLA Modules:
  0.0 304.8 jit_solution(17599634805127087322)
XLA Ops:
  11.2 4.1 %collective-permute-start = (bf16[24,2432]{1,0:T(8,128)(2,1)S(1)}, bf16[24,2432]{1,0:T(8,128)(2,1)S(1)}, u32[]{:S(2)}, u32[]{:S(2)}) collective-permute-start(bf16[24,2432]{1,0:T(8,128)(2,1)S(1)} %pack.1), channel_id=1, source_target_pairs={{0,4},{1,5},{2,6},{3,7},{4,0},{5,1},{6,2},{7,3},{8,12},{9,13},{10,... | collective-permute-start | bytes 350216 | tf_op jit(solution)/shard_map/ppermute | solution.py:647
  15.2 1.6 pad_maximum_fusion.12
  16.9 4.1 %collective-permute-done = bf16[24,2432]{1,0:T(8,128)(2,1)S(1)} collective-permute-done((bf16[24,2432]{1,0:T(8,128)(2,1)S(1)}, bf16[24,2432]{1,0:T(8,128)(2,1)S(1)}, u32[]{:S(2)}, u32[]{:S(2)}) %collective-permute-start) | collective-permute-done | bytes 116768 | tf_op jit(solution)/shard_map/ppermute | solution.py:647
  21.8 6.4 %collective-permute-done.1 = bf16[2,24,2432]{2,1,0:T(8,128)(2,1)S(1)} collective-permute-done((bf16[2,24,2432]{2,1,0:T(8,128)(2,1)S(1)}, bf16[2,24,2432]{2,1,0:T(8,128)(2,1)S(1)}, u32[]{:S(2)}, u32[]{:S(2)}) %collective-permute-start.1) | collective-permute-done | bytes 233504 | tf_op jit(solution)/shard_map/ppermute | solution.py:647
  28.4 4.2 %collective-permute-start.8 = (bf16[96,768]{1,0:T(8,128)(2,1)S(1)}, bf16[96,768]{1,0:T(8,128)(2,1)S(1)}, u32[]{:S(2)}, u32[]{:S(2)}) collective-permute-start(bf16[96,768]{1,0:T(8,128)(2,1)S(1)} %copy-done.27), channel_id=1, source_target_pairs={{0,4},{1,5},{2,6},{3,7},{4,0},{5,1},{6,2},{7,3},{8,12},{9,13},{10,... | collective-permute-start | bytes 442376 | tf_op jit(solution)/shard_map/ppermute | solution.py:647
  32.6 1.5 collective-permute-start.2
  34.1 1.5 collective-permute-start.5
  35.6 5.3 %collective-permute-done.8 = bf16[96,768]{1,0:T(8,128)(2,1)S(1)} collective-permute-done((bf16[96,768]{1,0:T(8,128)(2,1)S(1)}, bf16[96,768]{1,0:T(8,128)(2,1)S(1)}, u32[]{:S(2)}, u32[]{:S(2)}) %collective-permute-start.8) | collective-permute-done | bytes 147488 | tf_op jit(solution)/shard_map/ppermute | solution.py:647
  41.1 1.6 collective-permute-start.3
  42.8 1.6 collective-permute-start.6
  44.4 13.3 %collective-permute-done.3 = bf16[2,2,2,24,1152]{4,3,1,2,0:T(8,128)(2,1)S(1)} collective-permute-done((bf16[2,2,2,24,1152]{4,3,1,2,0:T(8,128)(2,1)S(1)}, bf16[2,2,2,24,1152]{4,3,1,2,0:T(8,128)(2,1)S(1)}, u32[]{:S(2)}, u32[]{:S(2)}) %collective-permute-start.3) | collective-permute-done | bytes 442400 | tf_op jit(solution)/shard_map/ppermute | solution.py:647
  57.8 1.0 pad_maximum_fusion.3
  60.5 1.1 collective-permute-done.4
  61.6 1.4 select_bitcast_fusion.3
  62.9 1.3 select_bitcast_fusion.1
  64.8 2.1 copy.49
  66.9 1.6 collective-permute-start.10
  68.5 1.7 collective-permute-start.11
  71.0 2.1 copy-done
  73.7 2.1 copy-done.1
  75.8 7.5 %attend.3 = (bf16[1024,768]{1,0:T(8,128)(2,1)S(1)}, bf16[1024,256]{1,0:T(8,128)(2,1)S(1)}, f32[8,1024]{1,0:T(8,128)S(1)}) custom-call(s32[1,9]{1,0:T(1,128)S(1)} %copy-done.22, bf16[1024,768]{1,0:T(8,128)(2,1)S(1)} %copy-done.2, bf16[768,2432]{1,0:T(8,128)(2,1)S(1)} %bitcast.196, f32[16,768]{1,0:T(8,128)S(1)} %turn.1.refs_3_.refs_8_.refs_5_, ...), custom_call_target="tpu_custom_call" | custom-call | flops 9000000 | tf_op jit(solution)/shard_map/attend/pallas_call | solution.py:52
  83.3 1.5 select_bitcast_fusion.15
  84.9 1.1 select_bitcast_fusion.13
  86.2 1.5 collective-permute-start.13
  87.7 1.3 collective-permute-start.12
  89.1 7.8 %attend.4 = (bf16[1024,768]{1,0:T(8,128)(2,1)S(1)}, bf16[1024,256]{1,0:T(8,128)(2,1)S(1)}, f32[8,1024]{1,0:T(8,128)S(1)}) custom-call(s32[1,9]{1,0:T(1,128)S(1)} %copy-done.22, bf16[1024,768]{1,0:T(8,128)(2,1)S(1)} %copy-done.2, bf16[768,2432]{1,0:T(8,128)(2,1)S(1)} %bitcast.197, f32[16,768]{1,0:T(8,128)S(1)} %turn.1.refs_3_.refs_8_.refs_5_, ...), custom_call_target="tpu_custom_call" | custom-call | flops 9000000 | tf_op jit(solution)/shard_map/attend/pallas_call | solution.py:52
  96.9 5.3 %collective-permute-done.13 = bf16[2,2,2,96,384]{4,3,2,1,0:T(8,128)(2,1)S(1)} collective-permute-done((bf16[2,2,2,96,384]{4,3,2,1,0:T(8,128)(2,1)S(1)}, bf16[2,2,2,96,384]{4,3,2,1,0:T(8,128)(2,1)S(1)}, u32[]{:S(2)}, u32[]{:S(2)}) %collective-permute-start.13) | collective-permute-done | bytes 589856 | tf_op jit(solution)/shard_map/ppermute | solution.py:647
  103.8 1.2 copy.54
  104.9 7.3 %attend.5 = (bf16[1024,768]{1,0:T(8,128)(2,1)S(1)}, bf16[1024,256]{1,0:T(8,128)(2,1)S(1)}, f32[8,1024]{1,0:T(8,128)S(1)}) custom-call(s32[1,9]{1,0:T(1,128)S(1)} %copy-done.22, bf16[1024,768]{1,0:T(8,128)(2,1)S(1)} %copy-done.2, bf16[768,2432]{1,0:T(8,128)(2,1)S(1)} %bitcast.198, f32[16,768]{1,0:T(8,128)S(1)} %turn.1.refs_3_.refs_8_.refs_5_, ...), custom_call_target="tpu_custom_call" | custom-call | flops 9000000 | tf_op jit(solution)/shard_map/attend/pallas_call | solution.py:52
  112.3 1.3 copy.55
  114.0 32.7 %forward.1 = (bf16[16,96,768]{2,1,0:T(8,128)(2,1)}, bf16[16,96,768]{2,1,0:T(8,128)(2,1)}, f32[1024,768]{1,0:T(8,128)}, f32[1024,128]{1,0:T(8,128)}, bf16[1024,76...) custom-call(s32[1,1]{1,0:T(1,128)} %bitcast.refs_0_.refs_1_, ...), custom_call_target="tpu_custom_call" | custom-call | flops 32000000 | tf_op jit(solution)/shard_map/forward/pallas_call | solution.py:52
  146.7 1.8 collective-permute-start.16
  148.5 26.4 %backward.1 = (bf16[16,24,3072]{2,1,0:T(8,128)(2,1)}, bf16[16,24,3072]{2,1,0:T(8,128)(2,1)}, bf16[16,24,768]{2,1,0:T(8,128)(2,1)}, bf16[16,24,768]{2,1,0:T(8,128...) custom-call(s32[1,1]{1,0:T(1,128)} %bitcast.refs_0_.refs_1_, ...), custom_call_target="tpu_custom_call" | custom-call | flops 26000000 | tf_op jit(solution)/shard_map/backward/pallas_call | solution.py:52
  175.6 3.1 %add_convert_fusion.1 = bf16[16,96,768]{2,1,0:T(8,128)(2,1)S(1)} fusion(bf16[16,96,768]{2,1,0:T(8,128)(2,1)} %collective-permute-done.16, bf16[16,96,768]{2,1,0:T(8,128)(2,1)} %get-tuple-element.117), kind=kLoop, calls=%fused_computation.1 | loop fusion | flops 4718592 | bytes 7077888 | tf_op jit(solution)/shard_map/convert_element_type | solution.py:689
  179.4 1.7 collective-permute-start.18
  181.9 12.5 %attend_back.3 = (bf16[16,24,1536]{2,1,0:T(8,128)(2,1)}, bf16[16,24,1536]{2,1,0:T(8,128)(2,1)}, bf16[1024,768]{1,0:T(8,128)(2,1)}, f32[8,768]{1,0:T(8,128)S(1)}) custom-call(s32[1,9]{1,0:T(1,128)S(1)} %copy-done.22, s32[1,1]{1,0:T(1,128)} %bitcast.refs_0_.refs_1_, bf16[768,1024]{1,0:T(8,128)(2,1)S(1)} %bitcast.200, ...), custom_call_target="tpu_custom_call" | custom-call | flops 15000000 | tf_op jit(solution)/shard_map/attend_back/pallas_call | solution.py:52
  194.5 1.9 collective-permute-start.24
  196.4 2.5 add_convert_fusion
  199.4 1.3 collective-permute-start.22
  201.8 1.2 collective-permute-start.21
  203.0 1.1 collective-permute-start.20
  204.2 12.0 %attend_back.4 = (bf16[16,24,768]{2,1,0:T(8,128)(2,1)}, bf16[16,24,768]{2,1,0:T(8,128)(2,1)}, bf16[1024,768]{1,0:T(8,128)(2,1)}, f32[8,768]{1,0:T(8,128)S(1)}) custom-call(s32[1,9]{1,0:T(1,128)S(1)} %copy-done.22, s32[1,1]{1,0:T(1,128)} %bitcast.refs_0_.refs_1_, bf16[768,1024]{1,0:T(8,128)(2,1)S(1)} %bitcast.201, ...), custom_call_target="tpu_custom_call" | custom-call | flops 15000000 | tf_op jit(solution)/shard_map/attend_back/pallas_call | solution.py:52
  216.4 2.9 collective-permute-start.26
  219.5 1.2 collective-permute-start.27
  220.7 2.6 collective-permute-done.20
  224.1 4.8 %collective-permute-done.26 = bf16[2,2,24,1536]{3,2,1,0:T(8,128)(2,1)S(1)} collective-permute-done((bf16[2,2,24,1536]{3,2,1,0:T(8,128)(2,1)S(1)}, bf16[2,2,24,1536]{3,2,1,0:T(8,128)(2,1)S(1)}, u32[]{:S(2)}, u32[]{:S(2)}) %collective-permute-start.26) | collective-permute-done | bytes 294944 | tf_op jit(solution)/shard_map/ppermute | solution.py:647
  229.8 3.3 %collective-permute-done.25 = bf16[2,96,768]{2,1,0:T(8,128)(2,1)S(1)} collective-permute-done((bf16[2,96,768]{2,1,0:T(8,128)(2,1)S(1)}, bf16[2,96,768]{2,1,0:T(8,128)(2,1)S(1)}, u32[]{:S(2)}, u32[]{:S(2)}) %collective-permute-start.25) | collective-permute-done | bytes 294944 | tf_op jit(solution)/shard_map/ppermute | solution.py:647
  233.3 11.9 %attend_back.5 = (bf16[16,24,896]{2,1,0:T(8,128)(2,1)}, bf16[16,24,896]{2,1,0:T(8,128)(2,1)}, bf16[1024,768]{1,0:T(8,128)(2,1)}, f32[8,768]{1,0:T(8,128)}) custom-call(s32[1,9]{1,0:T(1,128)S(1)} %copy-done.22, s32[1,1]{1,0:T(1,128)} %bitcast.refs_0_.refs_1_, bf16[768,1024]{1,0:T(8,128)(2,1)S(1)} %bitcast.202, bf16[768,3840]{1,0:T(8,128)(2,1)S(1)} %bitcast.193, ...), custom_call_target="tpu_custom_call" | custom-call | flops 15000000 | tf_op jit(solution)/shard_map/attend_back/pallas_call | solution.py:52
  245.3 1.8 collective-permute-start.29
  247.2 1.2 add_convert_fusion.4
  249.3 1.3 add_convert_fusion.3
  250.6 2.6 collective-permute-start.34
  253.2 1.0 collective-permute-start.32
  254.3 1.1 collective-permute-start.31
  255.5 2.3 collective-permute-start.35
  257.9 9.0 %tokens_back.1 = f32[1024,768]{1,0:T(8,128)} custom-call(f32[1024,768]{1,0:T(8,128)} %get-tuple-element.112.refs_0_, bf16[768,2432]{1,0:T(8,128)(2,1)} %bitcast.194, bf16[1024,768]{1,0:T(8,128)(2,1)} %get-tuple-element.119.refs_2_, bf16[1024,768]{1,0:T(8,128)(2,1)} %get-tuple-element.126.refs_3_, bf16[1024,768]{1,0:T(8,128)(2,1)} %get-tuple-element.139.refs_4_, ...), custom_call_target="tpu_custom_call" | custom-call | flops 8000000 | tf_op jit(solution)/shard_map/tokens_back/pallas_call | solution.py:52
  267.9 2.2 collective-permute-done.33
  271.1 1.3 collective-permute-start.36
  272.4 1.7 collective-permute-start.37
  274.6 4.3 %collective-permute-done.39 = bf16[24,3072]{1,0:T(8,128)(2,1)S(1)} collective-permute-done((bf16[24,3072]{1,0:T(8,128)(2,1)S(1)}, bf16[24,3072]{1,0:T(8,128)(2,1)S(1)}, u32[]{:S(2)}, u32[]{:S(2)}) %collective-permute-start.39) | collective-permute-done | bytes 147488 | tf_op jit(solution)/shard_map/ppermute | solution.py:647
  279.8 2.6 collective-permute-start.40
  282.9 2.9 collective-permute-done.40
  285.9 1.9 collective-permute-done.41
  289.0 5.1 %collective-permute-done.42 = bf16[24,1664]{1,0:T(8,128)(2,1)S(1)} collective-permute-done((bf16[24,1664]{1,0:T(8,128)(2,1)S(1)}, bf16[24,1664]{1,0:T(8,128)(2,1)S(1)}, u32[]{:S(2)}, u32[]{:S(2)}) %collective-permute-start.42) | collective-permute-done | bytes 79904 | tf_op jit(solution)/shard_map/ppermute | solution.py:647
  (208 shorter events, 26.4 us)
Async XLA Ops:
  7.2 106.8 %all-gather.2.cloned.1.call-start = ((), (), s32[]{:S(2)}) async-start(), calls=%async_computation | async-start | bytes 6082560 | tf_op jit(solution)/shard_map/all_gather | solution.py:747
  11.2 9.8 %collective-permute-start = (bf16[24,2432]{1,0:T(8,128)(2,1)S(1)}, bf16[24,2432]{1,0:T(8,128)(2,1)S(1)}, u32[]{:S(2)}, u32[]{:S(2)}) collective-permute-start(bf16[24,2432]{1,0:T(8,128)(2,1)S(1)} %pack.1), channel_id=1, source_target_pairs={{0,4},{1,5},{2,6},{3,7},{4,0},{5,1},{6,2},{7,3},{8,12},{9,13},{10,... | collective-permute-start | bytes 350216 | tf_op jit(solution)/shard_map/ppermute | solution.py:647
  21.0 7.4 %copy-start.27 = (bf16[96,768]{1,0:T(8,128)(2,1)S(1)}, bf16[96,768]{1,0:T(8,128)(2,1)}, u32[]{:S(2)}) copy-start(bf16[96,768]{1,0:T(8,128)(2,1)} %param.31) | copy-start | bytes 442372
  21.0 7.2 %collective-permute-start.1 = (bf16[2,24,2432]{2,1,0:T(8,128)(2,1)S(1)}, bf16[2,24,2432]{2,1,0:T(8,128)(2,1)S(1)}, u32[]{:S(2)}, u32[]{:S(2)}) collective-permute-start(bf16[2,24,2432]{2,1,0:T(8,128)(2,1)S(1)} %pad_maximum_fusion.11), channel_id=1, source_target_pairs={{0,2},{1,3},{2,0},{3,1},{4,6},{5,7},{6,4},{7,5},{8,10},{9,11},{10,... | collective-permute-start | bytes 700424 | tf_op jit(solution)/shard_map/ppermute | solution.py:647
  28.4 12.5 %collective-permute-start.8 = (bf16[96,768]{1,0:T(8,128)(2,1)S(1)}, bf16[96,768]{1,0:T(8,128)(2,1)S(1)}, u32[]{:S(2)}, u32[]{:S(2)}) collective-permute-start(bf16[96,768]{1,0:T(8,128)(2,1)S(1)} %copy-done.27), channel_id=1, source_target_pairs={{0,4},{1,5},{2,6},{3,7},{4,0},{5,1},{6,2},{7,3},{8,12},{9,13},{10,... | collective-permute-start | bytes 442376 | tf_op jit(solution)/shard_map/ppermute | solution.py:647
  32.6 8.4 %collective-permute-start.2 = (bf16[2,2,24,1152]{3,2,0,1:T(8,128)(2,1)S(1)}, bf16[2,2,24,1152]{3,2,0,1:T(8,128)(2,1)S(1)}, u32[]{:S(2)}, u32[]{:S(2)}) collective-permute-start(bf16[2,2,24,1152]{3,2,0,1:T(8,128)(2,1)S(1)} %fusion.20), channel_id=1, source_target_pairs={{0,16},{1,17},{2,18},{3,19},{4,20},{5,21},{6,22},{7,23},{8,24},{9,... | collective-permute-start | bytes 663560 | tf_op jit(solution)/shard_map/ppermute | solution.py:647
  34.1 8.6 %collective-permute-start.5 = (bf16[2,2,24,1280]{3,2,0,1:T(8,128)(2,1)S(1)}, bf16[2,2,24,1280]{3,2,0,1:T(8,128)(2,1)S(1)}, u32[]{:S(2)}, u32[]{:S(2)}) collective-permute-start(bf16[2,2,24,1280]{3,2,0,1:T(8,128)(2,1)S(1)} %fusion.19), channel_id=1, source_target_pairs={{0,8},{1,9},{2,10},{3,11},{4,12},{5,13},{6,14},{7,15},{8,0},{9,1},... | collective-permute-start | bytes 737288 | tf_op jit(solution)/shard_map/ppermute | solution.py:647
  41.1 16.6 %collective-permute-start.3 = (bf16[2,2,2,24,1152]{4,3,1,2,0:T(8,128)(2,1)S(1)}, bf16[2,2,2,24,1152]{4,3,1,2,0:T(8,128)(2,1)S(1)}, u32[]{:S(2)}, u32[]{:S(2)}) collective-permute-start(bf16[2,2,2,24,1152]{4,3,1,2,0:T(8,128)(2,1)S(1)} %pad_maximum_fusion.8), channel_id=1, source_target_pairs={{0,8},{1,9},{2,10},{3,11},{4,12},{5,13},{6,14},{7,15},{8,0},{9,1},... | collective-permute-start | bytes 1327112 | tf_op jit(solution)/shard_map/ppermute | solution.py:647
  42.8 16.0 %collective-permute-start.6 = (bf16[2,2,2,24,1280]{4,3,1,2,0:T(8,128)(2,1)S(1)}, bf16[2,2,2,24,1280]{4,3,1,2,0:T(8,128)(2,1)S(1)}, u32[]{:S(2)}, u32[]{:S(2)}) collective-permute-start(bf16[2,2,2,24,1280]{4,3,1,2,0:T(8,128)(2,1)S(1)} %pad_maximum_fusion.7), channel_id=1, source_target_pairs={{0,16},{1,17},{2,18},{3,19},{4,20},{5,21},{6,22},{7,23},{8,24},{9,... | collective-permute-start | bytes 1474568 | tf_op jit(solution)/shard_map/ppermute | solution.py:647
  44.4 15.1 %collective-permute-start.9 = (bf16[2,96,768]{2,1,0:T(8,128)(2,1)S(1)}, bf16[2,96,768]{2,1,0:T(8,128)(2,1)S(1)}, u32[]{:S(2)}, u32[]{:S(2)}) collective-permute-start(bf16[2,96,768]{2,1,0:T(8,128)(2,1)S(1)} %pad_maximum_fusion.10), channel_id=1, source_target_pairs={{0,2},{1,3},{2,0},{3,1},{4,6},{5,7},{6,4},{7,5},{8,10},{9,11},{10,... | collective-permute-start | bytes 884744 | tf_op jit(solution)/shard_map/ppermute | solution.py:647
  58.8 2.8 collective-permute-start.4
  59.0 3.9 %collective-permute-start.7 = (bf16[2,2,2,2,24,1280]{5,4,2,3,1,0:T(8,128)(2,1)S(1)}, bf16[2,2,2,2,24,1280]{5,4,2,3,1,0:T(8,128)(2,1)}, u32[]{:S(2)}, u32[]{:S(2)}) collective-permute-start(bf16[2,2,2,2,24,1280]{5,4,2,3,1,0:T(8,128)(2,1)S(1)} %pad_maximum_fusion.2), channel_id=1, source_target_pairs={{0,1},{1,0},{2,3},{3,2},{4,5},{5,4},{6,7},{7,6},{8,9},{9,8},{10,11... | collective-permute-start | bytes 2949128 | tf_op jit(solution)/shard_map/ppermute | solution.py:647
  64.8 5.4 %copy-start.2 = (bf16[1024,768]{1,0:T(8,128)(2,1)S(1)}, bf16[1024,768]{1,0:T(8,128)(2,1)}, u32[]{:S(2)}) copy-start(bf16[1024,768]{1,0:T(8,128)(2,1)} %refs_4_.1) | copy-start | bytes 4718596
  66.9 16.4 %collective-permute-start.10 = (bf16[2,2,96,384]{3,2,1,0:T(8,128)(2,1)}, bf16[2,2,96,384]{3,2,1,0:T(8,128)(2,1)}, u32[]{:S(2)}, u32[]{:S(2)}) collective-permute-start(bf16[2,2,96,384]{3,2,1,0:T(8,128)(2,1)} %get-tuple-element.96), channel_id=1, source_target_pairs={{0,16},{1,17},{2,18},{3,19},{4,20},{5,21},{6,22},{7,23},{8,24},{9,... | collective-permute-start | bytes 884744 | tf_op jit(solution)/shard_map/ppermute | solution.py:647
  68.5 16.4 %collective-permute-start.11 = (bf16[2,2,96,384]{3,2,1,0:T(8,128)(2,1)}, bf16[2,2,96,384]{3,2,1,0:T(8,128)(2,1)}, u32[]{:S(2)}, u32[]{:S(2)}) collective-permute-start(bf16[2,2,96,384]{3,2,1,0:T(8,128)(2,1)} %get-tuple-element.97), channel_id=1, source_target_pairs={{0,8},{1,9},{2,10},{3,11},{4,12},{5,13},{6,14},{7,15},{8,0},{9,1},... | collective-permute-start | bytes 884744 | tf_op jit(solution)/shard_map/ppermute | solution.py:647
  83.3 2.7 copy-start.9
  83.3 2.7 copy-start.15
  86.2 16.0 %collective-permute-start.13 = (bf16[2,2,2,96,384]{4,3,2,1,0:T(8,128)(2,1)S(1)}, bf16[2,2,2,96,384]{4,3,2,1,0:T(8,128)(2,1)S(1)}, u32[]{:S(2)}, u32[]{:S(2)}) collective-permute-start(bf16[2,2,2,96,384]{4,3,2,1,0:T(8,128)(2,1)S(1)} %get-tuple-element.101.refs_6_), channel_id=1, source_target_pairs={{0,16},{1,17},{2,18},{3,19},{4,20},{5,21},{6,22},{7,23},{8,24},{9,... | collective-permute-start | bytes 1769480 | tf_op jit(solution)/shard_map/ppermute | solution.py:647
  87.7 15.1 %collective-permute-start.12 = (bf16[2,2,2,96,384]{4,3,2,1,0:T(8,128)(2,1)S(1)}, bf16[2,2,2,96,384]{4,3,2,1,0:T(8,128)(2,1)S(1)}, u32[]{:S(2)}, u32[]{:S(2)}) collective-permute-start(bf16[2,2,2,96,384]{4,3,2,1,0:T(8,128)(2,1)S(1)} %get-tuple-element.100.refs_5_), channel_id=1, source_target_pairs={{0,8},{1,9},{2,10},{3,11},{4,12},{5,13},{6,14},{7,15},{8,0},{9,1},... | collective-permute-start | bytes 1769480 | tf_op jit(solution)/shard_map/ppermute | solution.py:647
  96.8 5.5 %copy-start.7 = (bf16[1024,256]{1,0:T(8,128)(2,1)}, bf16[1024,256]{1,0:T(8,128)(2,1)S(1)}, u32[]{:S(2)}) copy-start(bf16[1024,256]{1,0:T(8,128)(2,1)S(1)} %get-tuple-element.98.refs_2_.refs_10_.refs_5_) | copy-start | bytes 1572868
  96.9 5.5 %copy-start.13 = (bf16[1024,768]{1,0:T(8,128)(2,1)}, bf16[1024,768]{1,0:T(8,128)(2,1)S(1)}, u32[]{:S(2)}) copy-start(bf16[1024,768]{1,0:T(8,128)(2,1)S(1)} %get-tuple-element.120.refs_4_) | copy-start | bytes 4718596
  103.1 9.2 %collective-permute-start.14 = (bf16[2,2,2,2,96,384]{5,4,3,2,0,1:T(8,128)(2,1)S(1)}, bf16[2,2,2,2,96,384]{5,4,3,2,0,1:T(8,128)(2,1)S(1)}, u32[]{:S(2)}, u32[]{:S(2)}) collective-permute-start(bf16[2,2,2,2,96,384]{5,4,3,2,0,1:T(8,128)(2,1)S(1)} %pad_maximum_fusion), channel_id=1, source_target_pairs={{0,1},{1,0},{2,3},{3,2},{4,5},{5,4},{6,7},{7,6},{8,9},{9,8},{10,11... | collective-permute-start | bytes 3538952 | tf_op jit(solution)/shard_map/ppermute | solution.py:647
  103.2 10.8 %collective-permute-start.15 = (bf16[2,2,2,2,96,384]{5,4,3,2,1,0:T(8,128)(2,1)S(1)}, bf16[2,2,2,2,96,384]{5,4,3,2,1,0:T(8,128)(2,1)}, u32[]{:S(2)}, u32[]{:S(2)}) collective-permute-start(bf16[2,2,2,2,96,384]{5,4,3,2,1,0:T(8,128)(2,1)S(1)} %pad_maximum_fusion.1.refs_6_), channel_id=1, source_target_pairs={{0,1},{1,0},{2,3},{3,2},{4,5},{5,4},{6,7},{7,6},{8,9},{9,8},{10,11... | collective-permute-start | bytes 3538952 | tf_op jit(solution)/shard_map/ppermute | solution.py:647
  146.7 28.9 %collective-permute-start.16 = (bf16[16,96,768]{2,1,0:T(8,128)(2,1)}, bf16[16,96,768]{2,1,0:T(8,128)(2,1)}, u32[]{:S(2)}, u32[]{:S(2)}) collective-permute-start(bf16[16,96,768]{2,1,0:T(8,128)(2,1)} %get-tuple-element.118), channel_id=1, source_target_pairs={{0,1},{1,0},{2,3},{3,2},{4,5},{5,4},{6,7},{7,6},{8,9},{9,8},{10,11... | collective-permute-start | bytes 7077896 | tf_op jit(solution)/shard_map/ppermute | solution.py:647
  174.9 21.5 %collective-permute-start.19 = (bf16[16,24,3072]{2,1,0:T(8,128)(2,1)}, bf16[16,24,3072]{2,1,0:T(8,128)(2,1)}, u32[]{:S(2)}, u32[]{:S(2)}) collective-permute-start(bf16[16,24,3072]{2,1,0:T(8,128)(2,1)} %get-tuple-element.125), channel_id=1, source_target_pairs={{0,1},{1,0},{2,3},{3,2},{4,5},{5,4},{6,7},{7,6},{8,9},{9,8},{10,11... | collective-permute-start | bytes 7077896 | tf_op jit(solution)/shard_map/ppermute | solution.py:647
  178.7 3.2 %copy-start.18 = (bf16[16,24,768]{2,1,0:T(8,128)(2,1)S(1)}, bf16[16,24,768]{2,1,0:T(8,128)(2,1)}, u32[]{:S(2)}) copy-start(bf16[16,24,768]{2,1,0:T(8,128)(2,1)} %get-tuple-element.116.refs_9_) | copy-start | bytes 1769476
  179.1 2.8 copy-start.16
  179.1 2.8 copy-start.17
  179.3 2.6 copy-start.4
  179.3 2.6 copy-start.10
  179.4 22.0 %collective-permute-start.18 = (bf16[2,2,2,96,384]{4,3,2,1,0:T(8,128)(2,1)S(1)}, bf16[2,2,2,96,384]{4,3,2,1,0:T(8,128)(2,1)S(1)}, u32[]{:S(2)}, u32[]{:S(2)}) collective-permute-start(bf16[2,2,2,96,384]{4,3,2,1,0:T(8,128)(2,1)S(1)} %dynamic-slice_bitcast_fusion.2), channel_id=1, source_target_pairs={{0,16},{1,17},{2,18},{3,19},{4,20},{5,21},{6,22},{7,23},{8,24},{9,... | collective-permute-start | bytes 1769480 | tf_op jit(solution)/shard_map/ppermute | solution.py:647
  181.2 20.4 %collective-permute-start.17 = (bf16[2,2,2,96,384]{4,3,2,1,0:T(8,128)(2,1)S(1)}, bf16[2,2,2,96,384]{4,3,2,1,0:T(8,128)(2,1)S(1)}, u32[]{:S(2)}, u32[]{:S(2)}) collective-permute-start(bf16[2,2,2,96,384]{4,3,2,1,0:T(8,128)(2,1)S(1)} %dynamic-slice_bitcast_fusion.3), channel_id=1, source_target_pairs={{0,8},{1,9},{2,10},{3,11},{4,12},{5,13},{6,14},{7,15},{8,0},{9,1},... | collective-permute-start | bytes 1769480 | tf_op jit(solution)/shard_map/ppermute | solution.py:647
  181.9 14.5 %copy-start.23 = (bf16[16,24,3072]{2,1,0:T(8,128)(2,1)S(1)}, bf16[16,24,3072]{2,1,0:T(8,128)(2,1)}, u32[]{:S(2)}) copy-start(bf16[16,24,3072]{2,1,0:T(8,128)(2,1)} %get-tuple-element.124) | copy-start | bytes 7077892
  194.5 34.5 %collective-permute-start.24 = (bf16[16,24,1536]{2,1,0:T(8,128)(2,1)}, bf16[16,24,1536]{2,1,0:T(8,128)(2,1)S(1)}, u32[]{:S(2)}, u32[]{:S(2)}) collective-permute-start(bf16[16,24,1536]{2,1,0:T(8,128)(2,1)} %get-tuple-element.138), channel_id=1, source_target_pairs={{0,1},{1,0},{2,3},{3,2},{4,5},{5,4},{6,7},{7,6},{8,9},{9,8},{10,11... | collective-permute-start | bytes 3538952 | tf_op jit(solution)/shard_map/ppermute | solution.py:647
  199.4 16.9 %collective-permute-start.22 = (bf16[2,2,2,24,1536]{4,3,2,1,0:T(8,128)(2,1)S(1)}, bf16[2,2,2,24,1536]{4,3,2,1,0:T(8,128)(2,1)S(1)}, u32[]{:S(2)}, u32[]{:S(2)}) collective-permute-start(bf16[2,2,2,24,1536]{4,3,2,1,0:T(8,128)(2,1)S(1)} %dynamic-slice_bitcast_fusion.1), channel_id=1, source_target_pairs={{0,8},{1,9},{2,10},{3,11},{4,12},{5,13},{6,14},{7,15},{8,0},{9,1},... | collective-permute-start | bytes 1769480 | tf_op jit(solution)/shard_map/ppermute | solution.py:647
  200.7 18.6 %collective-permute-start.23 = (bf16[2,2,2,24,1536]{4,3,2,1,0:T(8,128)(2,1)S(1)}, bf16[2,2,2,24,1536]{4,3,2,1,0:T(8,128)(2,1)S(1)}, u32[]{:S(2)}, u32[]{:S(2)}) collective-permute-start(bf16[2,2,2,24,1536]{4,3,2,1,0:T(8,128)(2,1)S(1)} %dynamic-slice_bitcast_fusion), channel_id=1, source_target_pairs={{0,16},{1,17},{2,18},{3,19},{4,20},{5,21},{6,22},{7,23},{8,24},{9,... | collective-permute-start | bytes 1769480 | tf_op jit(solution)/shard_map/ppermute | solution.py:647
  201.6 2.6 copy-start.8
  201.6 2.6 copy-start.14
  201.8 21.6 %collective-permute-start.21 = (bf16[2,2,96,384]{3,2,1,0:T(8,128)(2,1)S(1)}, bf16[2,2,96,384]{3,2,1,0:T(8,128)(2,1)S(1)}, u32[]{:S(2)}, u32[]{:S(2)}) collective-permute-start(bf16[2,2,96,384]{3,2,1,0:T(8,128)(2,1)S(1)} %dynamic-slice_bitcast_fusion.11), channel_id=1, source_target_pairs={{0,8},{1,9},{2,10},{3,11},{4,12},{5,13},{6,14},{7,15},{8,0},{9,1},... | collective-permute-start | bytes 884744 | tf_op jit(solution)/shard_map/ppermute | solution.py:647
  203.0 20.2 %collective-permute-start.20 = (bf16[2,2,96,384]{3,2,1,0:T(8,128)(2,1)S(1)}, bf16[2,2,96,384]{3,2,1,0:T(8,128)(2,1)S(1)}, u32[]{:S(2)}, u32[]{:S(2)}) collective-permute-start(bf16[2,2,96,384]{3,2,1,0:T(8,128)(2,1)S(1)} %dynamic-slice_bitcast_fusion.12), channel_id=1, source_target_pairs={{0,16},{1,17},{2,18},{3,19},{4,20},{5,21},{6,22},{7,23},{8,24},{9,... | collective-permute-start | bytes 884744 | tf_op jit(solution)/shard_map/ppermute | solution.py:647
  216.2 17.0 %slice-start = ((s8[5898240]{0:T(1024)(128)(4,1)}), s8[4194304]{0:T(1024)(128)(4,1)S(1)}, s32[]{:S(2)}) async-start(s8[5898240]{0:T(1024)(128)(4,1)} %bitcast.192), calls=%async_computation.1 | async-start | bytes 8388608
  216.4 12.5 %collective-permute-start.26 = (bf16[2,2,24,1536]{3,2,1,0:T(8,128)(2,1)S(1)}, bf16[2,2,24,1536]{3,2,1,0:T(8,128)(2,1)S(1)}, u32[]{:S(2)}, u32[]{:S(2)}) collective-permute-start(bf16[2,2,24,1536]{3,2,1,0:T(8,128)(2,1)S(1)} %dynamic-slice_bitcast_fusion.9), channel_id=1, source_target_pairs={{0,16},{1,17},{2,18},{3,19},{4,20},{5,21},{6,22},{7,23},{8,24},{9,... | collective-permute-start | bytes 884744 | tf_op jit(solution)/shard_map/ppermute | solution.py:647
  219.5 10.3 %collective-permute-start.27 = (bf16[2,2,24,1536]{3,2,1,0:T(8,128)(2,1)S(1)}, bf16[2,2,24,1536]{3,2,1,0:T(8,128)(2,1)S(1)}, u32[]{:S(2)}, u32[]{:S(2)}) collective-permute-start(bf16[2,2,24,1536]{3,2,1,0:T(8,128)(2,1)S(1)} %dynamic-slice_bitcast_fusion.8), channel_id=1, source_target_pairs={{0,8},{1,9},{2,10},{3,11},{4,12},{5,13},{6,14},{7,15},{8,0},{9,1},... | collective-permute-start | bytes 884744 | tf_op jit(solution)/shard_map/ppermute | solution.py:647
  223.3 23.9 %collective-permute-start.30 = (bf16[16,24,768]{2,1,0:T(8,128)(2,1)}, bf16[16,24,768]{2,1,0:T(8,128)(2,1)}, u32[]{:S(2)}, u32[]{:S(2)}) collective-permute-start(bf16[16,24,768]{2,1,0:T(8,128)(2,1)} %get-tuple-element.150), channel_id=1, source_target_pairs={{0,1},{1,0},{2,3},{3,2},{4,5},{5,4},{6,7},{7,6},{8,9},{9,8},{10,11... | collective-permute-start | bytes 1769480 | tf_op jit(solution)/shard_map/ppermute | solution.py:647
  223.5 5.5 %copy-start.24 = (bf16[16,24,1536]{2,1,0:T(8,128)(2,1)S(1)}, bf16[16,24,1536]{2,1,0:T(8,128)(2,1)}, u32[]{:S(2)}) copy-start(bf16[16,24,1536]{2,1,0:T(8,128)(2,1)} %get-tuple-element.137) | copy-start | bytes 3538948
  223.6 9.6 %slice-start.1 = ((s8[5898240]{0:T(1024)(128)(4,1)}), s8[1703936]{0:T(1024)(128)(4,1)S(1)}, s32[]{:S(2)}) async-start(s8[5898240]{0:T(1024)(128)(4,1)} %bitcast.192), calls=%async_computation.2 | async-start | bytes 3407872
  223.6 9.5 %collective-permute-start.25 = (bf16[2,96,768]{2,1,0:T(8,128)(2,1)S(1)}, bf16[2,96,768]{2,1,0:T(8,128)(2,1)S(1)}, u32[]{:S(2)}, u32[]{:S(2)}) collective-permute-start(bf16[2,96,768]{2,1,0:T(8,128)(2,1)S(1)} %dynamic-slice_bitcast_fusion.10), channel_id=1, source_target_pairs={{0,2},{1,3},{2,0},{3,1},{4,6},{5,7},{6,4},{7,5},{8,10},{9,11},{10,... | collective-permute-start | bytes 884744 | tf_op jit(solution)/shard_map/ppermute | solution.py:647
  229.3 3.9 %copy-start.12 = (bf16[1024,768]{1,0:T(8,128)(2,1)S(1)}, bf16[1024,768]{1,0:T(8,128)(2,1)}, u32[]{:S(2)}) copy-start(bf16[1024,768]{1,0:T(8,128)(2,1)} %copy-done.11) | copy-start | bytes 4718596
  229.4 3.9 %copy-start.6 = (bf16[1024,256]{1,0:T(8,128)(2,1)S(1)}, bf16[1024,256]{1,0:T(8,128)(2,1)}, u32[]{:S(2)}) copy-start(bf16[1024,256]{1,0:T(8,128)(2,1)} %copy-done.5) | copy-start | bytes 1572868
  229.4 15.7 %collective-permute-start.28 = (bf16[2,2,2,24,1536]{4,3,1,2,0:T(8,128)(2,1)S(1)}, bf16[2,2,2,24,1536]{4,3,1,2,0:T(8,128)(2,1)S(1)}, u32[]{:S(2)}, u32[]{:S(2)}) collective-permute-start(bf16[2,2,2,24,1536]{4,3,1,2,0:T(8,128)(2,1)S(1)} %copy_bitcast_fusion), channel_id=1, source_target_pairs={{0,8},{1,9},{2,10},{3,11},{4,12},{5,13},{6,14},{7,15},{8,0},{9,1},... | collective-permute-start | bytes 1769480 | tf_op jit(solution)/shard_map/ppermute | solution.py:647
  245.3 4.0 %copy-start.25 = (bf16[16,24,896]{2,1,0:T(8,128)(2,1)S(1)}, bf16[16,24,896]{2,1,0:T(8,128)(2,1)}, u32[]{:S(2)}) copy-start(bf16[16,24,896]{2,1,0:T(8,128)(2,1)} %get-tuple-element.146) | copy-start | bytes 2064388
  245.3 4.0 %collective-permute-start.29 = (bf16[16,24,896]{2,1,0:T(8,128)(2,1)}, bf16[16,24,896]{2,1,0:T(8,128)(2,1)}, u32[]{:S(2)}, u32[]{:S(2)}) collective-permute-start(bf16[16,24,896]{2,1,0:T(8,128)(2,1)} %get-tuple-element.148), channel_id=1, source_target_pairs={{0,1},{1,0},{2,3},{3,2},{4,5},{5,4},{6,7},{7,6},{8,9},{9,8},{10,11... | collective-permute-start | bytes 2064392 | tf_op jit(solution)/shard_map/ppermute | solution.py:647
  250.6 16.4 %collective-permute-start.34 = (bf16[96,768]{1,0:T(8,128)(2,1)S(1)}, bf16[96,768]{1,0:T(8,128)(2,1)S(1)}, u32[]{:S(2)}, u32[]{:S(2)}) collective-permute-start(bf16[96,768]{1,0:T(8,128)(2,1)S(1)} %dynamic-slice_bitcast_fusion.18), channel_id=1, source_target_pairs={{0,4},{1,5},{2,6},{3,7},{4,0},{5,1},{6,2},{7,3},{8,12},{9,13},{10,... | collective-permute-start | bytes 442376 | tf_op jit(solution)/shard_map/ppermute | solution.py:647
  253.2 14.6 %collective-permute-start.32 = (bf16[2,2,2,24,768]{4,3,2,1,0:T(8,128)(2,1)S(1)}, bf16[2,2,2,24,768]{4,3,2,1,0:T(8,128)(2,1)S(1)}, u32[]{:S(2)}, u32[]{:S(2)}) collective-permute-start(bf16[2,2,2,24,768]{4,3,2,1,0:T(8,128)(2,1)S(1)} %dynamic-slice_bitcast_fusion.6), channel_id=1, source_target_pairs={{0,8},{1,9},{2,10},{3,11},{4,12},{5,13},{6,14},{7,15},{8,0},{9,1},... | collective-permute-start | bytes 884744 | tf_op jit(solution)/shard_map/ppermute | solution.py:647
  254.3 13.5 %collective-permute-start.31 = (bf16[2,2,24,1536]{3,2,0,1:T(8,128)(2,1)S(1)}, bf16[2,2,24,1536]{3,2,0,1:T(8,128)(2,1)S(1)}, u32[]{:S(2)}, u32[]{:S(2)}) collective-permute-start(bf16[2,2,24,1536]{3,2,0,1:T(8,128)(2,1)S(1)} %dynamic-slice_bitcast_fusion.7), channel_id=1, source_target_pairs={{0,16},{1,17},{2,18},{3,19},{4,20},{5,21},{6,22},{7,23},{8,24},{9,... | collective-permute-start | bytes 884744 | tf_op jit(solution)/shard_map/ppermute | solution.py:647
  255.5 12.2 %collective-permute-start.35 = (bf16[2,24,3072]{2,1,0:T(8,128)(2,1)S(1)}, bf16[2,24,3072]{2,1,0:T(8,128)(2,1)S(1)}, u32[]{:S(2)}, u32[]{:S(2)}) collective-permute-start(bf16[2,24,3072]{2,1,0:T(8,128)(2,1)S(1)} %dynamic-slice_bitcast_fusion.5), channel_id=1, source_target_pairs={{0,2},{1,3},{2,0},{3,1},{4,6},{5,7},{6,4},{7,5},{8,10},{9,11},{10,... | collective-permute-start | bytes 884744 | tf_op jit(solution)/shard_map/ppermute | solution.py:647
  257.9 12.3 %collective-permute-start.33 = (bf16[2,2,2,24,896]{4,3,2,1,0:T(8,128)(2,1)S(1)}, bf16[2,2,2,24,896]{4,3,2,1,0:T(8,128)(2,1)S(1)}, u32[]{:S(2)}, u32[]{:S(2)}) collective-permute-start(bf16[2,2,2,24,896]{4,3,2,1,0:T(8,128)(2,1)S(1)} %dynamic-slice_bitcast_fusion.4), channel_id=1, source_target_pairs={{0,16},{1,17},{2,18},{3,19},{4,20},{5,21},{6,22},{7,23},{8,24},{9,... | collective-permute-start | bytes 1032200 | tf_op jit(solution)/shard_map/ppermute | solution.py:647
  270.3 8.6 %collective-permute-start.39 = (bf16[24,3072]{1,0:T(8,128)(2,1)S(1)}, bf16[24,3072]{1,0:T(8,128)(2,1)S(1)}, u32[]{:S(2)}, u32[]{:S(2)}) collective-permute-start(bf16[24,3072]{1,0:T(8,128)(2,1)S(1)} %dynamic-slice_bitcast_fusion.15), channel_id=1, source_target_pairs={{0,4},{1,5},{2,6},{3,7},{4,0},{5,1},{6,2},{7,3},{8,12},{9,13},{10,... | collective-permute-start | bytes 442376 | tf_op jit(solution)/shard_map/ppermute | solution.py:647
  271.1 8.6 %collective-permute-start.36 = (bf16[2,24,1536]{2,1,0:T(8,128)(2,1)S(1)}, bf16[2,24,1536]{2,1,0:T(8,128)(2,1)S(1)}, u32[]{:S(2)}, u32[]{:S(2)}) collective-permute-start(bf16[2,24,1536]{2,1,0:T(8,128)(2,1)S(1)} %dynamic-slice_bitcast_fusion.17), channel_id=1, source_target_pairs={{0,2},{1,3},{2,0},{3,1},{4,6},{5,7},{6,4},{7,5},{8,10},{9,11},{10,... | collective-permute-start | bytes 442376 | tf_op jit(solution)/shard_map/ppermute | solution.py:647
  272.4 7.3 %collective-permute-start.37 = (bf16[2,2,24,768]{3,2,1,0:T(8,128)(2,1)S(1)}, bf16[2,2,24,768]{3,2,1,0:T(8,128)(2,1)S(1)}, u32[]{:S(2)}, u32[]{:S(2)}) collective-permute-start(bf16[2,2,24,768]{3,2,1,0:T(8,128)(2,1)S(1)} %dynamic-slice_bitcast_fusion.16), channel_id=1, source_target_pairs={{0,16},{1,17},{2,18},{3,19},{4,20},{5,21},{6,22},{7,23},{8,24},{9,... | collective-permute-start | bytes 442376 | tf_op jit(solution)/shard_map/ppermute | solution.py:647
  274.1 5.6 %collective-permute-start.38 = (bf16[2,2,24,896]{3,2,1,0:T(8,128)(2,1)S(1)}, bf16[2,2,24,896]{3,2,1,0:T(8,128)(2,1)S(1)}, u32[]{:S(2)}, u32[]{:S(2)}) collective-permute-start(bf16[2,2,24,896]{3,2,1,0:T(8,128)(2,1)S(1)} %dynamic-slice_bitcast_fusion.13), channel_id=1, source_target_pairs={{0,8},{1,9},{2,10},{3,11},{4,12},{5,13},{6,14},{7,15},{8,0},{9,1},... | collective-permute-start | bytes 516104 | tf_op jit(solution)/shard_map/ppermute | solution.py:647
  279.8 6.1 %collective-permute-start.40 = (bf16[24,1536]{1,0:T(8,128)(2,1)S(1)}, bf16[24,1536]{1,0:T(8,128)(2,1)S(1)}, u32[]{:S(2)}, u32[]{:S(2)}) collective-permute-start(bf16[24,1536]{1,0:T(8,128)(2,1)S(1)} %dynamic-slice_bitcast_fusion.20), channel_id=1, source_target_pairs={{0,4},{1,5},{2,6},{3,7},{4,0},{5,1},{6,2},{7,3},{8,12},{9,13},{10,... | collective-permute-start | bytes 221192 | tf_op jit(solution)/shard_map/ppermute | solution.py:647
  282.5 5.3 %collective-permute-start.41 = (bf16[2,24,1664]{2,1,0:T(8,128)(2,1)S(1)}, bf16[2,24,1664]{2,1,0:T(8,128)(2,1)S(1)}, u32[]{:S(2)}, u32[]{:S(2)}) collective-permute-start(bf16[2,24,1664]{2,1,0:T(8,128)(2,1)S(1)} %dynamic-slice_bitcast_fusion.14), channel_id=1, source_target_pairs={{0,2},{1,3},{2,0},{3,1},{4,6},{5,7},{6,4},{7,5},{8,10},{9,11},{10,... | collective-permute-start | bytes 479240 | tf_op jit(solution)/shard_map/ppermute | solution.py:647
  287.9 6.2 %collective-permute-start.42 = (bf16[24,1664]{1,0:T(8,128)(2,1)S(1)}, bf16[24,1664]{1,0:T(8,128)(2,1)S(1)}, u32[]{:S(2)}, u32[]{:S(2)}) collective-permute-start(bf16[24,1664]{1,0:T(8,128)(2,1)S(1)} %dynamic-slice_bitcast_fusion.19), channel_id=1, source_target_pairs={{0,4},{1,5},{2,6},{3,7},{4,0},{5,1},{6,2},{7,3},{8,12},{9,13},{10,... | collective-permute-start | bytes 239624 | tf_op jit(solution)/shard_map/ppermute | solution.py:647
  (10 other events, 14.6 us)
Sparse Core Ops, SparseCore 0:
  17.0 79.0 all-gather.1

commit v4 on v3

--- a/solution.py
+++ b/solution.py
@@ -760,15 +760,17 @@
             down_piece, down_done = cube.gather_near(down_piece, step, down_done)
     packed = cube.gather_core(parts, [cube.swap(p, 0) for p in parts])
     vecs = turn(packed, 3 * GROUP * groups)
-    up_b = vecs[8 : 8 + each].reshape(each, n, own).transpose(1, 0, 2).reshape(1, hidden)
 
     down_parts = [tie(p, packed) for p in cube.halve(down_piece)]
-    made, wait = [], [tok_t, up_b]
+    made, wait = [], [tok_t]
     for g in range(groups):
         if g < steps_far:
             down_parts = cube.gather_far(down_parts, g, down_done)
         made.append(attend(seq_lengths, tokens, packed, g, vecs, wait))
         wait = [made[-1][2], *down_parts]
+        if g == 0:
+            up_b = tie(vecs[8 : 8 + each], made[0][2])
+            up_b = up_b.reshape(each, n, own).transpose(1, 0, 2).reshape(1, hidden)
         down_parts = [tie(p, made[-1][2]) for p in down_parts] if g < steps_far else down_parts
     for step in range(groups, steps_far):
         down_parts = cube.gather_far(down_parts, step, down_done)

time: 308 us -> 312 us (1.013)
  Pallas kernels: 127 us -> 140 us
  starting transfers between devices: 55 us -> 45.8 us
  waiting for transfers between devices: 64 us -> 60.2 us
  local copies, waits for them, and re-layouts: 18.8 us -> 22 us
    pallas_call x11, Pallas kernels: 127 us -> 140 us  [call(): return lambda *operands: made(*map(place, operands), *after)]
    ppermute x43, starting transfers between devices: 55 us -> 45.8 us  [swap(): return lax.ppermute(value, AXES, [(i, i ^ 1 << bit) for i in range(self.n)])]
    ppermute x43, waiting for transfers between devices: 64 us -> 60.1 us  [swap(): return lax.ppermute(value, AXES, [(i, i ^ 1 << bit) for i in range(self.n)])]
    unnamed x63 -> x61, local copies, waits for them, and re-layouts: 7.25 us -> 5.87 us
  transfers between devices with their start and end apart: 44 -> 44, of which waited for: 16 -> 15; matrix products, arithmetic and copies ran while one was open for 10% -> 12% of each run, Pallas kernels for 31% -> 34%
where the time goes in v4:
time: 312 us; the launch traced here: 309 us
  Pallas kernels  140 us (45%)
  waiting for transfers between devices  60.2 us (19%)
  starting transfers between devices  45.8 us (15%)
  other arithmetic  26.3 us (8%)
  local copies, waits for them, and re-layouts  22 us (7%)
  between operations  15.5 us (5%)
    pallas_call x11, Pallas kernels, call(): return lambda *operands: made(*map(place, operands), *after)  140 us
    ppermute x43, waiting for transfers between devices, swap(): return lax.ppermute(value, AXES, [(i, i ^ 1 << bit) for i in range(self.n)])  60.1 us
    ppermute x43, starting transfers between devices, swap(): return lax.ppermute(value, AXES, [(i, i ^ 1 << bit) for i in range(self.n)])  45.8 us
    another operation x26, other arithmetic, join(): jnp.stack([jnp.where(last, other, mine), jnp.where(last, mine, other)], at)  10.6 us
    convert_element_type x5, other arithmetic, scatter_core(): part = (keep.astype(F32) + self.swap(give, 0).astype(F32)).astype(BF)  8.43 us
  transfers between devices with their start and end apart: 44, of which 15 were waited for; matrix products, arithmetic and copies ran while one was open for 12% of the time, Pallas kernels for 34%

profile of v4, /device:TPU:0, one launch (start us, length us, event | category | flops | bytes accessed | tf_op | source)
XLA Modules:
  0.0 309.4 jit_solution(8977237654110414116)
XLA Ops:
  11.2 4.1 %collective-permute-start = (bf16[24,2432]{1,0:T(8,128)(2,1)S(1)}, bf16[24,2432]{1,0:T(8,128)(2,1)S(1)}, u32[]{:S(2)}, u32[]{:S(2)}) collective-permute-start(bf16[24,2432]{1,0:T(8,128)(2,1)S(1)} %pack.1), channel_id=1, source_target_pairs={{0,4},{1,5},{2,6},{3,7},{4,0},{5,1},{6,2},{7,3},{8,12},{9,13},{10,... | collective-permute-start | bytes 350216 | tf_op jit(solution)/shard_map/ppermute | solution.py:647
  15.2 1.6 pad_maximum_fusion.12
  16.9 4.1 %collective-permute-done = bf16[24,2432]{1,0:T(8,128)(2,1)S(1)} collective-permute-done((bf16[24,2432]{1,0:T(8,128)(2,1)S(1)}, bf16[24,2432]{1,0:T(8,128)(2,1)S(1)}, u32[]{:S(2)}, u32[]{:S(2)}) %collective-permute-start) | collective-permute-done | bytes 116768 | tf_op jit(solution)/shard_map/ppermute | solution.py:647
  21.8 6.4 %collective-permute-done.1 = bf16[2,24,2432]{2,1,0:T(8,128)(2,1)S(1)} collective-permute-done((bf16[2,24,2432]{2,1,0:T(8,128)(2,1)S(1)}, bf16[2,24,2432]{2,1,0:T(8,128)(2,1)S(1)}, u32[]{:S(2)}, u32[]{:S(2)}) %collective-permute-start.1) | collective-permute-done | bytes 233504 | tf_op jit(solution)/shard_map/ppermute | solution.py:647
  28.4 4.2 %collective-permute-start.8 = (bf16[96,768]{1,0:T(8,128)(2,1)S(1)}, bf16[96,768]{1,0:T(8,128)(2,1)S(1)}, u32[]{:S(2)}, u32[]{:S(2)}) collective-permute-start(bf16[96,768]{1,0:T(8,128)(2,1)S(1)} %copy-done.26), channel_id=1, source_target_pairs={{0,4},{1,5},{2,6},{3,7},{4,0},{5,1},{6,2},{7,3},{8,12},{9,13},{10,... | collective-permute-start | bytes 442376 | tf_op jit(solution)/shard_map/ppermute | solution.py:647
  32.6 1.5 collective-permute-start.2
  34.1 1.5 collective-permute-start.5
  35.6 5.3 %collective-permute-done.8 = bf16[96,768]{1,0:T(8,128)(2,1)S(1)} collective-permute-done((bf16[96,768]{1,0:T(8,128)(2,1)S(1)}, bf16[96,768]{1,0:T(8,128)(2,1)S(1)}, u32[]{:S(2)}, u32[]{:S(2)}) %collective-permute-start.8) | collective-permute-done | bytes 147488 | tf_op jit(solution)/shard_map/ppermute | solution.py:647
  41.1 1.6 collective-permute-start.3
  42.8 1.6 collective-permute-start.6
  44.4 13.3 %collective-permute-done.3 = bf16[2,2,2,24,1152]{4,3,1,2,0:T(8,128)(2,1)S(1)} collective-permute-done((bf16[2,2,2,24,1152]{4,3,1,2,0:T(8,128)(2,1)S(1)}, bf16[2,2,2,24,1152]{4,3,1,2,0:T(8,128)(2,1)S(1)}, u32[]{:S(2)}, u32[]{:S(2)}) %collective-permute-start.3) | collective-permute-done | bytes 442400 | tf_op jit(solution)/shard_map/ppermute | solution.py:647
  57.8 1.0 pad_maximum_fusion.3
  59.6 0.9 pad_maximum_fusion.9
  60.5 1.1 collective-permute-done.4
  61.6 1.4 select_bitcast_fusion.3
  62.9 1.3 select_bitcast_fusion.1
  64.8 2.1 copy.49
  66.9 1.6 collective-permute-start.10
  68.5 1.7 collective-permute-start.11
  71.0 2.1 copy-done
  73.7 9.2 %attend.3 = (bf16[1024,768]{1,0:T(8,128)(2,1)S(1)}, bf16[1024,256]{1,0:T(8,128)(2,1)S(1)}, f32[8,1024]{1,0:T(8,128)S(1)}) custom-call(s32[1,9]{1,0:T(1,128)S(1)} %copy-done.21, bf16[1024,768]{1,0:T(8,128)(2,1)S(1)} %copy-done.2, bf16[768,2432]{1,0:T(8,128)(2,1)S(1)} %bitcast.196, f32[16,768]{1,0:T(8,128)S(1)} %turn.1.refs_3_.refs_8_.refs_5_, ...), custom_call_target="tpu_custom_call" | custom-call | flops 9000000 | tf_op jit(solution)/shard_map/attend/pallas_call | solution.py:52
  83.0 1.5 select_bitcast_fusion.15
  84.6 1.1 select_bitcast_fusion.13
  85.9 1.1 collective-permute-start.13
  86.9 1.7 collective-permute-start.12
  88.6 9.5 %attend.4 = (bf16[1024,768]{1,0:T(8,128)(2,1)S(1)}, bf16[1024,256]{1,0:T(8,128)(2,1)S(1)}, f32[8,1024]{1,0:T(8,128)S(1)}) custom-call(s32[1,9]{1,0:T(1,128)S(1)} %copy-done.21, bf16[1024,768]{1,0:T(8,128)(2,1)S(1)} %copy-done.2, bf16[768,2432]{1,0:T(8,128)(2,1)S(1)} %bitcast.197, f32[16,768]{1,0:T(8,128)S(1)} %turn.1.refs_3_.refs_8_.refs_5_, ...), custom_call_target="tpu_custom_call" | custom-call | flops 9000000 | tf_op jit(solution)/shard_map/attend/pallas_call | solution.py:52
  98.1 2.6 collective-permute-done.13
  100.9 1.2 pad_maximum_fusion.1.refs_6_
  102.2 1.1 pad_maximum_fusion
  104.1 1.5 copy.52.refs_5_
  105.7 2.4 copy.54
  108.1 9.0 %attend.5 = (bf16[1024,768]{1,0:T(8,128)(2,1)S(1)}, bf16[1024,256]{1,0:T(8,128)(2,1)S(1)}, f32[8,1024]{1,0:T(8,128)S(1)}) custom-call(s32[1,9]{1,0:T(1,128)S(1)} %copy-done.21, bf16[1024,768]{1,0:T(8,128)(2,1)S(1)} %copy-done.2, bf16[768,2432]{1,0:T(8,128)(2,1)S(1)} %bitcast.198, f32[16,768]{1,0:T(8,128)S(1)} %turn.1.refs_3_.refs_8_.refs_5_, ...), custom_call_target="tpu_custom_call" | custom-call | flops 9000000 | tf_op jit(solution)/shard_map/attend/pallas_call | solution.py:52
  117.1 3.2 %copy.55 = bf16[2,2,2,2,96,384]{5,4,3,2,1,0:T(8,128)(2,1)} copy(bf16[2,2,2,2,96,384]{5,4,3,2,0,1:T(8,128)(2,1)} %collective-permute-done.14) | data formatting | bytes 2359296 | tf_op jit(solution)/shard_map/ppermute | solution.py:647
  120.3 32.9 %forward.1 = (bf16[16,96,768]{2,1,0:T(8,128)(2,1)}, bf16[16,96,768]{2,1,0:T(8,128)(2,1)}, f32[1024,768]{1,0:T(8,128)}, f32[1024,128]{1,0:T(8,128)}, bf16[1024,76...) custom-call(s32[1,1]{1,0:T(1,128)} %bitcast.refs_0_.refs_1_, ...), custom_call_target="tpu_custom_call" | custom-call | flops 32000000 | tf_op jit(solution)/shard_map/forward/pallas_call | solution.py:52
  153.3 26.5 %backward.1 = (bf16[16,24,3072]{2,1,0:T(8,128)(2,1)}, bf16[16,24,3072]{2,1,0:T(8,128)(2,1)}, bf16[16,24,768]{2,1,0:T(8,128)(2,1)}, bf16[16,24,768]{2,1,0:T(8,128...) custom-call(s32[1,1]{1,0:T(1,128)} %bitcast.refs_0_.refs_1_, ...), custom_call_target="tpu_custom_call" | custom-call | flops 26000000 | tf_op jit(solution)/shard_map/backward/pallas_call | solution.py:52
  180.9 3.1 add_convert_fusion.1
  185.2 1.8 collective-permute-start.17
  187.1 14.8 %attend_back.3 = (bf16[16,24,1536]{2,1,0:T(8,128)(2,1)}, bf16[16,24,1536]{2,1,0:T(8,128)(2,1)}, bf16[1024,768]{1,0:T(8,128)(2,1)}, f32[8,768]{1,0:T(8,128)S(1)}) custom-call(s32[1,9]{1,0:T(1,128)S(1)} %copy-done.21, s32[1,1]{1,0:T(1,128)} %bitcast.refs_0_.refs_1_, bf16[768,1024]{1,0:T(8,128)(2,1)S(1)} %bitcast.200, ...), custom_call_target="tpu_custom_call" | custom-call | flops 15000000 | tf_op jit(solution)/shard_map/attend_back/pallas_call | solution.py:52
  201.9 2.5 add_convert_fusion
  205.5 1.0 collective-permute-start.23
  206.8 1.2 collective-permute-start.21
  208.1 1.5 collective-permute-start.20
  209.7 14.3 %attend_back.4 = (bf16[16,24,768]{2,1,0:T(8,128)(2,1)}, bf16[16,24,768]{2,1,0:T(8,128)(2,1)}, bf16[1024,768]{1,0:T(8,128)(2,1)}, f32[8,768]{1,0:T(8,128)S(1)}) custom-call(s32[1,9]{1,0:T(1,128)S(1)} %copy-done.21, s32[1,1]{1,0:T(1,128)} %bitcast.refs_0_.refs_1_, bf16[768,1024]{1,0:T(8,128)(2,1)S(1)} %bitcast.201, ...), custom_call_target="tpu_custom_call" | custom-call | flops 15000000 | tf_op jit(solution)/shard_map/attend_back/pallas_call | solution.py:52
  224.6 0.9 collective-permute-start.27
  225.5 2.6 collective-permute-done.20
  228.6 5.0 %collective-permute-done.26 = bf16[2,2,24,1536]{3,2,1,0:T(8,128)(2,1)S(1)} collective-permute-done((bf16[2,2,24,1536]{3,2,1,0:T(8,128)(2,1)S(1)}, bf16[2,2,24,1536]{3,2,1,0:T(8,128)(2,1)S(1)}, u32[]{:S(2)}, u32[]{:S(2)}) %collective-permute-start.26) | collective-permute-done | bytes 294944 | tf_op jit(solution)/shard_map/ppermute | solution.py:647
  234.1 1.6 collective-permute-start.28
  235.8 2.1 collective-permute-done.25
  238.0 14.2 %attend_back.5 = (bf16[16,24,896]{2,1,0:T(8,128)(2,1)}, bf16[16,24,896]{2,1,0:T(8,128)(2,1)}, bf16[1024,768]{1,0:T(8,128)(2,1)}, f32[8,768]{1,0:T(8,128)}) custom-call(s32[1,9]{1,0:T(1,128)S(1)} %copy-done.21, s32[1,1]{1,0:T(1,128)} %bitcast.refs_0_.refs_1_, bf16[768,1024]{1,0:T(8,128)(2,1)S(1)} %bitcast.202, bf16[768,3840]{1,0:T(8,128)(2,1)S(1)} %bitcast.193, ...), custom_call_target="tpu_custom_call" | custom-call | flops 15000000 | tf_op jit(solution)/shard_map/attend_back/pallas_call | solution.py:52
  253.3 1.2 add_convert_fusion.4
  254.9 1.3 add_convert_fusion.3
  256.2 0.9 collective-permute-start.34
  257.2 1.4 collective-permute-start.32
  258.6 1.2 collective-permute-start.31
  259.8 1.6 collective-permute-start.35
  261.4 1.2 collective-permute-start.33
  262.6 9.0 %tokens_back.1 = f32[1024,768]{1,0:T(8,128)} custom-call(f32[1024,768]{1,0:T(8,128)} %get-tuple-element.114.refs_0_, bf16[768,2432]{1,0:T(8,128)(2,1)} %bitcast.194, bf16[1024,768]{1,0:T(8,128)(2,1)} %get-tuple-element.121.refs_2_, bf16[1024,768]{1,0:T(8,128)(2,1)} %get-tuple-element.128.refs_3_, bf16[1024,768]{1,0:T(8,128)(2,1)} %get-tuple-element.141.refs_4_, ...), custom_call_target="tpu_custom_call" | custom-call | flops 8000000 | tf_op jit(solution)/shard_map/tokens_back/pallas_call | solution.py:52
  272.6 1.8 collective-permute-done.33
  274.6 2.1 collective-permute-start.39
  278.4 4.7 %collective-permute-done.39 = bf16[24,3072]{1,0:T(8,128)(2,1)S(1)} collective-permute-done((bf16[24,3072]{1,0:T(8,128)(2,1)S(1)}, bf16[24,3072]{1,0:T(8,128)(2,1)S(1)}, u32[]{:S(2)}, u32[]{:S(2)}) %collective-permute-start.39) | collective-permute-done | bytes 147488 | tf_op jit(solution)/shard_map/ppermute | solution.py:647
  284.1 1.9 collective-permute-start.40
  286.7 3.5 %collective-permute-done.40 = bf16[24,1536]{1,0:T(8,128)(2,1)S(1)} collective-permute-done((bf16[24,1536]{1,0:T(8,128)(2,1)S(1)}, bf16[24,1536]{1,0:T(8,128)(2,1)S(1)}, u32[]{:S(2)}, u32[]{:S(2)}) %collective-permute-start.40) | collective-permute-done | bytes 73760 | tf_op jit(solution)/shard_map/ppermute | solution.py:647
  290.3 2.5 collective-permute-done.41
  294.1 4.5 %collective-permute-done.42 = bf16[24,1664]{1,0:T(8,128)(2,1)S(1)} collective-permute-done((bf16[24,1664]{1,0:T(8,128)(2,1)S(1)}, bf16[24,1664]{1,0:T(8,128)(2,1)S(1)}, u32[]{:S(2)}, u32[]{:S(2)}) %collective-permute-start.42) | collective-permute-done | bytes 79904 | tf_op jit(solution)/shard_map/ppermute | solution.py:647
  (206 shorter events, 25.5 us)
Async XLA Ops:
  7.2 113.1 %all-gather.2.cloned.1.call-start = ((), (), s32[]{:S(2)}) async-start(), calls=%async_computation | async-start | bytes 6082560 | tf_op jit(solution)/shard_map/all_gather | solution.py:747
  11.2 9.8 %collective-permute-start = (bf16[24,2432]{1,0:T(8,128)(2,1)S(1)}, bf16[24,2432]{1,0:T(8,128)(2,1)S(1)}, u32[]{:S(2)}, u32[]{:S(2)}) collective-permute-start(bf16[24,2432]{1,0:T(8,128)(2,1)S(1)} %pack.1), channel_id=1, source_target_pairs={{0,4},{1,5},{2,6},{3,7},{4,0},{5,1},{6,2},{7,3},{8,12},{9,13},{10,... | collective-permute-start | bytes 350216 | tf_op jit(solution)/shard_map/ppermute | solution.py:647
  21.0 7.4 %copy-start.26 = (bf16[96,768]{1,0:T(8,128)(2,1)S(1)}, bf16[96,768]{1,0:T(8,128)(2,1)}, u32[]{:S(2)}) copy-start(bf16[96,768]{1,0:T(8,128)(2,1)} %param.31) | copy-start | bytes 442372
  21.0 7.2 %collective-permute-start.1 = (bf16[2,24,2432]{2,1,0:T(8,128)(2,1)S(1)}, bf16[2,24,2432]{2,1,0:T(8,128)(2,1)S(1)}, u32[]{:S(2)}, u32[]{:S(2)}) collective-permute-start(bf16[2,24,2432]{2,1,0:T(8,128)(2,1)S(1)} %pad_maximum_fusion.11), channel_id=1, source_target_pairs={{0,2},{1,3},{2,0},{3,1},{4,6},{5,7},{6,4},{7,5},{8,10},{9,11},{10,... | collective-permute-start | bytes 700424 | tf_op jit(solution)/shard_map/ppermute | solution.py:647
  28.4 12.5 %collective-permute-start.8 = (bf16[96,768]{1,0:T(8,128)(2,1)S(1)}, bf16[96,768]{1,0:T(8,128)(2,1)S(1)}, u32[]{:S(2)}, u32[]{:S(2)}) collective-permute-start(bf16[96,768]{1,0:T(8,128)(2,1)S(1)} %copy-done.26), channel_id=1, source_target_pairs={{0,4},{1,5},{2,6},{3,7},{4,0},{5,1},{6,2},{7,3},{8,12},{9,13},{10,... | collective-permute-start | bytes 442376 | tf_op jit(solution)/shard_map/ppermute | solution.py:647
  32.6 8.4 %collective-permute-start.2 = (bf16[2,2,24,1152]{3,2,0,1:T(8,128)(2,1)S(1)}, bf16[2,2,24,1152]{3,2,0,1:T(8,128)(2,1)S(1)}, u32[]{:S(2)}, u32[]{:S(2)}) collective-permute-start(bf16[2,2,24,1152]{3,2,0,1:T(8,128)(2,1)S(1)} %fusion.20), channel_id=1, source_target_pairs={{0,16},{1,17},{2,18},{3,19},{4,20},{5,21},{6,22},{7,23},{8,24},{9,... | collective-permute-start | bytes 663560 | tf_op jit(solution)/shard_map/ppermute | solution.py:647
  34.1 8.6 %collective-permute-start.5 = (bf16[2,2,24,1280]{3,2,0,1:T(8,128)(2,1)S(1)}, bf16[2,2,24,1280]{3,2,0,1:T(8,128)(2,1)S(1)}, u32[]{:S(2)}, u32[]{:S(2)}) collective-permute-start(bf16[2,2,24,1280]{3,2,0,1:T(8,128)(2,1)S(1)} %fusion.19), channel_id=1, source_target_pairs={{0,8},{1,9},{2,10},{3,11},{4,12},{5,13},{6,14},{7,15},{8,0},{9,1},... | collective-permute-start | bytes 737288 | tf_op jit(solution)/shard_map/ppermute | solution.py:647
  41.1 16.6 %collective-permute-start.3 = (bf16[2,2,2,24,1152]{4,3,1,2,0:T(8,128)(2,1)S(1)}, bf16[2,2,2,24,1152]{4,3,1,2,0:T(8,128)(2,1)S(1)}, u32[]{:S(2)}, u32[]{:S(2)}) collective-permute-start(bf16[2,2,2,24,1152]{4,3,1,2,0:T(8,128)(2,1)S(1)} %pad_maximum_fusion.8), channel_id=1, source_target_pairs={{0,8},{1,9},{2,10},{3,11},{4,12},{5,13},{6,14},{7,15},{8,0},{9,1},... | collective-permute-start | bytes 1327112 | tf_op jit(solution)/shard_map/ppermute | solution.py:647
  42.8 16.0 %collective-permute-start.6 = (bf16[2,2,2,24,1280]{4,3,1,2,0:T(8,128)(2,1)S(1)}, bf16[2,2,2,24,1280]{4,3,1,2,0:T(8,128)(2,1)S(1)}, u32[]{:S(2)}, u32[]{:S(2)}) collective-permute-start(bf16[2,2,2,24,1280]{4,3,1,2,0:T(8,128)(2,1)S(1)} %pad_maximum_fusion.7), channel_id=1, source_target_pairs={{0,16},{1,17},{2,18},{3,19},{4,20},{5,21},{6,22},{7,23},{8,24},{9,... | collective-permute-start | bytes 1474568 | tf_op jit(solution)/shard_map/ppermute | solution.py:647
  44.4 15.1 %collective-permute-start.9 = (bf16[2,96,768]{2,1,0:T(8,128)(2,1)S(1)}, bf16[2,96,768]{2,1,0:T(8,128)(2,1)S(1)}, u32[]{:S(2)}, u32[]{:S(2)}) collective-permute-start(bf16[2,96,768]{2,1,0:T(8,128)(2,1)S(1)} %pad_maximum_fusion.10), channel_id=1, source_target_pairs={{0,2},{1,3},{2,0},{3,1},{4,6},{5,7},{6,4},{7,5},{8,10},{9,11},{10,... | collective-permute-start | bytes 884744 | tf_op jit(solution)/shard_map/ppermute | solution.py:647
  58.8 2.8 collective-permute-start.4
  59.0 3.9 %collective-permute-start.7 = (bf16[2,2,2,2,24,1280]{5,4,2,3,1,0:T(8,128)(2,1)S(1)}, bf16[2,2,2,2,24,1280]{5,4,2,3,1,0:T(8,128)(2,1)}, u32[]{:S(2)}, u32[]{:S(2)}) collective-permute-start(bf16[2,2,2,2,24,1280]{5,4,2,3,1,0:T(8,128)(2,1)S(1)} %pad_maximum_fusion.2), channel_id=1, source_target_pairs={{0,1},{1,0},{2,3},{3,2},{4,5},{5,4},{6,7},{7,6},{8,9},{9,8},{10,11... | collective-permute-start | bytes 2949128 | tf_op jit(solution)/shard_map/ppermute | solution.py:647
  64.8 5.4 %copy-start.2 = (bf16[1024,768]{1,0:T(8,128)(2,1)S(1)}, bf16[1024,768]{1,0:T(8,128)(2,1)}, u32[]{:S(2)}) copy-start(bf16[1024,768]{1,0:T(8,128)(2,1)} %refs_4_.1) | copy-start | bytes 4718596
  66.9 16.1 %collective-permute-start.10 = (bf16[2,2,96,384]{3,2,1,0:T(8,128)(2,1)}, bf16[2,2,96,384]{3,2,1,0:T(8,128)(2,1)}, u32[]{:S(2)}, u32[]{:S(2)}) collective-permute-start(bf16[2,2,96,384]{3,2,1,0:T(8,128)(2,1)} %get-tuple-element.97), channel_id=1, source_target_pairs={{0,16},{1,17},{2,18},{3,19},{4,20},{5,21},{6,22},{7,23},{8,24},{9,... | collective-permute-start | bytes 884744 | tf_op jit(solution)/shard_map/ppermute | solution.py:647
  68.5 16.0 %collective-permute-start.11 = (bf16[2,2,96,384]{3,2,1,0:T(8,128)(2,1)}, bf16[2,2,96,384]{3,2,1,0:T(8,128)(2,1)}, u32[]{:S(2)}, u32[]{:S(2)}) collective-permute-start(bf16[2,2,96,384]{3,2,1,0:T(8,128)(2,1)} %get-tuple-element.98), channel_id=1, source_target_pairs={{0,8},{1,9},{2,10},{3,11},{4,12},{5,13},{6,14},{7,15},{8,0},{9,1},... | collective-permute-start | bytes 884744 | tf_op jit(solution)/shard_map/ppermute | solution.py:647
  83.0 2.7 copy-start.8
  83.0 2.7 copy-start.14
  85.9 14.9 %collective-permute-start.13 = (bf16[2,2,2,96,384]{4,3,2,1,0:T(8,128)(2,1)S(1)}, bf16[2,2,2,96,384]{4,3,2,1,0:T(8,128)(2,1)S(1)}, u32[]{:S(2)}, u32[]{:S(2)}) collective-permute-start(bf16[2,2,2,96,384]{4,3,2,1,0:T(8,128)(2,1)S(1)} %get-tuple-element.102.refs_6_), channel_id=1, source_target_pairs={{0,16},{1,17},{2,18},{3,19},{4,20},{5,21},{6,22},{7,23},{8,24},{9,... | collective-permute-start | bytes 1769480 | tf_op jit(solution)/shard_map/ppermute | solution.py:647
  86.9 15.1 %collective-permute-start.12 = (bf16[2,2,2,96,384]{4,3,2,1,0:T(8,128)(2,1)S(1)}, bf16[2,2,2,96,384]{4,3,2,1,0:T(8,128)(2,1)S(1)}, u32[]{:S(2)}, u32[]{:S(2)}) collective-permute-start(bf16[2,2,2,96,384]{4,3,2,1,0:T(8,128)(2,1)S(1)} %get-tuple-element.101.refs_5_), channel_id=1, source_target_pairs={{0,8},{1,9},{2,10},{3,11},{4,12},{5,13},{6,14},{7,15},{8,0},{9,1},... | collective-permute-start | bytes 1769480 | tf_op jit(solution)/shard_map/ppermute | solution.py:647
  98.1 2.8 copy-start.6
  98.1 2.8 copy-start.12
  103.3 13.8 %collective-permute-start.14 = (bf16[2,2,2,2,96,384]{5,4,3,2,0,1:T(8,128)(2,1)}, bf16[2,2,2,2,96,384]{5,4,3,2,0,1:T(8,128)(2,1)}, u32[]{:S(2)}, u32[]{:S(2)}) collective-permute-start(bf16[2,2,2,2,96,384]{5,4,3,2,0,1:T(8,128)(2,1)} %pad_maximum_fusion), channel_id=1, source_target_pairs={{0,1},{1,0},{2,3},{3,2},{4,5},{5,4},{6,7},{7,6},{8,9},{9,8},{10,11... | collective-permute-start | bytes 3538952 | tf_op jit(solution)/shard_map/ppermute | solution.py:647
  103.3 17.0 %collective-permute-start.15 = (bf16[2,2,2,2,96,384]{5,4,3,2,1,0:T(8,128)(2,1)}, bf16[2,2,2,2,96,384]{5,4,3,2,1,0:T(8,128)(2,1)}, u32[]{:S(2)}, u32[]{:S(2)}) collective-permute-start(bf16[2,2,2,2,96,384]{5,4,3,2,1,0:T(8,128)(2,1)} %pad_maximum_fusion.1.refs_6_), channel_id=1, source_target_pairs={{0,1},{1,0},{2,3},{3,2},{4,5},{5,4},{6,7},{7,6},{8,9},{9,8},{10,11... | collective-permute-start | bytes 3538952 | tf_op jit(solution)/shard_map/ppermute | solution.py:647
  104.1 4.0 %copy-start.1 = (bf16[2,2,2,2,2,24,2432]{6,5,4,3,2,1,0:T(8,128)(2,1)S(1)}, bf16[2,2,2,2,2,24,2432]{6,5,4,3,2,1,0:T(8,128)(2,1)}, u32[]{:S(2)}) copy-start(bf16[2,2,2,2,2,24,2432]{6,5,4,3,2,1,0:T(8,128)(2,1)} %copy.49) | copy-start | bytes 11206660
  117.1 3.2 %copy-start.4 = (bf16[1024,256]{1,0:T(8,128)(2,1)}, bf16[1024,256]{1,0:T(8,128)(2,1)S(1)}, u32[]{:S(2)}) copy-start(bf16[1024,256]{1,0:T(8,128)(2,1)S(1)} %get-tuple-element.103.refs_3_.refs_11_.refs_5_) | copy-start | bytes 1572868
  117.1 3.2 %copy-start.10 = (bf16[1024,768]{1,0:T(8,128)(2,1)}, bf16[1024,768]{1,0:T(8,128)(2,1)S(1)}, u32[]{:S(2)}) copy-start(bf16[1024,768]{1,0:T(8,128)(2,1)S(1)} %get-tuple-element.129.refs_4_) | copy-start | bytes 4718596
  153.2 27.7 %collective-permute-start.16 = (bf16[16,96,768]{2,1,0:T(8,128)(2,1)}, bf16[16,96,768]{2,1,0:T(8,128)(2,1)}, u32[]{:S(2)}, u32[]{:S(2)}) collective-permute-start(bf16[16,96,768]{2,1,0:T(8,128)(2,1)} %get-tuple-element.120), channel_id=1, source_target_pairs={{0,1},{1,0},{2,3},{3,2},{4,5},{5,4},{6,7},{7,6},{8,9},{9,8},{10,11... | collective-permute-start | bytes 7077896 | tf_op jit(solution)/shard_map/ppermute | solution.py:647
  179.8 22.1 %collective-permute-start.19 = (bf16[16,24,3072]{2,1,0:T(8,128)(2,1)}, bf16[16,24,3072]{2,1,0:T(8,128)(2,1)}, u32[]{:S(2)}, u32[]{:S(2)}) collective-permute-start(bf16[16,24,3072]{2,1,0:T(8,128)(2,1)} %get-tuple-element.127), channel_id=1, source_target_pairs={{0,1},{1,0},{2,3},{3,2},{4,5},{5,4},{6,7},{7,6},{8,9},{9,8},{10,11... | collective-permute-start | bytes 7077896 | tf_op jit(solution)/shard_map/ppermute | solution.py:647
  184.0 3.0 copy-start.17
  184.4 2.6 copy-start.15
  184.4 2.6 copy-start.16
  184.7 21.8 %collective-permute-start.18 = (bf16[2,2,2,96,384]{4,3,2,1,0:T(8,128)(2,1)S(1)}, bf16[2,2,2,96,384]{4,3,2,1,0:T(8,128)(2,1)S(1)}, u32[]{:S(2)}, u32[]{:S(2)}) collective-permute-start(bf16[2,2,2,96,384]{4,3,2,1,0:T(8,128)(2,1)S(1)} %dynamic-slice_bitcast_fusion.2), channel_id=1, source_target_pairs={{0,16},{1,17},{2,18},{3,19},{4,20},{5,21},{6,22},{7,23},{8,24},{9,... | collective-permute-start | bytes 1769480 | tf_op jit(solution)/shard_map/ppermute | solution.py:647
  185.2 21.4 %collective-permute-start.17 = (bf16[2,2,2,96,384]{4,3,2,1,0:T(8,128)(2,1)S(1)}, bf16[2,2,2,96,384]{4,3,2,1,0:T(8,128)(2,1)S(1)}, u32[]{:S(2)}, u32[]{:S(2)}) collective-permute-start(bf16[2,2,2,96,384]{4,3,2,1,0:T(8,128)(2,1)S(1)} %dynamic-slice_bitcast_fusion.3), channel_id=1, source_target_pairs={{0,8},{1,9},{2,10},{3,11},{4,12},{5,13},{6,14},{7,15},{8,0},{9,1},... | collective-permute-start | bytes 1769480 | tf_op jit(solution)/shard_map/ppermute | solution.py:647
  187.1 14.9 %copy-start.22 = (bf16[16,24,3072]{2,1,0:T(8,128)(2,1)S(1)}, bf16[16,24,3072]{2,1,0:T(8,128)(2,1)}, u32[]{:S(2)}) copy-start(bf16[16,24,3072]{2,1,0:T(8,128)(2,1)} %get-tuple-element.126) | copy-start | bytes 7077892
  201.9 31.8 %collective-permute-start.24 = (bf16[16,24,1536]{2,1,0:T(8,128)(2,1)}, bf16[16,24,1536]{2,1,0:T(8,128)(2,1)S(1)}, u32[]{:S(2)}, u32[]{:S(2)}) collective-permute-start(bf16[16,24,1536]{2,1,0:T(8,128)(2,1)} %get-tuple-element.140), channel_id=1, source_target_pairs={{0,1},{1,0},{2,3},{3,2},{4,5},{5,4},{6,7},{7,6},{8,9},{9,8},{10,11... | collective-permute-start | bytes 3538952 | tf_op jit(solution)/shard_map/ppermute | solution.py:647
  204.9 19.2 %collective-permute-start.22 = (bf16[2,2,2,24,1536]{4,3,2,1,0:T(8,128)(2,1)S(1)}, bf16[2,2,2,24,1536]{4,3,2,1,0:T(8,128)(2,1)S(1)}, u32[]{:S(2)}, u32[]{:S(2)}) collective-permute-start(bf16[2,2,2,24,1536]{4,3,2,1,0:T(8,128)(2,1)S(1)} %dynamic-slice_bitcast_fusion.1), channel_id=1, source_target_pairs={{0,8},{1,9},{2,10},{3,11},{4,12},{5,13},{6,14},{7,15},{8,0},{9,1},... | collective-permute-start | bytes 1769480 | tf_op jit(solution)/shard_map/ppermute | solution.py:647
  205.5 18.9 %collective-permute-start.23 = (bf16[2,2,2,24,1536]{4,3,2,1,0:T(8,128)(2,1)S(1)}, bf16[2,2,2,24,1536]{4,3,2,1,0:T(8,128)(2,1)S(1)}, u32[]{:S(2)}, u32[]{:S(2)}) collective-permute-start(bf16[2,2,2,24,1536]{4,3,2,1,0:T(8,128)(2,1)S(1)} %dynamic-slice_bitcast_fusion), channel_id=1, source_target_pairs={{0,16},{1,17},{2,18},{3,19},{4,20},{5,21},{6,22},{7,23},{8,24},{9,... | collective-permute-start | bytes 1769480 | tf_op jit(solution)/shard_map/ppermute | solution.py:647
  206.6 3.1 copy-start.7
  206.6 3.1 copy-start.13
  206.8 21.3 %collective-permute-start.21 = (bf16[2,2,96,384]{3,2,1,0:T(8,128)(2,1)S(1)}, bf16[2,2,96,384]{3,2,1,0:T(8,128)(2,1)S(1)}, u32[]{:S(2)}, u32[]{:S(2)}) collective-permute-start(bf16[2,2,96,384]{3,2,1,0:T(8,128)(2,1)S(1)} %dynamic-slice_bitcast_fusion.11), channel_id=1, source_target_pairs={{0,8},{1,9},{2,10},{3,11},{4,12},{5,13},{6,14},{7,15},{8,0},{9,1},... | collective-permute-start | bytes 884744 | tf_op jit(solution)/shard_map/ppermute | solution.py:647
  208.1 19.9 %collective-permute-start.20 = (bf16[2,2,96,384]{3,2,1,0:T(8,128)(2,1)S(1)}, bf16[2,2,96,384]{3,2,1,0:T(8,128)(2,1)S(1)}, u32[]{:S(2)}, u32[]{:S(2)}) collective-permute-start(bf16[2,2,96,384]{3,2,1,0:T(8,128)(2,1)S(1)} %dynamic-slice_bitcast_fusion.12), channel_id=1, source_target_pairs={{0,16},{1,17},{2,18},{3,19},{4,20},{5,21},{6,22},{7,23},{8,24},{9,... | collective-permute-start | bytes 884744 | tf_op jit(solution)/shard_map/ppermute | solution.py:647
  224.0 13.9 %slice-start = ((s8[5898240]{0:T(1024)(128)(4,1)}), s8[4194304]{0:T(1024)(128)(4,1)S(1)}, s32[]{:S(2)}) async-start(s8[5898240]{0:T(1024)(128)(4,1)} %bitcast.192), calls=%async_computation.1 | async-start | bytes 8388608
  224.2 9.4 %collective-permute-start.26 = (bf16[2,2,24,1536]{3,2,1,0:T(8,128)(2,1)S(1)}, bf16[2,2,24,1536]{3,2,1,0:T(8,128)(2,1)S(1)}, u32[]{:S(2)}, u32[]{:S(2)}) collective-permute-start(bf16[2,2,24,1536]{3,2,1,0:T(8,128)(2,1)S(1)} %dynamic-slice_bitcast_fusion.9), channel_id=1, source_target_pairs={{0,16},{1,17},{2,18},{3,19},{4,20},{5,21},{6,22},{7,23},{8,24},{9,... | collective-permute-start | bytes 884744 | tf_op jit(solution)/shard_map/ppermute | solution.py:647
  224.6 11.2 %collective-permute-start.27 = (bf16[2,2,24,1536]{3,2,1,0:T(8,128)(2,1)S(1)}, bf16[2,2,24,1536]{3,2,1,0:T(8,128)(2,1)S(1)}, u32[]{:S(2)}, u32[]{:S(2)}) collective-permute-start(bf16[2,2,24,1536]{3,2,1,0:T(8,128)(2,1)S(1)} %dynamic-slice_bitcast_fusion.8), channel_id=1, source_target_pairs={{0,8},{1,9},{2,10},{3,11},{4,12},{5,13},{6,14},{7,15},{8,0},{9,1},... | collective-permute-start | bytes 884744 | tf_op jit(solution)/shard_map/ppermute | solution.py:647
  228.0 24.4 %collective-permute-start.30 = (bf16[16,24,768]{2,1,0:T(8,128)(2,1)}, bf16[16,24,768]{2,1,0:T(8,128)(2,1)}, u32[]{:S(2)}, u32[]{:S(2)}) collective-permute-start(bf16[16,24,768]{2,1,0:T(8,128)(2,1)} %get-tuple-element.152), channel_id=1, source_target_pairs={{0,1},{1,0},{2,3},{3,2},{4,5},{5,4},{6,7},{7,6},{8,9},{9,8},{10,11... | collective-permute-start | bytes 1769480 | tf_op jit(solution)/shard_map/ppermute | solution.py:647
  228.3 5.4 %copy-start.23 = (bf16[16,24,1536]{2,1,0:T(8,128)(2,1)S(1)}, bf16[16,24,1536]{2,1,0:T(8,128)(2,1)}, u32[]{:S(2)}) copy-start(bf16[16,24,1536]{2,1,0:T(8,128)(2,1)} %get-tuple-element.139) | copy-start | bytes 3538948
  228.3 9.6 %slice-start.1 = ((s8[5898240]{0:T(1024)(128)(4,1)}), s8[1703936]{0:T(1024)(128)(4,1)S(1)}, s32[]{:S(2)}) async-start(s8[5898240]{0:T(1024)(128)(4,1)} %bitcast.192), calls=%async_computation.2 | async-start | bytes 3407872
  228.4 9.5 %collective-permute-start.25 = (bf16[2,96,768]{2,1,0:T(8,128)(2,1)S(1)}, bf16[2,96,768]{2,1,0:T(8,128)(2,1)S(1)}, u32[]{:S(2)}, u32[]{:S(2)}) collective-permute-start(bf16[2,96,768]{2,1,0:T(8,128)(2,1)S(1)} %dynamic-slice_bitcast_fusion.10), channel_id=1, source_target_pairs={{0,2},{1,3},{2,0},{3,1},{4,6},{5,7},{6,4},{7,5},{8,10},{9,11},{10,... | collective-permute-start | bytes 884744 | tf_op jit(solution)/shard_map/ppermute | solution.py:647
  234.0 4.0 %copy-start.11 = (bf16[1024,768]{1,0:T(8,128)(2,1)S(1)}, bf16[1024,768]{1,0:T(8,128)(2,1)}, u32[]{:S(2)}) copy-start(bf16[1024,768]{1,0:T(8,128)(2,1)} %copy-done.10) | copy-start | bytes 4718596
  234.1 3.9 %copy-start.5 = (bf16[1024,256]{1,0:T(8,128)(2,1)S(1)}, bf16[1024,256]{1,0:T(8,128)(2,1)}, u32[]{:S(2)}) copy-start(bf16[1024,256]{1,0:T(8,128)(2,1)} %copy-done.4) | copy-start | bytes 1572868
  234.1 18.1 %collective-permute-start.28 = (bf16[2,2,2,24,1536]{4,3,1,2,0:T(8,128)(2,1)S(1)}, bf16[2,2,2,24,1536]{4,3,1,2,0:T(8,128)(2,1)S(1)}, u32[]{:S(2)}, u32[]{:S(2)}) collective-permute-start(bf16[2,2,2,24,1536]{4,3,1,2,0:T(8,128)(2,1)S(1)} %copy_bitcast_fusion), channel_id=1, source_target_pairs={{0,8},{1,9},{2,10},{3,11},{4,12},{5,13},{6,14},{7,15},{8,0},{9,1},... | collective-permute-start | bytes 1769480 | tf_op jit(solution)/shard_map/ppermute | solution.py:647
  252.4 2.6 collective-permute-start.29
  256.2 15.3 %collective-permute-start.34 = (bf16[96,768]{1,0:T(8,128)(2,1)S(1)}, bf16[96,768]{1,0:T(8,128)(2,1)S(1)}, u32[]{:S(2)}, u32[]{:S(2)}) collective-permute-start(bf16[96,768]{1,0:T(8,128)(2,1)S(1)} %dynamic-slice_bitcast_fusion.18), channel_id=1, source_target_pairs={{0,4},{1,5},{2,6},{3,7},{4,0},{5,1},{6,2},{7,3},{8,12},{9,13},{10,... | collective-permute-start | bytes 442376 | tf_op jit(solution)/shard_map/ppermute | solution.py:647
  257.2 15.3 %collective-permute-start.32 = (bf16[2,2,2,24,768]{4,3,2,1,0:T(8,128)(2,1)S(1)}, bf16[2,2,2,24,768]{4,3,2,1,0:T(8,128)(2,1)S(1)}, u32[]{:S(2)}, u32[]{:S(2)}) collective-permute-start(bf16[2,2,2,24,768]{4,3,2,1,0:T(8,128)(2,1)S(1)} %dynamic-slice_bitcast_fusion.6), channel_id=1, source_target_pairs={{0,8},{1,9},{2,10},{3,11},{4,12},{5,13},{6,14},{7,15},{8,0},{9,1},... | collective-permute-start | bytes 884744 | tf_op jit(solution)/shard_map/ppermute | solution.py:647
  258.6 13.8 %collective-permute-start.31 = (bf16[2,2,24,1536]{3,2,0,1:T(8,128)(2,1)S(1)}, bf16[2,2,24,1536]{3,2,0,1:T(8,128)(2,1)S(1)}, u32[]{:S(2)}, u32[]{:S(2)}) collective-permute-start(bf16[2,2,24,1536]{3,2,0,1:T(8,128)(2,1)S(1)} %dynamic-slice_bitcast_fusion.7), channel_id=1, source_target_pairs={{0,16},{1,17},{2,18},{3,19},{4,20},{5,21},{6,22},{7,23},{8,24},{9,... | collective-permute-start | bytes 884744 | tf_op jit(solution)/shard_map/ppermute | solution.py:647
  259.8 12.5 %collective-permute-start.35 = (bf16[2,24,3072]{2,1,0:T(8,128)(2,1)S(1)}, bf16[2,24,3072]{2,1,0:T(8,128)(2,1)S(1)}, u32[]{:S(2)}, u32[]{:S(2)}) collective-permute-start(bf16[2,24,3072]{2,1,0:T(8,128)(2,1)S(1)} %dynamic-slice_bitcast_fusion.5), channel_id=1, source_target_pairs={{0,2},{1,3},{2,0},{3,1},{4,6},{5,7},{6,4},{7,5},{8,10},{9,11},{10,... | collective-permute-start | bytes 884744 | tf_op jit(solution)/shard_map/ppermute | solution.py:647
  261.4 13.0 %collective-permute-start.33 = (bf16[2,2,2,24,896]{4,3,2,1,0:T(8,128)(2,1)S(1)}, bf16[2,2,2,24,896]{4,3,2,1,0:T(8,128)(2,1)S(1)}, u32[]{:S(2)}, u32[]{:S(2)}) collective-permute-start(bf16[2,2,2,24,896]{4,3,2,1,0:T(8,128)(2,1)S(1)} %dynamic-slice_bitcast_fusion.4), channel_id=1, source_target_pairs={{0,16},{1,17},{2,18},{3,19},{4,20},{5,21},{6,22},{7,23},{8,24},{9,... | collective-permute-start | bytes 1032200 | tf_op jit(solution)/shard_map/ppermute | solution.py:647
  274.6 8.5 %collective-permute-start.39 = (bf16[24,3072]{1,0:T(8,128)(2,1)S(1)}, bf16[24,3072]{1,0:T(8,128)(2,1)S(1)}, u32[]{:S(2)}, u32[]{:S(2)}) collective-permute-start(bf16[24,3072]{1,0:T(8,128)(2,1)S(1)} %dynamic-slice_bitcast_fusion.15), channel_id=1, source_target_pairs={{0,4},{1,5},{2,6},{3,7},{4,0},{5,1},{6,2},{7,3},{8,12},{9,13},{10,... | collective-permute-start | bytes 442376 | tf_op jit(solution)/shard_map/ppermute | solution.py:647
  276.7 7.2 %collective-permute-start.36 = (bf16[2,24,1536]{2,1,0:T(8,128)(2,1)S(1)}, bf16[2,24,1536]{2,1,0:T(8,128)(2,1)S(1)}, u32[]{:S(2)}, u32[]{:S(2)}) collective-permute-start(bf16[2,24,1536]{2,1,0:T(8,128)(2,1)S(1)} %dynamic-slice_bitcast_fusion.17), channel_id=1, source_target_pairs={{0,2},{1,3},{2,0},{3,1},{4,6},{5,7},{6,4},{7,5},{8,10},{9,11},{10,... | collective-permute-start | bytes 442376 | tf_op jit(solution)/shard_map/ppermute | solution.py:647
  277.0 6.9 %collective-permute-start.37 = (bf16[2,2,24,768]{3,2,1,0:T(8,128)(2,1)S(1)}, bf16[2,2,24,768]{3,2,1,0:T(8,128)(2,1)S(1)}, u32[]{:S(2)}, u32[]{:S(2)}) collective-permute-start(bf16[2,2,24,768]{3,2,1,0:T(8,128)(2,1)S(1)} %dynamic-slice_bitcast_fusion.16), channel_id=1, source_target_pairs={{0,16},{1,17},{2,18},{3,19},{4,20},{5,21},{6,22},{7,23},{8,24},{9,... | collective-permute-start | bytes 442376 | tf_op jit(solution)/shard_map/ppermute | solution.py:647
  277.7 6.2 %collective-permute-start.38 = (bf16[2,2,24,896]{3,2,1,0:T(8,128)(2,1)S(1)}, bf16[2,2,24,896]{3,2,1,0:T(8,128)(2,1)S(1)}, u32[]{:S(2)}, u32[]{:S(2)}) collective-permute-start(bf16[2,2,24,896]{3,2,1,0:T(8,128)(2,1)S(1)} %dynamic-slice_bitcast_fusion.13), channel_id=1, source_target_pairs={{0,8},{1,9},{2,10},{3,11},{4,12},{5,13},{6,14},{7,15},{8,0},{9,1},... | collective-permute-start | bytes 516104 | tf_op jit(solution)/shard_map/ppermute | solution.py:647
  284.1 6.2 %collective-permute-start.40 = (bf16[24,1536]{1,0:T(8,128)(2,1)S(1)}, bf16[24,1536]{1,0:T(8,128)(2,1)S(1)}, u32[]{:S(2)}, u32[]{:S(2)}) collective-permute-start(bf16[24,1536]{1,0:T(8,128)(2,1)S(1)} %dynamic-slice_bitcast_fusion.20), channel_id=1, source_target_pairs={{0,4},{1,5},{2,6},{3,7},{4,0},{5,1},{6,2},{7,3},{8,12},{9,13},{10,... | collective-permute-start | bytes 221192 | tf_op jit(solution)/shard_map/ppermute | solution.py:647
  286.0 6.7 %collective-permute-start.41 = (bf16[2,24,1664]{2,1,0:T(8,128)(2,1)S(1)}, bf16[2,24,1664]{2,1,0:T(8,128)(2,1)S(1)}, u32[]{:S(2)}, u32[]{:S(2)}) collective-permute-start(bf16[2,24,1664]{2,1,0:T(8,128)(2,1)S(1)} %dynamic-slice_bitcast_fusion.14), channel_id=1, source_target_pairs={{0,2},{1,3},{2,0},{3,1},{4,6},{5,7},{6,4},{7,5},{8,10},{9,11},{10,... | collective-permute-start | bytes 479240 | tf_op jit(solution)/shard_map/ppermute | solution.py:647
  292.8 5.8 %collective-permute-start.42 = (bf16[24,1664]{1,0:T(8,128)(2,1)S(1)}, bf16[24,1664]{1,0:T(8,128)(2,1)S(1)}, u32[]{:S(2)}, u32[]{:S(2)}) collective-permute-start(bf16[24,1664]{1,0:T(8,128)(2,1)S(1)} %dynamic-slice_bitcast_fusion.19), channel_id=1, source_target_pairs={{0,4},{1,5},{2,6},{3,7},{4,0},{5,1},{6,2},{7,3},{8,12},{9,13},{10,... | collective-permute-start | bytes 239624 | tf_op jit(solution)/shard_map/ppermute | solution.py:647
  (9 other events, 13.6 us)
Sparse Core Ops, SparseCore 0:
  17.0 79.0 all-gather.1
